TPU v7x, 256 devices: a whole 4x4x8 slice. The times are simulated.
256 devices in a mesh: sec: 32 (over z_lo, y, core), sym: 8 (over x, z_hi).
Axes of the slice: x: 4, y: 4, z: 8 (z_hi: 2, z_lo: 4; z = z_hi * 4 + z_lo), core: 2. Of those that a mesh axis runs over, the one named last changes fastest.
Arguments:
- start_state: float32 [32, 64, 128, 128], P('sec', 'sym'), may hold values from -6 to 6
- left_env: bfloat16 [32, 24, 64, 128, 128], P('sec', None, 'sym'), may hold values from -0.5 to 0.5
- right_env: bfloat16 [32, 24, 64, 128, 128], P('sec', None, 'sym'), may hold values from -0.5 to 0.5
- joining: int32 [32, 24, 64], P('sec'), may hold values from 0 to 63, as said below
- kept: int32 [32, 64], P('sec', 'sym'), may hold values from 64 to 128
Outputs:
- state: float32 [32, 64, 128, 128], P('sec', 'sym')
- energy: float32 [32], P('sec')
Inputs may be any that keep to these rules, and one draw needn't show every extreme that they name: For every section s and term w, joining[s, w, :] is a permutation of the 64 sectors.
All inputs are finite; a program needn't handle non-finite values.
Results may differ from a plain program's by a relative error of at most 0.017.
Values may be sent and summed in bfloat16 or wider, within the bound.
No kernel may reach another device: no remote copies, remote signals or barrier semaphores. Data moves between devices by JAX's collectives and lax.ppermute only.
A program may use at most 128 MiB of HBM per device.

v0:
```python
import jax
import jax.numpy as jnp
from jax import lax
from jax.sharding import PartitionSpec as P

ITERS = 4


def passed_along(value, axis, steps):
    count = lax.axis_size(axis)
    leading, last = (max(0, -steps), min(count, count - steps))
    return lax.ppermute(value, axis, [(source, source + steps) for source in range(leading, last)])


def shards(start_state, left_env, right_env, joining, kept):
    q_dev = start_state.shape[1]
    block = start_state.shape[2]
    sectors = joining.shape[2]
    terms_count = left_env.shape[1]
    sym_index = lax.axis_index("sym")
    received = passed_along(right_env, "sec", -1)
    at_end = lax.axis_index("sec") == lax.axis_size("sec") - 1
    right = jnp.where(at_end, right_env[0], received[0])
    left = left_env[0]
    table_own = lax.dynamic_slice_in_dim(joining[0], sym_index * q_dev, q_dev, 1)
    rows = lax.broadcasted_iota(jnp.int32, (block, block), 0)
    cols = lax.broadcasted_iota(jnp.int32, (block, block), 1)
    limit = kept[0][:, None, None]
    mask = ((rows[None] < limit) & (cols[None] < limit)).astype(jnp.float32)
    state = start_state[0] * mask
    energy = jnp.zeros((), jnp.float32)
    for step in range(ITERS):
        state_b = state.astype(jnp.bfloat16)

        def one_term(total, term_index):
            middle = jnp.einsum(
                "qab,qbc->qac", left[term_index], state_b, preferred_element_type=jnp.float32
            ).astype(jnp.bfloat16)
            term = jnp.einsum(
                "qac,qdc->qad", middle, right[term_index], preferred_element_type=jnp.float32
            )
            return (total.at[table_own[term_index]].add(term), None)

        partial_value, unused = lax.scan(
            one_term, jnp.zeros((sectors, block, block), jnp.float32), jnp.arange(terms_count)
        )
        partial_low = partial_value.astype(jnp.bfloat16)
        summed = lax.psum(partial_low, "sym").astype(jnp.float32)
        image = lax.dynamic_slice_in_dim(summed, sym_index * q_dev, q_dev, 0)
        image = image * mask
        first, second = lax.psum((jnp.sum(state * state), jnp.sum(state * image)), "sym")
        energy = second / first
        moved = state - 0.15 * (image - energy * state)
        size = lax.psum(jnp.sum(moved * moved), "sym")
        state = moved / jnp.sqrt(size / float(sectors * block * block) + 1e-06)
    return (state[None], jnp.reshape(energy, (1,)))


def solution(mesh):
    return jax.shard_map(
        shards,
        mesh=mesh,
        in_specs=(
            P("sec", "sym", None, None),
            P("sec", None, "sym", None, None),
            P("sec", None, "sym", None, None),
            P("sec", None, None),
            P("sec", "sym"),
        ),
        out_specs=(P("sec", "sym", None, None), P("sec")),
        check_vma=False,
    )
```

profile of v0, /device:TPU:8, one launch (start us, length us, event | category | flops | bytes accessed | tf_op | source)
XLA Modules:
  0.0 1783.2 jit_solution(10831383014010926488)
XLA Ops:
  10.4 67.5 %collective-permute-done = bf16[1,24,8,128,128]{4,3,2,1,0:T(8,128)(2,1)} collective-permute-done((bf16[1,24,8,128,128]{4,3,2,1,0:T(8,128)(2,1)}, bf16[1,24,8,128,128]{4,3,2,1,0:T(8,128)(2,1)}, u32[]{:S(2)}, u32[]{:S(2)}) %collective-permute-start) | collective-permute-done | bytes 6291488 | tf_op jit(solution)/shard_map/ppermute | solution.py:12
  77.9 6.1 select_bitcast_fusion
  86.6 160.8 %while.40 = (s32[]{:T(128)}, f32[64,128,128]{2,1,0:T(8,128)}, s32[24]{0:T(128)S(1)}, s32[24,8]{1,0:T(8,128)S(1)}, bf16[24,8,128,128]{3,2,1,0:T(8,128)(2,1)}, /*i...) while((s32[]{:T(128)}, f32[64,128,128]{2,1,0:T(8,128)}, ...), condition=%wide.region_2.3_spmd, body=%wide.region_0.2_spmd.sunk | while | flops 67371040 | bytes 2884855 | solution.py:44
  157.6 2.7 scatter_fusion
  247.4 3.9 convert_element_type.50
  251.4 200.9 %all-reduce.9.cloned.1.call-done = bf16[64,128,128]{2,1,0:T(8,128)(2,1)} async-done(((bf16[64,128,128]{2,1,0:T(8,128)(2,1)}), bf16[64,128,128]{2,1,0:T(8,128)(2,1)}) %all-reduce.9.cloned.1.call-update) | async-done | bytes 2097168 | tf_op jit(solution)/shard_map/psum | solution.py:48
  454.0 27.9 %all-reduce.3 = (f32[]{:T(128)}, f32[]{:T(128)}) all-reduce(f32[]{:T(128)} %get-tuple-element.155, f32[]{:T(128)} %get-tuple-element.154), channel_id=1, replica_groups=mesh['sec'=32,'sym'=8] {'sym'}, use_global_device_ids=true, to_apply=%region_5.6 | all-reduce | flops 2 | bytes 16 | tf_op jit(solution)/shard_map/psum | solution.py:51
  485.1 27.0 %psum.115 = f32[]{:T(128)} all-reduce(f32[]{:T(128)} %multiply_reduce_fusion.9), channel_id=1, replica_groups=mesh['sec'=32,'sym'=8] {'sym'}, use_global_device_ids=true, to_apply=%region_9.10 | all-reduce | flops 1 | bytes 8 | tf_op jit(solution)/shard_map/psum | solution.py:54
  516.5 160.8 %while.41 = (s32[]{:T(128)}, f32[64,128,128]{2,1,0:T(8,128)}, s32[24]{0:T(128)S(1)}, s32[24,8]{1,0:T(8,128)S(1)}, bf16[24,8,128,128]{3,2,1,0:T(8,128)(2,1)}, /*i...) while((s32[]{:T(128)}, f32[64,128,128]{2,1,0:T(8,128)}, ...), condition=%wide.region_12.13_spmd, body=%wide.region_10.12_spmd.sunk | while | flops 67371040 | bytes 2884855 | solution.py:44
  677.3 3.9 convert_element_type.53
  681.3 191.3 %all-reduce.11.cloned.1.call-done = bf16[64,128,128]{2,1,0:T(8,128)(2,1)} async-done(((bf16[64,128,128]{2,1,0:T(8,128)(2,1)}), bf16[64,128,128]{2,1,0:T(8,128)(2,1)}) %all-reduce.11.cloned.1.call-update) | async-done | bytes 2097168 | tf_op jit(solution)/shard_map/psum | solution.py:48
  874.3 27.9 %all-reduce.2 = (f32[]{:T(128)}, f32[]{:T(128)}) all-reduce(f32[]{:T(128)} %get-tuple-element.161, f32[]{:T(128)} %get-tuple-element.160), channel_id=1, replica_groups=mesh['sec'=32,'sym'=8] {'sym'}, use_global_device_ids=true, to_apply=%region_15.16 | all-reduce | flops 2 | bytes 16 | tf_op jit(solution)/shard_map/psum | solution.py:51
  905.3 27.0 %psum.119 = f32[]{:T(128)} all-reduce(f32[]{:T(128)} %multiply_reduce_fusion.6), channel_id=1, replica_groups=mesh['sec'=32,'sym'=8] {'sym'}, use_global_device_ids=true, to_apply=%region_19.20 | all-reduce | flops 1 | bytes 8 | tf_op jit(solution)/shard_map/psum | solution.py:54
  936.8 160.8 %while.42 = (s32[]{:T(128)}, f32[64,128,128]{2,1,0:T(8,128)}, s32[24]{0:T(128)S(1)}, s32[24,8]{1,0:T(8,128)S(1)}, bf16[24,8,128,128]{3,2,1,0:T(8,128)(2,1)}, /*i...) while((s32[]{:T(128)}, f32[64,128,128]{2,1,0:T(8,128)}, ...), condition=%wide.region_22.23_spmd, body=%wide.region_20.22_spmd.sunk | while | flops 67371040 | bytes 2884855 | solution.py:44
  1097.6 3.9 convert_element_type.56
  1101.5 191.0 %all-reduce.13.cloned.1.call-done = bf16[64,128,128]{2,1,0:T(8,128)(2,1)} async-done(((bf16[64,128,128]{2,1,0:T(8,128)(2,1)}), bf16[64,128,128]{2,1,0:T(8,128)(2,1)}) %all-reduce.13.cloned.1.call-update) | async-done | bytes 2097168 | tf_op jit(solution)/shard_map/psum | solution.py:48
  1294.3 27.9 %all-reduce.1 = (f32[]{:T(128)}, f32[]{:T(128)}) all-reduce(f32[]{:T(128)} %get-tuple-element.159, f32[]{:T(128)} %get-tuple-element.158), channel_id=1, replica_groups=mesh['sec'=32,'sym'=8] {'sym'}, use_global_device_ids=true, to_apply=%region_25.26 | all-reduce | flops 2 | bytes 16 | tf_op jit(solution)/shard_map/psum | solution.py:51
  1325.3 27.0 %psum.123 = f32[]{:T(128)} all-reduce(f32[]{:T(128)} %multiply_reduce_fusion.3), channel_id=1, replica_groups=mesh['sec'=32,'sym'=8] {'sym'}, use_global_device_ids=true, to_apply=%region_29.30 | all-reduce | flops 1 | bytes 8 | tf_op jit(solution)/shard_map/psum | solution.py:54
  1356.8 160.8 %while.43 = (s32[]{:T(128)}, f32[64,128,128]{2,1,0:T(8,128)}, s32[24]{0:T(128)S(1)}, s32[24,8]{1,0:T(8,128)S(1)}, bf16[24,8,128,128]{3,2,1,0:T(8,128)(2,1)}, /*i...) while((s32[]{:T(128)}, f32[64,128,128]{2,1,0:T(8,128)}, ...), condition=%wide.region_32.33_spmd, body=%wide.region_30.32_spmd.sunk | while | flops 67371040 | bytes 2884855 | solution.py:44
  1427.7 2.7 scatter_fusion.3
  1517.5 3.9 convert_element_type.59
  1521.5 191.6 %all-reduce.15.cloned.1.call-done = bf16[64,128,128]{2,1,0:T(8,128)(2,1)} async-done(((bf16[64,128,128]{2,1,0:T(8,128)(2,1)}), bf16[64,128,128]{2,1,0:T(8,128)(2,1)}) %all-reduce.15.cloned.1.call-update) | async-done | bytes 2097168 | tf_op jit(solution)/shard_map/psum | solution.py:48
  1714.9 27.9 %all-reduce = (f32[]{:T(128)}, f32[]{:T(128)}) all-reduce(f32[]{:T(128)} %get-tuple-element.157, f32[]{:T(128)} %get-tuple-element.156), channel_id=1, replica_groups=mesh['sec'=32,'sym'=8] {'sym'}, use_global_device_ids=true, to_apply=%region_35.36 | all-reduce | flops 2 | bytes 16 | tf_op jit(solution)/shard_map/psum | solution.py:51
  1745.9 27.0 %psum.127 = f32[]{:T(128)} all-reduce(f32[]{:T(128)} %multiply_reduce_fusion), channel_id=1, replica_groups=mesh['sec'=32,'sym'=8] {'sym'}, use_global_device_ids=true, to_apply=%region_39.40 | all-reduce | flops 1 | bytes 8 | tf_op jit(solution)/shard_map/psum | solution.py:54
  (419 shorter events, 483.8 us)
Async XLA Ops:
  7.2 2.0 copy-start
  7.2 445.1 %all-reduce.9.cloned.1.call-start = ((), (), s32[]{:S(2)}) async-start(), calls=%async_computation | async-start | bytes 4194304 | tf_op jit(solution)/shard_map/psum | solution.py:48
  7.2 70.7 %collective-permute-start = (bf16[1,24,8,128,128]{4,3,2,1,0:T(8,128)(2,1)}, bf16[1,24,8,128,128]{4,3,2,1,0:T(8,128)(2,1)}, u32[]{:S(2)}, u32[]{:S(2)}) collective-permute-start(bf16[1,24,8,128,128]{4,3,2,1,0:T(8,128)(2,1)} %param.15), channel_id=1, source_target_pairs={{8,0},{16,8},{24,16},{32,24},{40,32},{48,40},{56,48},{64,56},{72,6... | collective-permute-start | bytes 18874376 | tf_op jit(solution)/shard_map/ppermute | solution.py:12
  247.4 204.9 %copy-start.1 = (f32[1,8,128,128]{3,2,1,0:T(8,128)S(1)}, f32[1,8,128,128]{3,2,1,0:T(8,128)}, u32[]{:S(2)}) copy-start(f32[1,8,128,128]{3,2,1,0:T(8,128)} %param.13) | copy-start | bytes 1572868
  247.4 204.9 %copy-start.2 = (s32[1,8]{1,0:T(1,128)S(1)}, s32[1,8]{1,0:T(1,128)}, u32[]{:S(2)}) copy-start(s32[1,8]{1,0:T(1,128)} %param.17) | copy-start | bytes 100
  251.3 621.2 %all-reduce.11.cloned.1.call-start = ((), (), s32[]{:S(2)}) async-start(), calls=%async_computation.1 | async-start | bytes 4194304 | tf_op jit(solution)/shard_map/psum | solution.py:48
  681.2 611.3 %all-reduce.13.cloned.1.call-start = ((), (), s32[]{:S(2)}) async-start(), calls=%async_computation.2 | async-start | bytes 4194304 | tf_op jit(solution)/shard_map/psum | solution.py:48
  1101.5 611.6 %all-reduce.15.cloned.1.call-start = ((), (), s32[]{:S(2)}) async-start(), calls=%async_computation.3 | async-start | bytes 4194304 | tf_op jit(solution)/shard_map/psum | solution.py:48
Sparse Core Ops, SparseCore 0:
  251.5 200.7 all-reduce.8
  681.3 191.1 all-reduce.10
  1101.6 190.8 all-reduce.12
  1521.6 191.4 all-reduce.14
where the time goes:
time: 1790 us; the launch traced here: 1780 us
  waiting for transfers between devices  842 us (47%)
  other arithmetic  303 us (17%)
  blocking collectives  219 us (12%)
  loops' own time  187 us (10%)
  matrix products  139 us (8%)
  local copies, waits for them, and re-layouts  66.2 us (4%)
  between operations  23.1 us (1%)
    psum x4, waiting for transfers between devices, shards(): summed = lax.psum(partial_low, 'sym').astype(jnp.float32)  775 us
    scatter-add x96, other arithmetic, one_term(): return (total.at[table_own[term_index]].add(term), None)  260 us
    another operation x4, loops' own time, shards(): lax.scan(one_term, jnp.zeros((sectors, block, block), jnp.float32), jnp.a...  187 us
    dot_general x96, matrix products, one_term(): jnp.einsum('qac,qdc->qad', middle, right[term_index], preferred_element_t...  139 us
    psum x4, blocking collectives, shards(): lax.psum((jnp.sum(state * state), jnp.sum(state * image)), 'sym')  111 us
    psum x4, blocking collectives, shards(): size = lax.psum(jnp.sum(moved * moved), 'sym')  108 us
    ppermute x1, waiting for transfers between devices, passed_along(): lax.ppermute(value, axis, [(source, source + steps) for source in range(l...  67.5 us
    dynamic_slice x96, local copies, waits for them, and re-layouts, shards(): lax.scan(one_term, jnp.zeros((sectors, block, block), jnp.float32), jnp.a...  55.9 us
  transfers between devices with their start and end apart: 5, of which 5 were waited for; matrix products, arithmetic and copies ran while one was open for 0% of the time, Pallas kernels for 0%

commit v1 on v0

v1 whole, which is shorter than its diff:
```python
import functools

import jax
import jax.numpy as jnp
from jax import lax
from jax.experimental import pallas as pl
from jax.experimental.pallas import tpu as pltpu
from jax.sharding import PartitionSpec as P

ITERS = 4
STEP = 0.15
SCALE = 2.0**-8
TERMS_PER_STEP = 4
ALONG_X = 4
ALONG_Z = 2
HALVES = 2
NT = (((1,), (1,)), ((), ()))
F32 = jnp.float32
BF16 = jnp.bfloat16


def params():
    return pltpu.CompilerParams(vmem_limit_bytes=48 * 2**20)


def sector_mask(limit, block):
    rows = lax.broadcasted_iota(jnp.int32, (block, block), 0)
    cols = lax.broadcasted_iota(jnp.int32, (block, block), 1)
    return ((rows < limit) & (cols < limit)).astype(F32)


def apply_kernel(first, slot_ref, kept_ref, at_end_ref, *refs):
    inputs = 1 if first else 4
    sources, (left_ref, here_ref, came_ref), refs = refs[:inputs], refs[inputs : inputs + 3], refs[inputs + 3 :]
    pieces, (vector_ref, total, middle, state_b, right_buffer, arrived) = refs[:8], refs[8:]
    step, steps = pl.program_id(0), pl.num_programs(0)
    terms, sectors, block = left_ref.shape[0], left_ref.shape[1], left_ref.shape[2]
    half = sectors // HALVES
    now = step % 2

    def copy(source_ref, at, slot):
        source = source_ref.at[pl.ds(at * terms, terms)]
        return pltpu.make_async_copy(source, right_buffer.at[slot], arrived.at[slot])

    def fetch(at, slot):
        @pl.when(at_end_ref[0] == 1)
        def _():
            copy(here_ref, at, slot).start()

        @pl.when(at_end_ref[0] != 1)
        def _():
            copy(came_ref, at, slot).start()

    @pl.when(step == 0)
    def _():
        fetch(0, 0)

    @pl.when(step + 1 < steps)
    def _():
        fetch(step + 1, 1 - now)

    @pl.when(step == 0)
    def _():
        total[...] = jnp.zeros_like(total)
        for q in range(sectors):
            mask = sector_mask(kept_ref[q], block)
            if first:
                value = sources[0][q] * mask
            else:
                own, came = sources[q // half], sources[2 + q // half]
                value = (own[q % half] + came[q % half].astype(F32)) * (mask * SCALE)
            vector_ref[q] = value
            state_b[q] = value.astype(BF16)

    for q in range(sectors):
        product = jnp.dot(
            left_ref[:, q].reshape(terms * block, block), state_b[q], preferred_element_type=F32
        )
        middle[:, q] = product.astype(BF16).reshape(terms, block, block)

    copy(here_ref, step, now).wait()
    right_ref = right_buffer.at[now]

    def one_term(k, carry):
        for q in range(sectors):
            term = lax.dot_general(middle[k, q], right_ref[k, q], NT, preferred_element_type=F32)
            slot = slot_ref[step * terms + k, q]
            total[slot] = total[slot] + term
        return carry

    lax.fori_loop(0, terms, one_term, 0)

    @pl.when(step == steps - 1)
    def _():
        per = ALONG_Z * half
        for index, piece in enumerate(pieces):
            for z in range(ALONG_Z):
                low = index * per + z * half
                piece[z] = total[low : low + half].astype(BF16)


def apply_operator(first, slots, kept, at_end, sources, left, rights):
    terms, sectors, block = left.shape[0], left.shape[1], left.shape[2]
    half = sectors // HALVES
    per = TERMS_PER_STEP
    whole = lambda shape: pl.BlockSpec(shape, lambda i, *_: (0,) * len(shape))
    stream = pl.BlockSpec((per, sectors, block, block), lambda i, *_: (i, 0, 0, 0))
    piece = (ALONG_Z, half, block, block)
    count = ALONG_X * HALVES
    out = pl.pallas_call(
        functools.partial(apply_kernel, first),
        grid_spec=pltpu.PrefetchScalarGridSpec(
            num_scalar_prefetch=3,
            grid=(terms // per,),
            in_specs=[whole(s.shape) for s in sources] + [stream] + [pl.BlockSpec(memory_space=pl.ANY)] * 2,
            out_specs=[whole(piece)] * count + [whole((sectors, block, block))],
            scratch_shapes=[
                pltpu.VMEM((count * ALONG_Z * half, block, block), F32),
                pltpu.VMEM((per, sectors, block, block), BF16),
                pltpu.VMEM((sectors, block, block), BF16),
                pltpu.VMEM((2, per, sectors, block, block), BF16),
                pltpu.SemaphoreType.DMA((2,)),
            ],
        ),
        out_shape=[jax.ShapeDtypeStruct(piece, BF16)] * count
        + [jax.ShapeDtypeStruct((sectors, block, block), F32)],
        compiler_params=params(),
        cost_estimate=pl.CostEstimate(
            flops=4 * terms * sectors * block**3, bytes_accessed=4 * terms * sectors * block**2, transcendentals=0
        ),
    )(slots, kept, at_end, *sources, left, *rights)
    return out[:count], out[count]


def dots(vectors, rows):
    newest = vectors[-1]
    sums = []
    for other in vectors:
        sums.append(jnp.sum(jnp.sum(newest * other, axis=0), axis=0, keepdims=True))
    sums += [jnp.zeros_like(sums[0])] * (rows - len(sums))
    return jnp.concatenate(sums, axis=0)


def dots_kernel(*refs):
    refs[-1][...] = dots([ref[...] for ref in refs[:-1]], 8)


def row_dots(vectors):
    return pl.pallas_call(
        dots_kernel,
        out_shape=jax.ShapeDtypeStruct((8, vectors[0].shape[-1]), F32),
        compiler_params=params(),
    )(*vectors)


def last_kernel(kept_ref, *refs):
    own, came, earlier = refs[:2], refs[2:4], refs[4:-2]
    vector_ref, dots_ref = refs[-2:]
    sectors, block = vector_ref.shape[0], vector_ref.shape[1]
    half = sectors // HALVES
    for q in range(sectors):
        mask = sector_mask(kept_ref[q], block) * SCALE
        vector_ref[q] = (own[q // half][q % half] + came[q // half][q % half].astype(F32)) * mask
    dots_ref[...] = dots([ref[...] for ref in earlier] + [vector_ref[...]], 8)


def last_vector(kept, own, came, earlier):
    shape = earlier[0].shape
    count = 4 + len(earlier)
    return pl.pallas_call(
        last_kernel,
        in_specs=[pl.BlockSpec(memory_space=pltpu.SMEM)] + [pl.BlockSpec(memory_space=pltpu.VMEM)] * count,
        out_shape=[jax.ShapeDtypeStruct(shape, F32), jax.ShapeDtypeStruct((8, shape[-1]), F32)],
        compiler_params=params(),
    )(kept, *own, *came, *earlier)


def combine_kernel(elements, *refs):
    grams, vectors, (state_ref, energy_ref) = refs[:8], refs[8 : 8 + ITERS + 1], refs[-2:]
    level = [ref[...] for ref in grams]
    while len(level) > 1:
        level = [level[i] + level[i + 1] for i in range(0, len(level), 2)]
    sums = jnp.broadcast_to(jnp.sum(level[0], axis=1, keepdims=True), level[0].shape)
    gram = {}
    for k in range(ITERS + 1):
        for j in range(k + 1):
            gram[k, j] = gram[j, k] = sums[8 * k + j : 8 * k + j + 1]

    def inner(one, two):
        result = None
        for i, x in enumerate(one):
            for j, y in enumerate(two):
                if x is not None and y is not None:
                    part = (x * y) * gram[i, j]
                    result = part if result is None else result + part
        return result

    weights = [jnp.ones_like(gram[0, 0])]
    energy = None
    for _ in range(ITERS):
        image = [None] + [w * (1.0 / SCALE) for w in weights]
        energy = inner(weights, image) / inner(weights, weights)
        moved = []
        for w, b in zip(weights + [None], image):
            if b is None:
                moved.append(w + STEP * energy * w)
            elif w is None:
                moved.append(-STEP * b)
            else:
                moved.append(w - STEP * (b - energy * w))
        scale = 1.0 / jnp.sqrt(inner(moved, moved) / float(elements) + 1e-6)
        weights = [m * scale for m in moved]
    energy_ref[...] = jnp.broadcast_to(energy, energy_ref.shape)
    for q in range(state_ref.shape[0]):
        value = weights[0] * vectors[0][q]
        for w, vector in zip(weights[1:], vectors[1:]):
            value = value + w * vector[q]
        state_ref[q] = value


def combine(grams, vectors, elements):
    shape = vectors[0].shape
    return pl.pallas_call(
        functools.partial(combine_kernel, elements),
        out_shape=[jax.ShapeDtypeStruct(shape, F32), jax.ShapeDtypeStruct((8, shape[-1]), F32)],
        compiler_params=params(),
    )(*grams, *vectors)


def around_x(value, steps):
    count = ALONG_X * ALONG_Z
    return lax.ppermute(value, "sym", [(i, (i + steps * ALONG_Z) % count) for i in range(count)])


def across(value, bits):
    count = ALONG_X * ALONG_Z
    return lax.ppermute(value, "sym", [(i, i ^ bits) for i in range(count)])


def add(*parts):
    total = parts[0].astype(F32)
    for part in parts[1:]:
        total = total + part.astype(F32)
    return total


def reduce_scatter(pieces):
    (own0, own1), (next0, next1), (far0, far1), (prev0, prev1) = [
        (pieces[2 * r], pieces[2 * r + 1]) for r in range(ALONG_X)
    ]
    went_right = around_x(far0, 1)
    went_left = around_x(far1, -1)
    from_left1 = around_x(next1, 1)
    from_right0 = around_x(prev0, -1)
    from_left0 = around_x(add(next0, went_right).astype(BF16), 1)
    from_right1 = around_x(add(prev1, went_left).astype(BF16), -1)
    sums = [add(own0, from_left0, from_right0), add(own1, from_left1, from_right1)]
    came = [across(s[1].astype(BF16), 1) for s in sums]
    return [s[0] for s in sums], came


def shards(start_state, left_env, right_env, joining, kept):
    sectors, block = start_state.shape[1], start_state.shape[2]
    half = sectors // HALVES
    count = lax.axis_size("sec")
    sym_index = lax.axis_index("sym")
    me_x, me_z = sym_index // ALONG_Z, sym_index % ALONG_Z
    at_end = jnp.reshape(lax.axis_index("sec") == count - 1, (1,)).astype(jnp.int32)
    rights = (right_env[0], lax.ppermute(right_env, "sec", [(s, s - 1) for s in range(1, count)])[0])
    left = left_env[0]
    table = lax.dynamic_slice_in_dim(joining[0], sym_index * sectors, sectors, 1)
    device, place = table // sectors, table % sectors
    piece = ((device // ALONG_Z - me_x) % ALONG_X) * HALVES + place // half
    slots = (piece * ALONG_Z + (device % ALONG_Z - me_z) % ALONG_Z) * half + place % half
    limits = kept[0]

    sources = [start_state[0]]
    vectors, rows = [], []
    for step in range(ITERS):
        pieces, vector = apply_operator(step == 0, slots, limits, at_end, sources, left, rights)
        vectors.append(vector)
        rows.append(row_dots(vectors))
        own, came = reduce_scatter(pieces)
        sources = own + came
    vector, last_rows = last_vector(limits, own, came, vectors)
    gram = jnp.concatenate(rows + [last_rows], axis=0)
    grams = [gram] + [across(gram, bits) for bits in range(1, ALONG_X * ALONG_Z)]
    elements = sectors * ALONG_X * ALONG_Z * block * block
    state, energy = combine(grams, vectors + [vector], elements)
    return (state[None], energy[0, :1])


def solution(mesh):
    return jax.shard_map(
        shards,
        mesh=mesh,
        in_specs=(
            P("sec", "sym", None, None),
            P("sec", None, "sym", None, None),
            P("sec", None, "sym", None, None),
            P("sec", None, None),
            P("sec", "sym"),
        ),
        out_specs=(P("sec", "sym", None, None), P("sec")),
        check_vma=False,
    )
```

time: 1790 us -> 295 us (0.16)
  the two profiles are of different devices: /device:TPU:8 before, /device:TPU:24 now
where the time goes in v1:
time: 295 us
  waiting for transfers between devices  134 us (45%)
  starting transfers between devices  99.5 us (34%)
  Pallas kernels  55.4 us (19%)
    ppermute x1, waiting for transfers between devices, shards(): lax.ppermute(right_env, 'sec', [(s, s - 1) for s in range(1, count)])[0]  67.9 us
    ppermute x15, starting transfers between devices, across(): return lax.ppermute(value, 'sym', [(i, i ^ bits) for i in range(count)])  61.7 us
    pallas_call x4, Pallas kernels, apply_operator(): pl.pallas_call(functools.partial(apply_kernel, first), grid_spec=pltpu.Pr...  52.6 us
    ppermute x24, starting transfers between devices, around_x(): lax.ppermute(value, 'sym', [(i, (i + steps * ALONG_Z) % count) for i in r...  35.7 us
    ppermute x24, waiting for transfers between devices, around_x(): lax.ppermute(value, 'sym', [(i, (i + steps * ALONG_Z) % count) for i in r...  35.6 us
    ppermute x15, waiting for transfers between devices, across(): return lax.ppermute(value, 'sym', [(i, i ^ bits) for i in range(count)])  30.8 us
  transfers between devices with their start and end apart: 40, of which 21 were waited for; matrix products, arithmetic and copies ran while one was open for 1% of the time, Pallas kernels for 0%

profile of v1, /device:TPU:24, one launch (start us, length us, event | category | flops | bytes accessed | tf_op | source)
XLA Modules:
  0.0 295.1 jit_solution(3847404127082215247)
XLA Ops:
  3.6 67.9 %collective-permute-done = bf16[1,24,8,128,128]{4,3,2,1,0:T(8,128)(2,1)} collective-permute-done((bf16[1,24,8,128,128]{4,3,2,1,0:T(8,128)(2,1)}, bf16[1,24,8,128,128]{4,3,2,1,0:T(8,128)(2,1)}, u32[]{:S(2)}, u32[]{:S(2)}) %collective-permute-start) | collective-permute-done | bytes 6291488 | tf_op jit(solution)/shard_map/ppermute | solution.py:269
  73.2 13.1 %shard_map.68 = (bf16[2,4,128,128]{3,2,1,0:T(8,128)(2,1)S(1)}, bf16[2,4,128,128]{3,2,1,0:T(8,128)(2,1)S(1)}, bf16[2,4,128,128]{3,2,1,0:T(8,128)(2,1)S(1)}, bf16[...) custom-call(s32[24,8]{1,0:T(8,128)S(1)} %fusion.15.slot_ref, ...), custom_call_target="tpu_custom_call" | custom-call | flops 1610612736 | bytes 12582912 | tf_op jit(solution)/shard_map/pallas_call | solution.py:110
  93.1 3.8 %collective-permute-start.6 = (bf16[2,4,128,128]{3,2,1,0:T(8,128)(2,1)S(1)}, bf16[2,4,128,128]{3,2,1,0:T(8,128)(2,1)S(1)}, u32[]{:S(2)}, u32[]{:S(2)}) collective-permute-start(bf16[2,4,128,128]{3,2,1,0:T(8,128)(2,1)S(1)} %add_convert_fusion.6), channel_id=1, source_target_pairs={{0,6},{1,7},{2,0},{3,1},{4,2},{5,3},{6,4},{7,5},{8,14},{9,15},{10,... | collective-permute-start | bytes 786440 | tf_op jit(solution)/shard_map/ppermute | solution.py:232
  102.8 7.3 %collective-permute-start.8 = (bf16[4,128,128]{2,1,0:T(8,128)(2,1)S(1)}, bf16[4,128,128]{2,1,0:T(8,128)(2,1)S(1)}, u32[]{:S(2)}, u32[]{:S(2)}) collective-permute-start(bf16[4,128,128]{2,1,0:T(8,128)(2,1)S(1)} %fusion.1), channel_id=1, source_target_pairs={{0,1},{1,0},{2,3},{3,2},{4,5},{5,4},{6,7},{7,6},{8,9},{9,8},{10,11... | collective-permute-start | bytes 393224 | tf_op jit(solution)/shard_map/ppermute | solution.py:237
  110.2 5.4 %collective-permute-start.7 = (bf16[4,128,128]{2,1,0:T(8,128)(2,1)S(1)}, bf16[4,128,128]{2,1,0:T(8,128)(2,1)S(1)}, u32[]{:S(2)}, u32[]{:S(2)}) collective-permute-start(bf16[4,128,128]{2,1,0:T(8,128)(2,1)S(1)} %fusion), channel_id=1, source_target_pairs={{0,1},{1,0},{2,3},{3,2},{4,5},{5,4},{6,7},{7,6},{8,9},{9,8},{10,11... | collective-permute-start | bytes 393224 | tf_op jit(solution)/shard_map/ppermute | solution.py:237
  115.7 6.2 %collective-permute-done.7.refs_2_ = bf16[4,128,128]{2,1,0:T(8,128)(2,1)S(1)} collective-permute-done((bf16[4,128,128]{2,1,0:T(8,128)(2,1)S(1)}, bf16[4,128,128]{2,1,0:T(8,128)(2,1)S(1)}, u32[]{:S(2)}, u32[]{:S(2)}) %collective-permute-start.7) | collective-permute-done | bytes 131104 | tf_op jit(solution)/shard_map/ppermute | solution.py:237
  121.9 13.1 %shard_map.70 = (bf16[2,4,128,128]{3,2,1,0:T(8,128)(2,1)S(1)}, bf16[2,4,128,128]{3,2,1,0:T(8,128)(2,1)S(1)}, bf16[2,4,128,128]{3,2,1,0:T(8,128)(2,1)S(1)}, bf16[...) custom-call(s32[24,8]{1,0:T(8,128)S(1)} %fusion.15.slot_ref, ...), custom_call_target="tpu_custom_call" | custom-call | flops 1610612736 | bytes 12582912 | tf_op jit(solution)/shard_map/pallas_call | solution.py:110
  138.1 5.6 %collective-permute-done.13 = bf16[2,4,128,128]{3,2,1,0:T(8,128)(2,1)S(1)} collective-permute-done((bf16[2,4,128,128]{3,2,1,0:T(8,128)(2,1)S(1)}, bf16[2,4,128,128]{3,2,1,0:T(8,128)(2,1)S(1)}, u32[]{:S(2)}, u32[]{:S(2)}) %collective-permute-start.13) | collective-permute-done | bytes 262176 | tf_op jit(solution)/shard_map/ppermute | solution.py:232
  154.3 6.4 %collective-permute-start.16 = (bf16[4,128,128]{2,1,0:T(8,128)(2,1)S(1)}, bf16[4,128,128]{2,1,0:T(8,128)(2,1)S(1)}, u32[]{:S(2)}, u32[]{:S(2)}) collective-permute-start(bf16[4,128,128]{2,1,0:T(8,128)(2,1)S(1)} %fusion.3), channel_id=1, source_target_pairs={{0,1},{1,0},{2,3},{3,2},{4,5},{5,4},{6,7},{7,6},{8,9},{9,8},{10,11... | collective-permute-start | bytes 393224 | tf_op jit(solution)/shard_map/ppermute | solution.py:237
  160.9 4.2 %collective-permute-start.15 = (bf16[4,128,128]{2,1,0:T(8,128)(2,1)S(1)}, bf16[4,128,128]{2,1,0:T(8,128)(2,1)S(1)}, u32[]{:S(2)}, u32[]{:S(2)}) collective-permute-start(bf16[4,128,128]{2,1,0:T(8,128)(2,1)S(1)} %fusion.2), channel_id=1, source_target_pairs={{0,1},{1,0},{2,3},{3,2},{4,5},{5,4},{6,7},{7,6},{8,9},{9,8},{10,11... | collective-permute-start | bytes 393224 | tf_op jit(solution)/shard_map/ppermute | solution.py:237
  165.1 7.2 %collective-permute-done.15.refs_2_ = bf16[4,128,128]{2,1,0:T(8,128)(2,1)S(1)} collective-permute-done((bf16[4,128,128]{2,1,0:T(8,128)(2,1)S(1)}, bf16[4,128,128]{2,1,0:T(8,128)(2,1)S(1)}, u32[]{:S(2)}, u32[]{:S(2)}) %collective-permute-start.15) | collective-permute-done | bytes 131104 | tf_op jit(solution)/shard_map/ppermute | solution.py:237
  172.3 13.3 %shard_map.72 = (bf16[2,4,128,128]{3,2,1,0:T(8,128)(2,1)S(1)}, bf16[2,4,128,128]{3,2,1,0:T(8,128)(2,1)S(1)}, bf16[2,4,128,128]{3,2,1,0:T(8,128)(2,1)S(1)}, bf16[...) custom-call(s32[24,8]{1,0:T(8,128)S(1)} %fusion.15.slot_ref, ...), custom_call_target="tpu_custom_call" | custom-call | flops 1610612736 | bytes 12582912 | tf_op jit(solution)/shard_map/pallas_call | solution.py:110
  189.2 3.9 %collective-permute-done.21 = bf16[2,4,128,128]{3,2,1,0:T(8,128)(2,1)S(1)} collective-permute-done((bf16[2,4,128,128]{3,2,1,0:T(8,128)(2,1)S(1)}, bf16[2,4,128,128]{3,2,1,0:T(8,128)(2,1)S(1)}, u32[]{:S(2)}, u32[]{:S(2)}) %collective-permute-start.21) | collective-permute-done | bytes 262176 | tf_op jit(solution)/shard_map/ppermute | solution.py:232
  199.8 4.6 %collective-permute-done.20 = bf16[2,4,128,128]{3,2,1,0:T(8,128)(2,1)S(1)} collective-permute-done((bf16[2,4,128,128]{3,2,1,0:T(8,128)(2,1)S(1)}, bf16[2,4,128,128]{3,2,1,0:T(8,128)(2,1)S(1)}, u32[]{:S(2)}, u32[]{:S(2)}) %collective-permute-start.20) | collective-permute-done | bytes 262176 | tf_op jit(solution)/shard_map/ppermute | solution.py:232
  204.6 5.2 %collective-permute-start.24 = (bf16[4,128,128]{2,1,0:T(8,128)(2,1)S(1)}, bf16[4,128,128]{2,1,0:T(8,128)(2,1)S(1)}, u32[]{:S(2)}, u32[]{:S(2)}) collective-permute-start(bf16[4,128,128]{2,1,0:T(8,128)(2,1)S(1)} %fusion.5), channel_id=1, source_target_pairs={{0,1},{1,0},{2,3},{3,2},{4,5},{5,4},{6,7},{7,6},{8,9},{9,8},{10,11... | collective-permute-start | bytes 393224 | tf_op jit(solution)/shard_map/ppermute | solution.py:237
  210.0 3.9 %collective-permute-start.23 = (bf16[4,128,128]{2,1,0:T(8,128)(2,1)S(1)}, bf16[4,128,128]{2,1,0:T(8,128)(2,1)S(1)}, u32[]{:S(2)}, u32[]{:S(2)}) collective-permute-start(bf16[4,128,128]{2,1,0:T(8,128)(2,1)S(1)} %fusion.4), channel_id=1, source_target_pairs={{0,1},{1,0},{2,3},{3,2},{4,5},{5,4},{6,7},{7,6},{8,9},{9,8},{10,11... | collective-permute-start | bytes 393224 | tf_op jit(solution)/shard_map/ppermute | solution.py:237
  214.2 6.0 %collective-permute-done.23.refs_2_ = bf16[4,128,128]{2,1,0:T(8,128)(2,1)S(1)} collective-permute-done((bf16[4,128,128]{2,1,0:T(8,128)(2,1)S(1)}, bf16[4,128,128]{2,1,0:T(8,128)(2,1)S(1)}, u32[]{:S(2)}, u32[]{:S(2)}) %collective-permute-start.23) | collective-permute-done | bytes 131104 | tf_op jit(solution)/shard_map/ppermute | solution.py:237
  220.3 13.1 %shard_map.74 = (bf16[2,4,128,128]{3,2,1,0:T(8,128)(2,1)S(1)}, bf16[2,4,128,128]{3,2,1,0:T(8,128)(2,1)S(1)}, bf16[2,4,128,128]{3,2,1,0:T(8,128)(2,1)S(1)}, bf16[...) custom-call(s32[24,8]{1,0:T(8,128)S(1)} %fusion.15.slot_ref, ...), custom_call_target="tpu_custom_call" | custom-call | flops 1610612736 | bytes 12582912 | tf_op jit(solution)/shard_map/pallas_call | solution.py:110
  251.3 5.0 %collective-permute-start.32 = (bf16[4,128,128]{2,1,0:T(8,128)(2,1)S(1)}, bf16[4,128,128]{2,1,0:T(8,128)(2,1)S(1)}, u32[]{:S(2)}, u32[]{:S(2)}) collective-permute-start(bf16[4,128,128]{2,1,0:T(8,128)(2,1)S(1)} %fusion.7), channel_id=1, source_target_pairs={{0,1},{1,0},{2,3},{3,2},{4,5},{5,4},{6,7},{7,6},{8,9},{9,8},{10,11... | collective-permute-start | bytes 393224 | tf_op jit(solution)/shard_map/ppermute | solution.py:237
  256.9 5.3 %collective-permute-start.31 = (bf16[4,128,128]{2,1,0:T(8,128)(2,1)S(1)}, bf16[4,128,128]{2,1,0:T(8,128)(2,1)S(1)}, u32[]{:S(2)}, u32[]{:S(2)}) collective-permute-start(bf16[4,128,128]{2,1,0:T(8,128)(2,1)S(1)} %fusion.6), channel_id=1, source_target_pairs={{0,1},{1,0},{2,3},{3,2},{4,5},{5,4},{6,7},{7,6},{8,9},{9,8},{10,11... | collective-permute-start | bytes 393224 | tf_op jit(solution)/shard_map/ppermute | solution.py:237
  262.2 4.1 %collective-permute-done.31.refs_2_ = bf16[4,128,128]{2,1,0:T(8,128)(2,1)S(1)} collective-permute-done((bf16[4,128,128]{2,1,0:T(8,128)(2,1)S(1)}, bf16[4,128,128]{2,1,0:T(8,128)(2,1)S(1)}, u32[]{:S(2)}, u32[]{:S(2)}) %collective-permute-start.31) | collective-permute-done | bytes 131104 | tf_op jit(solution)/shard_map/ppermute | solution.py:237
  267.4 4.8 %collective-permute-start.33 = (f32[40,128]{1,0:T(8,128)S(1)}, f32[40,128]{1,0:T(8,128)S(1)}, u32[]{:S(2)}, u32[]{:S(2)}) collective-permute-start(f32[40,128]{1,0:T(8,128)S(1)} %constant_dynamic-update-slice_fusion.refs_0_), channel_id=1, source_target_pairs={{0,1},{1,0},{2,3},{3,2},{4,5},{5,4},{6,7},{7,6},{8,9},{9,8},{10,11... | collective-permute-start | bytes 61448 | tf_op jit(solution)/shard_map/ppermute | solution.py:237
  277.0 5.6 %collective-permute-start.37 = (f32[40,128]{1,0:T(8,128)S(1)}, f32[40,128]{1,0:T(8,128)S(1)}, u32[]{:S(2)}, u32[]{:S(2)}) collective-permute-start(f32[40,128]{1,0:T(8,128)S(1)} %constant_dynamic-update-slice_fusion.refs_0_), channel_id=1, source_target_pairs={{0,5},{1,4},{2,7},{3,6},{4,1},{5,0},{6,3},{7,2},{8,13},{9,12},{10,... | collective-permute-start | bytes 61448 | tf_op jit(solution)/shard_map/ppermute | solution.py:237
  287.6 5.7 %collective-permute-done.39.refs_7_ = f32[40,128]{1,0:T(8,128)S(1)} collective-permute-done((f32[40,128]{1,0:T(8,128)S(1)}, f32[40,128]{1,0:T(8,128)S(1)}, u32[]{:S(2)}, u32[]{:S(2)}) %collective-permute-start.39) | collective-permute-done | bytes 20512 | tf_op jit(solution)/shard_map/ppermute | solution.py:237
  (111 shorter events, 73.2 us)
Async XLA Ops:
  0.6 70.9 %collective-permute-start = (bf16[1,24,8,128,128]{4,3,2,1,0:T(8,128)(2,1)}, bf16[1,24,8,128,128]{4,3,2,1,0:T(8,128)(2,1)}, u32[]{:S(2)}, u32[]{:S(2)}) collective-permute-start(bf16[1,24,8,128,128]{4,3,2,1,0:T(8,128)(2,1)} %param.7), channel_id=1, source_target_pairs={{8,0},{16,8},{24,16},{32,24},{40,32},{48,40},{56,48},{64,56},{72,6... | collective-permute-start | bytes 18874376 | tf_op jit(solution)/shard_map/ppermute | solution.py:269
  89.1 13.5 %collective-permute-start.4 = (bf16[2,4,128,128]{3,2,1,0:T(8,128)(2,1)S(1)}, bf16[2,4,128,128]{3,2,1,0:T(8,128)(2,1)S(1)}, u32[]{:S(2)}, u32[]{:S(2)}) collective-permute-start(bf16[2,4,128,128]{3,2,1,0:T(8,128)(2,1)S(1)} %get-tuple-element.48), channel_id=1, source_target_pairs={{0,2},{1,3},{2,4},{3,5},{4,6},{5,7},{6,0},{7,1},{8,10},{9,11},{10,... | collective-permute-start | bytes 786440 | tf_op jit(solution)/shard_map/ppermute | solution.py:232
  96.9 13.2 %collective-permute-start.3 = (bf16[2,4,128,128]{3,2,1,0:T(8,128)(2,1)S(1)}, bf16[2,4,128,128]{3,2,1,0:T(8,128)(2,1)S(1)}, u32[]{:S(2)}, u32[]{:S(2)}) collective-permute-start(bf16[2,4,128,128]{3,2,1,0:T(8,128)(2,1)S(1)} %get-tuple-element.46), channel_id=1, source_target_pairs={{0,6},{1,7},{2,0},{3,1},{4,2},{5,3},{6,4},{7,5},{8,14},{9,15},{10,... | collective-permute-start | bytes 786440 | tf_op jit(solution)/shard_map/ppermute | solution.py:232
  97.1 13.0 %collective-permute-start.2 = (bf16[2,4,128,128]{3,2,1,0:T(8,128)(2,1)S(1)}, bf16[2,4,128,128]{3,2,1,0:T(8,128)(2,1)S(1)}, u32[]{:S(2)}, u32[]{:S(2)}) collective-permute-start(bf16[2,4,128,128]{3,2,1,0:T(8,128)(2,1)S(1)} %add_convert_fusion.7), channel_id=1, source_target_pairs={{0,2},{1,3},{2,4},{3,5},{4,6},{5,7},{6,0},{7,1},{8,10},{9,11},{10,... | collective-permute-start | bytes 786440 | tf_op jit(solution)/shard_map/ppermute | solution.py:232
  102.8 12.9 %collective-permute-start.8 = (bf16[4,128,128]{2,1,0:T(8,128)(2,1)S(1)}, bf16[4,128,128]{2,1,0:T(8,128)(2,1)S(1)}, u32[]{:S(2)}, u32[]{:S(2)}) collective-permute-start(bf16[4,128,128]{2,1,0:T(8,128)(2,1)S(1)} %fusion.1), channel_id=1, source_target_pairs={{0,1},{1,0},{2,3},{3,2},{4,5},{5,4},{6,7},{7,6},{8,9},{9,8},{10,11... | collective-permute-start | bytes 393224 | tf_op jit(solution)/shard_map/ppermute | solution.py:237
  110.2 11.7 %collective-permute-start.7 = (bf16[4,128,128]{2,1,0:T(8,128)(2,1)S(1)}, bf16[4,128,128]{2,1,0:T(8,128)(2,1)S(1)}, u32[]{:S(2)}, u32[]{:S(2)}) collective-permute-start(bf16[4,128,128]{2,1,0:T(8,128)(2,1)S(1)} %fusion), channel_id=1, source_target_pairs={{0,1},{1,0},{2,3},{3,2},{4,5},{5,4},{6,7},{7,6},{8,9},{9,8},{10,11... | collective-permute-start | bytes 393224 | tf_op jit(solution)/shard_map/ppermute | solution.py:237
  138.1 15.2 %collective-permute-start.12 = (bf16[2,4,128,128]{3,2,1,0:T(8,128)(2,1)S(1)}, bf16[2,4,128,128]{3,2,1,0:T(8,128)(2,1)S(1)}, u32[]{:S(2)}, u32[]{:S(2)}) collective-permute-start(bf16[2,4,128,128]{3,2,1,0:T(8,128)(2,1)S(1)} %get-tuple-element.57), channel_id=1, source_target_pairs={{0,2},{1,3},{2,4},{3,5},{4,6},{5,7},{6,0},{7,1},{8,10},{9,11},{10,... | collective-permute-start | bytes 786440 | tf_op jit(solution)/shard_map/ppermute | solution.py:232
  143.7 10.5 %collective-permute-start.14 = (bf16[2,4,128,128]{3,2,1,0:T(8,128)(2,1)S(1)}, bf16[2,4,128,128]{3,2,1,0:T(8,128)(2,1)S(1)}, u32[]{:S(2)}, u32[]{:S(2)}) collective-permute-start(bf16[2,4,128,128]{3,2,1,0:T(8,128)(2,1)S(1)} %add_convert_fusion.4), channel_id=1, source_target_pairs={{0,6},{1,7},{2,0},{3,1},{4,2},{5,3},{6,4},{7,5},{8,14},{9,15},{10,... | collective-permute-start | bytes 786440 | tf_op jit(solution)/shard_map/ppermute | solution.py:232
  147.5 13.3 %collective-permute-start.11 = (bf16[2,4,128,128]{3,2,1,0:T(8,128)(2,1)S(1)}, bf16[2,4,128,128]{3,2,1,0:T(8,128)(2,1)S(1)}, u32[]{:S(2)}, u32[]{:S(2)}) collective-permute-start(bf16[2,4,128,128]{3,2,1,0:T(8,128)(2,1)S(1)} %get-tuple-element.55), channel_id=1, source_target_pairs={{0,6},{1,7},{2,0},{3,1},{4,2},{5,3},{6,4},{7,5},{8,14},{9,15},{10,... | collective-permute-start | bytes 786440 | tf_op jit(solution)/shard_map/ppermute | solution.py:232
  147.9 12.9 %collective-permute-start.10 = (bf16[2,4,128,128]{3,2,1,0:T(8,128)(2,1)S(1)}, bf16[2,4,128,128]{3,2,1,0:T(8,128)(2,1)S(1)}, u32[]{:S(2)}, u32[]{:S(2)}) collective-permute-start(bf16[2,4,128,128]{3,2,1,0:T(8,128)(2,1)S(1)} %add_convert_fusion.5), channel_id=1, source_target_pairs={{0,2},{1,3},{2,4},{3,5},{4,6},{5,7},{6,0},{7,1},{8,10},{9,11},{10,... | collective-permute-start | bytes 786440 | tf_op jit(solution)/shard_map/ppermute | solution.py:232
  154.3 10.8 %collective-permute-start.16 = (bf16[4,128,128]{2,1,0:T(8,128)(2,1)S(1)}, bf16[4,128,128]{2,1,0:T(8,128)(2,1)S(1)}, u32[]{:S(2)}, u32[]{:S(2)}) collective-permute-start(bf16[4,128,128]{2,1,0:T(8,128)(2,1)S(1)} %fusion.3), channel_id=1, source_target_pairs={{0,1},{1,0},{2,3},{3,2},{4,5},{5,4},{6,7},{7,6},{8,9},{9,8},{10,11... | collective-permute-start | bytes 393224 | tf_op jit(solution)/shard_map/ppermute | solution.py:237
  160.9 11.4 %collective-permute-start.15 = (bf16[4,128,128]{2,1,0:T(8,128)(2,1)S(1)}, bf16[4,128,128]{2,1,0:T(8,128)(2,1)S(1)}, u32[]{:S(2)}, u32[]{:S(2)}) collective-permute-start(bf16[4,128,128]{2,1,0:T(8,128)(2,1)S(1)} %fusion.2), channel_id=1, source_target_pairs={{0,1},{1,0},{2,3},{3,2},{4,5},{5,4},{6,7},{7,6},{8,9},{9,8},{10,11... | collective-permute-start | bytes 393224 | tf_op jit(solution)/shard_map/ppermute | solution.py:237
  189.2 10.5 %collective-permute-start.17 = (bf16[2,4,128,128]{3,2,1,0:T(8,128)(2,1)S(1)}, bf16[2,4,128,128]{3,2,1,0:T(8,128)(2,1)S(1)}, u32[]{:S(2)}, u32[]{:S(2)}) collective-permute-start(bf16[2,4,128,128]{3,2,1,0:T(8,128)(2,1)S(1)} %get-tuple-element.63), channel_id=1, source_target_pairs={{0,2},{1,3},{2,4},{3,5},{4,6},{5,7},{6,0},{7,1},{8,10},{9,11},{10,... | collective-permute-start | bytes 786440 | tf_op jit(solution)/shard_map/ppermute | solution.py:232
  189.2 15.3 %collective-permute-start.20 = (bf16[2,4,128,128]{3,2,1,0:T(8,128)(2,1)S(1)}, bf16[2,4,128,128]{3,2,1,0:T(8,128)(2,1)S(1)}, u32[]{:S(2)}, u32[]{:S(2)}) collective-permute-start(bf16[2,4,128,128]{3,2,1,0:T(8,128)(2,1)S(1)} %get-tuple-element.66), channel_id=1, source_target_pairs={{0,2},{1,3},{2,4},{3,5},{4,6},{5,7},{6,0},{7,1},{8,10},{9,11},{10,... | collective-permute-start | bytes 786440 | tf_op jit(solution)/shard_map/ppermute | solution.py:232
  193.2 11.3 %collective-permute-start.22 = (bf16[2,4,128,128]{3,2,1,0:T(8,128)(2,1)S(1)}, bf16[2,4,128,128]{3,2,1,0:T(8,128)(2,1)S(1)}, u32[]{:S(2)}, u32[]{:S(2)}) collective-permute-start(bf16[2,4,128,128]{3,2,1,0:T(8,128)(2,1)S(1)} %add_convert_fusion.2), channel_id=1, source_target_pairs={{0,6},{1,7},{2,0},{3,1},{4,2},{5,3},{6,4},{7,5},{8,14},{9,15},{10,... | collective-permute-start | bytes 786440 | tf_op jit(solution)/shard_map/ppermute | solution.py:232
  197.0 12.8 %collective-permute-start.19 = (bf16[2,4,128,128]{3,2,1,0:T(8,128)(2,1)S(1)}, bf16[2,4,128,128]{3,2,1,0:T(8,128)(2,1)S(1)}, u32[]{:S(2)}, u32[]{:S(2)}) collective-permute-start(bf16[2,4,128,128]{3,2,1,0:T(8,128)(2,1)S(1)} %get-tuple-element.64), channel_id=1, source_target_pairs={{0,6},{1,7},{2,0},{3,1},{4,2},{5,3},{6,4},{7,5},{8,14},{9,15},{10,... | collective-permute-start | bytes 786440 | tf_op jit(solution)/shard_map/ppermute | solution.py:232
  236.4 12.9 %collective-permute-start.28 = (bf16[2,4,128,128]{3,2,1,0:T(8,128)(2,1)S(1)}, bf16[2,4,128,128]{3,2,1,0:T(8,128)(2,1)S(1)}, u32[]{:S(2)}, u32[]{:S(2)}) collective-permute-start(bf16[2,4,128,128]{3,2,1,0:T(8,128)(2,1)S(1)} %get-tuple-element.75), channel_id=1, source_target_pairs={{0,2},{1,3},{2,4},{3,5},{4,6},{5,7},{6,0},{7,1},{8,10},{9,11},{10,... | collective-permute-start | bytes 786440 | tf_op jit(solution)/shard_map/ppermute | solution.py:232
  236.5 12.6 %collective-permute-start.25 = (bf16[2,4,128,128]{3,2,1,0:T(8,128)(2,1)S(1)}, bf16[2,4,128,128]{3,2,1,0:T(8,128)(2,1)S(1)}, u32[]{:S(2)}, u32[]{:S(2)}) collective-permute-start(bf16[2,4,128,128]{3,2,1,0:T(8,128)(2,1)S(1)} %get-tuple-element.72), channel_id=1, source_target_pairs={{0,2},{1,3},{2,4},{3,5},{4,6},{5,7},{6,0},{7,1},{8,10},{9,11},{10,... | collective-permute-start | bytes 786440 | tf_op jit(solution)/shard_map/ppermute | solution.py:232
  236.6 19.7 %collective-permute-start.27 = (bf16[2,4,128,128]{3,2,1,0:T(8,128)(2,1)S(1)}, bf16[2,4,128,128]{3,2,1,0:T(8,128)(2,1)S(1)}, u32[]{:S(2)}, u32[]{:S(2)}) collective-permute-start(bf16[2,4,128,128]{3,2,1,0:T(8,128)(2,1)S(1)} %get-tuple-element.73), channel_id=1, source_target_pairs={{0,6},{1,7},{2,0},{3,1},{4,2},{5,3},{6,4},{7,5},{8,14},{9,15},{10,... | collective-permute-start | bytes 786440 | tf_op jit(solution)/shard_map/ppermute | solution.py:232
  251.3 10.9 %collective-permute-start.32 = (bf16[4,128,128]{2,1,0:T(8,128)(2,1)S(1)}, bf16[4,128,128]{2,1,0:T(8,128)(2,1)S(1)}, u32[]{:S(2)}, u32[]{:S(2)}) collective-permute-start(bf16[4,128,128]{2,1,0:T(8,128)(2,1)S(1)} %fusion.7), channel_id=1, source_target_pairs={{0,1},{1,0},{2,3},{3,2},{4,5},{5,4},{6,7},{7,6},{8,9},{9,8},{10,11... | collective-permute-start | bytes 393224 | tf_op jit(solution)/shard_map/ppermute | solution.py:237
  267.4 15.2 %collective-permute-start.33 = (f32[40,128]{1,0:T(8,128)S(1)}, f32[40,128]{1,0:T(8,128)S(1)}, u32[]{:S(2)}, u32[]{:S(2)}) collective-permute-start(f32[40,128]{1,0:T(8,128)S(1)} %constant_dynamic-update-slice_fusion.refs_0_), channel_id=1, source_target_pairs={{0,1},{1,0},{2,3},{3,2},{4,5},{5,4},{6,7},{7,6},{8,9},{9,8},{10,11... | collective-permute-start | bytes 61448 | tf_op jit(solution)/shard_map/ppermute | solution.py:237
  272.2 11.3 %collective-permute-start.34 = (f32[40,128]{1,0:T(8,128)S(1)}, f32[40,128]{1,0:T(8,128)S(1)}, u32[]{:S(2)}, u32[]{:S(2)}) collective-permute-start(f32[40,128]{1,0:T(8,128)S(1)} %constant_dynamic-update-slice_fusion.refs_0_), channel_id=1, source_target_pairs={{0,2},{1,3},{2,0},{3,1},{4,6},{5,7},{6,4},{7,5},{8,10},{9,11},{10,... | collective-permute-start | bytes 61448 | tf_op jit(solution)/shard_map/ppermute | solution.py:237
  272.2 14.2 %collective-permute-start.35 = (f32[40,128]{1,0:T(8,128)S(1)}, f32[40,128]{1,0:T(8,128)S(1)}, u32[]{:S(2)}, u32[]{:S(2)}) collective-permute-start(f32[40,128]{1,0:T(8,128)S(1)} %constant_dynamic-update-slice_fusion.refs_0_), channel_id=1, source_target_pairs={{0,3},{1,2},{2,1},{3,0},{4,7},{5,6},{6,5},{7,4},{8,11},{9,10},{10,... | collective-permute-start | bytes 61448 | tf_op jit(solution)/shard_map/ppermute | solution.py:237
  274.9 11.6 %collective-permute-start.36 = (f32[40,128]{1,0:T(8,128)S(1)}, f32[40,128]{1,0:T(8,128)S(1)}, u32[]{:S(2)}, u32[]{:S(2)}) collective-permute-start(f32[40,128]{1,0:T(8,128)S(1)} %constant_dynamic-update-slice_fusion.refs_0_), channel_id=1, source_target_pairs={{0,4},{1,5},{2,6},{3,7},{4,0},{5,1},{6,2},{7,3},{8,12},{9,13},{10,... | collective-permute-start | bytes 61448 | tf_op jit(solution)/shard_map/ppermute | solution.py:237
  (19 other events, 176.1 us)

commit v2 on v1

v2 whole, which is shorter than its diff:
```python
import functools

import jax
import jax.numpy as jnp
from jax import lax
from jax.experimental import pallas as pl
from jax.experimental.pallas import tpu as pltpu
from jax.sharding import PartitionSpec as P

ITERS = 4
STEP = 0.15
SCALE = 2.0**-8
GROUP = 16
STRAIGHT = (10, 9)
ALONG_X = 4
ALONG_Y = 4
ALONG_Z = 2
HALVES = 2
NT = (((1,), (1,)), ((), ()))
F32 = jnp.float32
BF16 = jnp.bfloat16


def params(mebibytes=24):
    return pltpu.CompilerParams(vmem_limit_bytes=mebibytes * 2**20)


def sector_mask(limit, block):
    rows = lax.broadcasted_iota(jnp.int32, (block, block), 0)
    cols = lax.broadcasted_iota(jnp.int32, (block, block), 1)
    return ((rows < limit) & (cols < limit)).astype(F32)


def gather_kernel(where_ref, here_ref, *refs):
    parts, (right_ref, arrived) = refs[:-2], refs[-2:]
    at_end, is_odd = where_ref[0] == 1, where_ref[1] == 1
    straight, (beside, around) = parts[:-2], parts[-2:]
    low = 0
    for part in straight + (beside,):
        rows = pl.ds(low, part.shape[0])
        low += part.shape[0]

        @pl.when(at_end)
        def _(rows=rows):
            pltpu.make_async_copy(here_ref.at[rows], right_ref.at[rows], arrived).start()

        if part is not beside:

            @pl.when(jnp.logical_not(at_end))
            def _(rows=rows, part=part):
                pltpu.make_async_copy(part, right_ref.at[rows], arrived).start()

        else:

            @pl.when(jnp.logical_not(at_end) & is_odd)
            def _(rows=rows):
                pltpu.make_async_copy(around, right_ref.at[rows], arrived).start()

            @pl.when(jnp.logical_not(at_end) & jnp.logical_not(is_odd))
            def _(rows=rows):
                pltpu.make_async_copy(beside, right_ref.at[rows], arrived).start()

    pltpu.make_async_copy(here_ref, right_ref, arrived).wait()


def gather_right(where, here, parts):
    anywhere = pl.BlockSpec(memory_space=pl.ANY)
    return pl.pallas_call(
        gather_kernel,
        in_specs=[pl.BlockSpec(memory_space=pltpu.SMEM), pl.BlockSpec(memory_space=pltpu.HBM)]
        + [anywhere] * len(parts),
        out_specs=pl.BlockSpec(memory_space=pltpu.VMEM),
        out_shape=jax.ShapeDtypeStruct(here.shape, here.dtype),
        scratch_shapes=[pltpu.SemaphoreType.DMA],
        compiler_params=params(),
    )(where, here, *parts)


def cut_kernel(value_ref, *refs):
    parts, arrived = refs[:-1], refs[-1]
    low, copies = 0, []
    for part in parts:
        for at in range(0, part.shape[0], 2):
            here = pl.ds(at, min(2, part.shape[0] - at))
            there = pl.ds(low + at, here.size)
            copies.append(pltpu.make_async_copy(value_ref.at[there], part.at[here], arrived.at[len(copies)]))
        low += part.shape[0]
    for copy in copies:
        copy.start()
    for copy in copies:
        copy.wait()


def cut(value, lengths):
    return pl.pallas_call(
        cut_kernel,
        in_specs=[pl.BlockSpec(memory_space=pltpu.HBM)],
        out_specs=[pl.BlockSpec(memory_space=pltpu.VMEM)] * len(lengths),
        out_shape=[jax.ShapeDtypeStruct((n,) + value.shape[1:], value.dtype) for n in lengths],
        scratch_shapes=[pltpu.SemaphoreType.DMA((value.shape[0],))],
        compiler_params=params(59),
    )(value)


def next_section(value):
    count = lax.axis_size("sec")
    pairs = [(s, s - 1) for s in range(1, count)]
    *straight, rest = cut(value, STRAIGHT + (value.shape[0] - sum(STRAIGHT),))
    parts = [lax.ppermute(part, "sec", pairs) for part in straight]
    beside = lax.ppermute(rest, "sec", [(s, d) for s, d in pairs if s % 2 == 1])

    def after(s, steps):
        ring = 2 * ALONG_Y
        return s // ring * ring + (s + 2 * steps) % ring

    around = rest
    for steps in range(2):
        around = lax.ppermute(around, "sec", [(after(s, steps), after(s, steps + 1)) for s in range(2, count, 2)])
    around = lax.ppermute(around, "sec", [(after(s, 2), s - 1) for s in range(2, count, 2)])
    return parts + [beside, around]


def middle_kernel(first, kept_ref, *refs):
    sources, (left_ref, vector_ref, middle_ref, state_b) = refs[:-4], refs[-4:]
    terms, sectors, block = left_ref.shape[0], left_ref.shape[1], left_ref.shape[2]
    half = sectors // HALVES
    middle_ref[terms * sectors] = jnp.zeros((block, block), BF16)
    for q in range(sectors):
        mask = sector_mask(kept_ref[q], block)
        if first:
            value = sources[0][q] * mask
        else:
            value = (sources[0][q // half, q % half] + sources[1][q // half, q % half].astype(F32)) * (mask * SCALE)
        vector_ref[q] = value
        state_b[q] = value.astype(BF16)
    for q in range(sectors):
        product = jnp.dot(
            left_ref[:, q].reshape(terms * block, block), state_b[q], preferred_element_type=F32
        )
        for w in range(terms):
            middle_ref[w * sectors + q] = product[w * block : (w + 1) * block].astype(BF16)


def apply_left(first, kept, sources, left):
    terms, sectors, block = left.shape[0], left.shape[1], left.shape[2]
    in_vmem = pl.BlockSpec(memory_space=pltpu.VMEM)
    return pl.pallas_call(
        functools.partial(middle_kernel, first),
        in_specs=[pl.BlockSpec(memory_space=pltpu.SMEM)] + [in_vmem] * (len(sources) + 1),
        out_specs=[in_vmem] * 2,
        out_shape=[
            jax.ShapeDtypeStruct((sectors, block, block), F32),
            jax.ShapeDtypeStruct((terms * sectors + 1, block, block), BF16),
        ],
        scratch_shapes=[pltpu.VMEM((sectors, block, block), BF16)],
        compiler_params=params(),
        cost_estimate=pl.CostEstimate(
            flops=8 * terms * sectors * block**3, bytes_accessed=4 * terms * sectors * block**2, transcendentals=0
        ),
    )(kept, *sources, left)


def target_kernel(pairs_ref, middle_ref, right_ref, *refs):
    pieces, total = refs[:-1], refs[-1]
    sectors = right_ref.shape[1]
    last = right_ref.shape[0] * sectors - 1
    total[...] = jnp.zeros_like(total)

    def group(index, carry):
        for i in range(GROUP):
            at = index * GROUP + i
            one, two, slot = pairs_ref[0, at], pairs_ref[1, at], pairs_ref[2, at]
            left = jnp.concatenate([middle_ref[one], middle_ref[two]], axis=1)
            one, two = jnp.minimum(one, last), jnp.minimum(two, last)
            right = jnp.concatenate(
                [right_ref[one // sectors, one % sectors], right_ref[two // sectors, two % sectors]], axis=1
            )
            total[slot] += lax.dot_general(left, right, NT, preferred_element_type=F32)
        return carry

    lax.fori_loop(0, pairs_ref[3, 0], group, 0)
    start = 0
    for piece in pieces:
        for index in range(piece.shape[0]):
            piece[index] = total[start : start + piece.shape[1]].astype(BF16)
            start += piece.shape[1]


def sum_targets(pairs, middle, right, shapes, share):
    terms, sectors, block = right.shape[0], right.shape[1], right.shape[2]
    in_vmem = pl.BlockSpec(memory_space=pltpu.VMEM)
    slots = sum(shape[0] * shape[1] for shape in shapes)
    return pl.pallas_call(
        target_kernel,
        in_specs=[pl.BlockSpec(memory_space=pltpu.SMEM), in_vmem, in_vmem],
        out_specs=[in_vmem] * len(shapes),
        out_shape=[jax.ShapeDtypeStruct(shape, BF16) for shape in shapes],
        scratch_shapes=[pltpu.VMEM((slots, block, block), F32)],
        compiler_params=params(),
        cost_estimate=pl.CostEstimate(
            flops=int(share * 16 * terms * sectors * block**3), bytes_accessed=1 << 20, transcendentals=0
        ),
    )(pairs, middle, right)


def pair_up(slots, low, high):
    slots = slots.reshape(-1)
    count = slots.shape[0]
    inside = (slots >= low) & (slots < high)
    number = jnp.arange(count)
    same = slots[:, None] == slots[None, :]
    rank = jnp.sum(same & (number[None, :] < number[:, None]), axis=1)
    opens = inside & (rank % 2 == 0)
    before = opens[None, :] & ((slots[None, :] < slots[:, None]) | (same & (number[None, :] < number[:, None])))
    place = jnp.sum(before, axis=1)
    place = jnp.where(rank % 2 == 0, place, place - 1)
    length = -(-(count // 2 + (high - low)) // GROUP) * GROUP
    at = inside[None, :] & (place[None, :] == jnp.arange(length)[:, None])
    is_first, is_second = at & (rank[None, :] % 2 == 0), at & (rank[None, :] % 2 == 1)

    def pick(chosen, values, otherwise):
        return jnp.sum(jnp.where(chosen, values[None, :] - otherwise, 0), axis=1) + otherwise

    groups = jnp.broadcast_to((jnp.sum(opens) + GROUP - 1) // GROUP, (length,))
    rows = [pick(is_first, number, count), pick(is_second, number, count), pick(is_first, slots - low, 0), groups]
    return jnp.stack(rows).astype(jnp.int32)


def dots(vectors, rows):
    newest = vectors[-1]
    sums = []
    for other in vectors:
        sums.append(jnp.sum(jnp.sum(newest * other, axis=0), axis=0, keepdims=True))
    sums += [jnp.zeros_like(sums[0])] * (rows - len(sums))
    return jnp.concatenate(sums, axis=0)


def dots_kernel(*refs):
    refs[-1][...] = dots([ref[...] for ref in refs[:-1]], 8)


def row_dots(vectors):
    return pl.pallas_call(
        dots_kernel,
        out_shape=jax.ShapeDtypeStruct((8, vectors[0].shape[-1]), F32),
        compiler_params=params(),
    )(*vectors)


def last_kernel(kept_ref, *refs):
    own, came, earlier = refs[0], refs[1], refs[2:-2]
    vector_ref, dots_ref = refs[-2:]
    sectors, block = vector_ref.shape[0], vector_ref.shape[1]
    half = sectors // HALVES
    for q in range(sectors):
        mask = sector_mask(kept_ref[q], block) * SCALE
        vector_ref[q] = (own[q // half, q % half] + came[q // half, q % half].astype(F32)) * mask
    dots_ref[...] = dots([ref[...] for ref in earlier] + [vector_ref[...]], 8)


def last_vector(kept, own, came, earlier):
    shape = earlier[0].shape
    count = 2 + len(earlier)
    return pl.pallas_call(
        last_kernel,
        in_specs=[pl.BlockSpec(memory_space=pltpu.SMEM)] + [pl.BlockSpec(memory_space=pltpu.VMEM)] * count,
        out_shape=[jax.ShapeDtypeStruct(shape, F32), jax.ShapeDtypeStruct((8, shape[-1]), F32)],
        compiler_params=params(),
    )(kept, own, came, *earlier)


def combine_kernel(elements, *refs):
    gram_ref, vectors, (state_ref, energy_ref) = refs[0], refs[1:-2], refs[-2:]
    sums = jnp.broadcast_to(jnp.sum(gram_ref[...], axis=1, keepdims=True), gram_ref.shape)
    gram = {}
    for k in range(ITERS + 1):
        for j in range(k + 1):
            gram[k, j] = gram[j, k] = sums[8 * k + j : 8 * k + j + 1]

    def inner(one, two):
        result = None
        for i, x in enumerate(one):
            for j, y in enumerate(two):
                if x is not None and y is not None:
                    part = (x * y) * gram[i, j]
                    result = part if result is None else result + part
        return result

    weights = [jnp.ones_like(gram[0, 0])]
    energy = None
    for _ in range(ITERS):
        image = [None] + [w * (1.0 / SCALE) for w in weights]
        energy = inner(weights, image) / inner(weights, weights)
        moved = []
        for w, b in zip(weights + [None], image):
            if b is None:
                moved.append(w + STEP * energy * w)
            elif w is None:
                moved.append(-STEP * b)
            else:
                moved.append(w - STEP * (b - energy * w))
        scale = 1.0 / jnp.sqrt(inner(moved, moved) / float(elements) + 1e-6)
        weights = [m * scale for m in moved]
    energy_ref[...] = jnp.broadcast_to(energy, energy_ref.shape)
    for q in range(state_ref.shape[0]):
        value = weights[0] * vectors[0][q]
        for w, vector in zip(weights[1:], vectors[1:]):
            value = value + w * vector[q]
        state_ref[q] = value


def combine(gram, vectors, elements):
    shape = vectors[0].shape
    return pl.pallas_call(
        functools.partial(combine_kernel, elements),
        out_shape=[jax.ShapeDtypeStruct(shape, F32), jax.ShapeDtypeStruct((8, shape[-1]), F32)],
        compiler_params=params(),
    )(gram, *vectors)


def around_x(value, steps):
    count = ALONG_X * ALONG_Z
    return lax.ppermute(value, "sym", [(i, (i + steps * ALONG_Z) % count) for i in range(count)])


def across(value, bits):
    count = ALONG_X * ALONG_Z
    return lax.ppermute(value, "sym", [(i, i ^ bits) for i in range(count)])


def add(*parts):
    total = parts[0].astype(F32)
    for part in parts[1:]:
        total = total + part.astype(F32)
    return total


def reduce_scatter(far, rest):
    prev, own, following = rest
    went_right = around_x(far[0], 1)
    went_left = around_x(far[1], -1)
    from_left = around_x(following.at[0].set(add(following[0], went_right).astype(BF16)), 1)
    from_right = around_x(prev.at[1].set(add(prev[1], went_left).astype(BF16)), -1)
    sums = add(own, from_left, from_right)
    return sums[:, 0], across(sums[:, 1].astype(BF16), 1)


def shards(start_state, left_env, right_env, joining, kept):
    sectors, block = start_state.shape[1], start_state.shape[2]
    half = sectors // HALVES
    count = lax.axis_size("sec")
    sym_index = lax.axis_index("sym")
    me_x, me_z = sym_index // ALONG_Z, sym_index % ALONG_Z
    section = lax.axis_index("sec")
    where = jnp.stack([section == count - 1, section % 2 == 1]).astype(jnp.int32)
    parts = next_section(right_env[0])
    left = left_env[0]
    table = lax.dynamic_slice_in_dim(joining[0], sym_index * sectors, sectors, 1)
    device, place = table // sectors, table % sectors
    piece = ((device // ALONG_Z - me_x + 2) % ALONG_X) * HALVES + place // half
    slots = (piece * ALONG_Z + (device % ALONG_Z - me_z) % ALONG_Z) * half + place % half
    per = HALVES * ALONG_Z * half
    far_pairs, rest_pairs = pair_up(slots, 0, per), pair_up(slots, per, ALONG_X * per)
    limits = kept[0]

    far_shape = (ALONG_Z, half, block, block)
    rest_shape = (HALVES * ALONG_Z, half, block, block)
    sources = [start_state[0]]
    vectors, rows, right = [], [], None
    for step in range(ITERS):
        vector, middle = apply_left(step == 0, limits, sources, left)
        if right is None:
            right = gather_right(where, right_env[0], parts)
        far = sum_targets(far_pairs, middle, right, [far_shape] * HALVES, 0.25)
        rest = sum_targets(rest_pairs, middle, right, [rest_shape] * (ALONG_X - 1), 0.75)
        rest = [r.reshape((HALVES,) + far_shape) for r in rest]
        vectors.append(vector)
        rows.append(row_dots(vectors))
        sources = reduce_scatter(far, rest)
    vector, last_rows = last_vector(limits, *sources, vectors)
    gram = jnp.concatenate(rows + [last_rows], axis=0)
    gram = (gram + across(gram, 2)) + (across(gram, 4) + across(gram, 6))
    gram = gram + across(gram, 1)
    elements = sectors * ALONG_X * ALONG_Z * block * block
    state, energy = combine(gram, vectors + [vector], elements)
    return (state[None], energy[0, :1])


def solution(mesh):
    return jax.shard_map(
        shards,
        mesh=mesh,
        in_specs=(
            P("sec", "sym", None, None),
            P("sec", None, "sym", None, None),
            P("sec", None, "sym", None, None),
            P("sec", None, None),
            P("sec", "sym"),
        ),
        out_specs=(P("sec", "sym", None, None), P("sec")),
        check_vma=False,
    )
```

time: 295 us -> 263 us (0.89)
  the two profiles are of different devices: /device:TPU:24 before, /device:TPU:8 now
where the time goes in v2:
time: 263 us
  waiting for transfers between devices  129 us (49%)
  starting transfers between devices  78 us (30%)
  Pallas kernels  44.8 us (17%)
  local copies, waits for them, and re-layouts  4.41 us (2%)
  other arithmetic  3.66 us (1%)
    ppermute x16, waiting for transfers between devices, around_x(): lax.ppermute(value, 'sym', [(i, (i + steps * ALONG_Z) % count) for i in r...  45 us
    ppermute x8, waiting for transfers between devices, across(): return lax.ppermute(value, 'sym', [(i, i ^ bits) for i in range(count)])  43.2 us
    ppermute x8, starting transfers between devices, across(): return lax.ppermute(value, 'sym', [(i, i ^ bits) for i in range(count)])  35.9 us
    ppermute x16, starting transfers between devices, around_x(): lax.ppermute(value, 'sym', [(i, (i + steps * ALONG_Z) % count) for i in r...  29.1 us
    ppermute x2, waiting for transfers between devices, next_section(): lax.ppermute(around, 'sec', [(after(s, steps), after(s, steps + 1)) for s...  25.9 us
    pallas_call x8, Pallas kernels, sum_targets(): pl.pallas_call(target_kernel, in_specs=[pl.BlockSpec(memory_space=pltpu.S...  23.8 us
    ppermute x2, waiting for transfers between devices, next_section(): parts = [lax.ppermute(part, 'sec', pairs) for part in straight]  15.3 us
    pallas_call x4, Pallas kernels, apply_left(): pl.pallas_call(functools.partial(middle_kernel, first), in_specs=[pl.Bloc...  9.52 us
  transfers between devices with their start and end apart: 30, of which 20 were waited for; matrix products, arithmetic and copies ran while one was open for 1% of the time, Pallas kernels for 7%

profile of v2, /device:TPU:8, one launch (start us, length us, event | category | flops | bytes accessed | tf_op | source)
XLA Modules:
  0.0 262.8 jit_solution(1007190481061122414)
XLA Ops:
  0.7 5.8 %shard_map.70 = (bf16[10,8,128,128]{3,2,1,0:T(8,128)(2,1)}, bf16[9,8,128,128]{3,2,1,0:T(8,128)(2,1)}, bf16[5,8,128,128]{3,2,1,0:T(8,128)(2,1)}) custom-call(bf16[24,8,128,128]{3,2,1,0:T(8,128)(2,1)} %bitcast.82), custom_call_target="tpu_custom_call" | custom-call | tf_op jit(solution)/shard_map/pallas_call | solution.py:95
  6.4 4.6 %collective-permute-start.3 = (bf16[5,8,128,128]{3,2,1,0:T(8,128)(2,1)}, bf16[5,8,128,128]{3,2,1,0:T(8,128)(2,1)}, u32[]{:S(2)}, u32[]{:S(2)}) collective-permute-start(bf16[5,8,128,128]{3,2,1,0:T(8,128)(2,1)} %get-tuple-element.137), channel_id=1, source_target_pairs={{16,32},{32,48},{48,0},{64,80},{80,96},{96,112},{112,64},{128,144}... | collective-permute-start | bytes 3932168 | tf_op jit(solution)/shard_map/ppermute | solution.py:118
  17.3 8.1 %collective-permute-done.3 = bf16[5,8,128,128]{3,2,1,0:T(8,128)(2,1)} collective-permute-done((bf16[5,8,128,128]{3,2,1,0:T(8,128)(2,1)}, bf16[5,8,128,128]{3,2,1,0:T(8,128)(2,1)}, u32[]{:S(2)}, u32[]{:S(2)}) %collective-permute-start.3) | collective-permute-done | bytes 1310752 | tf_op jit(solution)/shard_map/ppermute | solution.py:118
  29.6 17.9 %collective-permute-done.4 = bf16[5,8,128,128]{3,2,1,0:T(8,128)(2,1)} collective-permute-done((bf16[5,8,128,128]{3,2,1,0:T(8,128)(2,1)}, bf16[5,8,128,128]{3,2,1,0:T(8,128)(2,1)}, u32[]{:S(2)}, u32[]{:S(2)}) %collective-permute-start.4) | collective-permute-done | bytes 1310752 | tf_op jit(solution)/shard_map/ppermute | solution.py:118
  54.4 15.3 %collective-permute-done.1.refs_1_ = bf16[9,8,128,128]{3,2,1,0:T(8,128)(2,1)} collective-permute-done((bf16[9,8,128,128]{3,2,1,0:T(8,128)(2,1)}, bf16[9,8,128,128]{3,2,1,0:T(8,128)(2,1)}, u32[]{:S(2)}, u32[]{:S(2)}) %collective-permute-start.1) | collective-permute-done | bytes 2359328 | tf_op jit(solution)/shard_map/ppermute | solution.py:109
  78.1 3.6 %shard_map.72 = (bf16[4,4,128,128]{3,2,1,0:T(8,128)(2,1)S(1)}, bf16[4,4,128,128]{3,2,1,0:T(8,128)(2,1)S(1)}, bf16[4,4,128,128]{3,2,1,0:T(8,128)(2,1)S(1)}) custom-call(s32[4,144]{1,0:T(4,128)S(1)} %add_add_fusion.1.pairs_ref, bf16[193,128,128]{2,1,0:T(8,128)(2,1)S(1)} %get-tuple-element.134.middle_ref, bf16[24,8,128,128]{3,2,1,0:T(8,128)(2,1)S(1)} %shard_map.71.right_ref), custom_call_target="tpu_custom_call" | custom-call | flops 4831838208 | bytes 1048576 | tf_op jit(solution)/shard_map/pallas_call | solution.py:193
  87.3 12.1 %collective-permute-done.7 = bf16[2,2,4,128,128]{4,3,2,0,1:T(8,128)(2,1)S(1)} collective-permute-done((bf16[2,2,4,128,128]{4,3,2,0,1:T(8,128)(2,1)S(1)}, bf16[2,2,4,128,128]{4,3,2,0,1:T(8,128)(2,1)S(1)}, u32[]{:S(2)}, u32[]{:S(2)}) %collective-permute-start.7) | collective-permute-done | bytes 524320 | tf_op jit(solution)/shard_map/ppermute | solution.py:323
  99.7 5.3 %collective-permute-start.10 = (bf16[2,4,128,128]{3,2,1,0:T(8,128)(2,1)S(1)}, bf16[2,4,128,128]{3,2,1,0:T(8,128)(2,1)S(1)}, u32[]{:S(2)}, u32[]{:S(2)}) collective-permute-start(bf16[2,4,128,128]{3,2,1,0:T(8,128)(2,1)S(1)} %fusion.20), channel_id=1, source_target_pairs={{0,1},{1,0},{2,3},{3,2},{4,5},{5,4},{6,7},{7,6},{8,9},{9,8},{10,11... | collective-permute-start | bytes 786440 | tf_op jit(solution)/shard_map/ppermute | solution.py:328
  105.1 7.5 %collective-permute-done.10.refs_1_ = bf16[2,4,128,128]{3,2,1,0:T(8,128)(2,1)S(1)} collective-permute-done((bf16[2,4,128,128]{3,2,1,0:T(8,128)(2,1)S(1)}, bf16[2,4,128,128]{3,2,1,0:T(8,128)(2,1)S(1)}, u32[]{:S(2)}, u32[]{:S(2)}) %collective-permute-start.10) | collective-permute-done | bytes 262176 | tf_op jit(solution)/shard_map/ppermute | solution.py:328
  117.4 5.1 %collective-permute-start.11 = (bf16[2,4,128,128]{3,2,1,0:T(8,128)(2,1)S(1)}, bf16[2,4,128,128]{3,2,1,0:T(8,128)(2,1)S(1)}, u32[]{:S(2)}, u32[]{:S(2)}) collective-permute-start(bf16[2,4,128,128]{3,2,1,0:T(8,128)(2,1)S(1)} %get-tuple-element.147), channel_id=1, source_target_pairs={{0,2},{1,3},{2,4},{3,5},{4,6},{5,7},{6,0},{7,1},{8,10},{9,11},{10,... | collective-permute-start | bytes 786440 | tf_op jit(solution)/shard_map/ppermute | solution.py:323
  122.5 3.6 %shard_map.76 = (bf16[4,4,128,128]{3,2,1,0:T(8,128)(2,1)S(1)}, bf16[4,4,128,128]{3,2,1,0:T(8,128)(2,1)S(1)}, bf16[4,4,128,128]{3,2,1,0:T(8,128)(2,1)S(1)}) custom-call(s32[4,144]{1,0:T(4,128)S(1)} %add_add_fusion.1.pairs_ref, bf16[193,128,128]{2,1,0:T(8,128)(2,1)S(1)} %get-tuple-element.144.middle_ref, bf16[24,8,128,128]{3,2,1,0:T(8,128)(2,1)S(1)} %shard_map.71.right_ref), custom_call_target="tpu_custom_call" | custom-call | flops 4831838208 | bytes 1048576 | tf_op jit(solution)/shard_map/pallas_call | solution.py:193
  132.1 10.4 %collective-permute-done.12 = bf16[2,2,4,128,128]{4,3,2,0,1:T(8,128)(2,1)S(1)} collective-permute-done((bf16[2,2,4,128,128]{4,3,2,0,1:T(8,128)(2,1)S(1)}, bf16[2,2,4,128,128]{4,3,2,0,1:T(8,128)(2,1)S(1)}, u32[]{:S(2)}, u32[]{:S(2)}) %collective-permute-start.12) | collective-permute-done | bytes 524320 | tf_op jit(solution)/shard_map/ppermute | solution.py:323
  143.9 7.9 %collective-permute-start.15 = (bf16[2,4,128,128]{3,2,1,0:T(8,128)(2,1)S(1)}, bf16[2,4,128,128]{3,2,1,0:T(8,128)(2,1)S(1)}, u32[]{:S(2)}, u32[]{:S(2)}) collective-permute-start(bf16[2,4,128,128]{3,2,1,0:T(8,128)(2,1)S(1)} %fusion.21), channel_id=1, source_target_pairs={{0,1},{1,0},{2,3},{3,2},{4,5},{5,4},{6,7},{7,6},{8,9},{9,8},{10,11... | collective-permute-start | bytes 786440 | tf_op jit(solution)/shard_map/ppermute | solution.py:328
  151.9 9.5 %collective-permute-done.15.refs_1_ = bf16[2,4,128,128]{3,2,1,0:T(8,128)(2,1)S(1)} collective-permute-done((bf16[2,4,128,128]{3,2,1,0:T(8,128)(2,1)S(1)}, bf16[2,4,128,128]{3,2,1,0:T(8,128)(2,1)S(1)}, u32[]{:S(2)}, u32[]{:S(2)}) %collective-permute-start.15) | collective-permute-done | bytes 262176 | tf_op jit(solution)/shard_map/ppermute | solution.py:328
  169.4 3.6 %shard_map.80 = (bf16[4,4,128,128]{3,2,1,0:T(8,128)(2,1)S(1)}, bf16[4,4,128,128]{3,2,1,0:T(8,128)(2,1)S(1)}, bf16[4,4,128,128]{3,2,1,0:T(8,128)(2,1)S(1)}) custom-call(s32[4,144]{1,0:T(4,128)S(1)} %add_add_fusion.1.pairs_ref, bf16[193,128,128]{2,1,0:T(8,128)(2,1)S(1)} %get-tuple-element.151.middle_ref, bf16[24,8,128,128]{3,2,1,0:T(8,128)(2,1)S(1)} %shard_map.71.right_ref), custom_call_target="tpu_custom_call" | custom-call | flops 4831838208 | bytes 1048576 | tf_op jit(solution)/shard_map/pallas_call | solution.py:193
  180.4 6.7 %collective-permute-done.17 = bf16[2,2,4,128,128]{4,3,2,0,1:T(8,128)(2,1)S(1)} collective-permute-done((bf16[2,2,4,128,128]{4,3,2,0,1:T(8,128)(2,1)S(1)}, bf16[2,2,4,128,128]{4,3,2,0,1:T(8,128)(2,1)S(1)}, u32[]{:S(2)}, u32[]{:S(2)}) %collective-permute-start.17) | collective-permute-done | bytes 524320 | tf_op jit(solution)/shard_map/ppermute | solution.py:323
  187.4 5.9 %collective-permute-start.20 = (bf16[2,4,128,128]{3,2,1,0:T(8,128)(2,1)S(1)}, bf16[2,4,128,128]{3,2,1,0:T(8,128)(2,1)S(1)}, u32[]{:S(2)}, u32[]{:S(2)}) collective-permute-start(bf16[2,4,128,128]{3,2,1,0:T(8,128)(2,1)S(1)} %fusion.22), channel_id=1, source_target_pairs={{0,1},{1,0},{2,3},{3,2},{4,5},{5,4},{6,7},{7,6},{8,9},{9,8},{10,11... | collective-permute-start | bytes 786440 | tf_op jit(solution)/shard_map/ppermute | solution.py:328
  193.3 9.5 %collective-permute-done.20.refs_1_ = bf16[2,4,128,128]{3,2,1,0:T(8,128)(2,1)S(1)} collective-permute-done((bf16[2,4,128,128]{3,2,1,0:T(8,128)(2,1)S(1)}, bf16[2,4,128,128]{3,2,1,0:T(8,128)(2,1)S(1)}, u32[]{:S(2)}, u32[]{:S(2)}) %collective-permute-start.20) | collective-permute-done | bytes 262176 | tf_op jit(solution)/shard_map/ppermute | solution.py:328
  210.8 3.6 %shard_map.84 = (bf16[4,4,128,128]{3,2,1,0:T(8,128)(2,1)S(1)}, bf16[4,4,128,128]{3,2,1,0:T(8,128)(2,1)S(1)}, bf16[4,4,128,128]{3,2,1,0:T(8,128)(2,1)S(1)}) custom-call(s32[4,144]{1,0:T(4,128)S(1)} %add_add_fusion.1.pairs_ref, bf16[193,128,128]{2,1,0:T(8,128)(2,1)S(1)} %get-tuple-element.158.middle_ref, bf16[24,8,128,128]{3,2,1,0:T(8,128)(2,1)S(1)} %shard_map.71.right_ref), custom_call_target="tpu_custom_call" | custom-call | flops 4831838208 | bytes 1048576 | tf_op jit(solution)/shard_map/pallas_call | solution.py:193
  219.5 6.7 %collective-permute-done.22 = bf16[2,2,4,128,128]{4,3,2,0,1:T(8,128)(2,1)S(1)} collective-permute-done((bf16[2,2,4,128,128]{4,3,2,0,1:T(8,128)(2,1)S(1)}, bf16[2,2,4,128,128]{4,3,2,0,1:T(8,128)(2,1)S(1)}, u32[]{:S(2)}, u32[]{:S(2)}) %collective-permute-start.22) | collective-permute-done | bytes 524320 | tf_op jit(solution)/shard_map/ppermute | solution.py:323
  226.5 6.5 %collective-permute-start.25 = (bf16[2,4,128,128]{3,2,1,0:T(8,128)(2,1)S(1)}, bf16[2,4,128,128]{3,2,1,0:T(8,128)(2,1)S(1)}, u32[]{:S(2)}, u32[]{:S(2)}) collective-permute-start(bf16[2,4,128,128]{3,2,1,0:T(8,128)(2,1)S(1)} %fusion.23), channel_id=1, source_target_pairs={{0,1},{1,0},{2,3},{3,2},{4,5},{5,4},{6,7},{7,6},{8,9},{9,8},{10,11... | collective-permute-start | bytes 786440 | tf_op jit(solution)/shard_map/ppermute | solution.py:328
  233.0 9.8 %collective-permute-done.25.refs_1_ = bf16[2,4,128,128]{3,2,1,0:T(8,128)(2,1)S(1)} collective-permute-done((bf16[2,4,128,128]{3,2,1,0:T(8,128)(2,1)S(1)}, bf16[2,4,128,128]{3,2,1,0:T(8,128)(2,1)S(1)}, u32[]{:S(2)}, u32[]{:S(2)}) %collective-permute-start.25) | collective-permute-done | bytes 262176 | tf_op jit(solution)/shard_map/ppermute | solution.py:328
  243.9 4.3 %collective-permute-start.27 = (f32[40,128]{1,0:T(8,128)S(1)}, f32[40,128]{1,0:T(8,128)S(1)}, u32[]{:S(2)}, u32[]{:S(2)}) collective-permute-start(f32[40,128]{1,0:T(8,128)S(1)} %constant_dynamic-update-slice_fusion), channel_id=1, source_target_pairs={{0,4},{1,5},{2,6},{3,7},{4,0},{5,1},{6,2},{7,3},{8,12},{9,13},{10,... | collective-permute-start | bytes 61448 | tf_op jit(solution)/shard_map/ppermute | solution.py:328
  253.2 5.5 %collective-permute-start.29 = (f32[40,128]{1,0:T(8,128)S(1)}, f32[40,128]{1,0:T(8,128)S(1)}, u32[]{:S(2)}, u32[]{:S(2)}) collective-permute-start(f32[40,128]{1,0:T(8,128)S(1)} %add_add_fusion), channel_id=1, source_target_pairs={{0,1},{1,0},{2,3},{3,2},{4,5},{5,4},{6,7},{7,6},{8,9},{9,8},{10,11... | collective-permute-start | bytes 61448 | tf_op jit(solution)/shard_map/ppermute | solution.py:328
  (131 shorter events, 81.5 us)
Async XLA Ops:
  6.4 18.9 %collective-permute-start.3 = (bf16[5,8,128,128]{3,2,1,0:T(8,128)(2,1)}, bf16[5,8,128,128]{3,2,1,0:T(8,128)(2,1)}, u32[]{:S(2)}, u32[]{:S(2)}) collective-permute-start(bf16[5,8,128,128]{3,2,1,0:T(8,128)(2,1)} %get-tuple-element.137), channel_id=1, source_target_pairs={{16,32},{32,48},{48,0},{64,80},{80,96},{96,112},{112,64},{128,144}... | collective-permute-start | bytes 3932168 | tf_op jit(solution)/shard_map/ppermute | solution.py:118
  11.1 43.3 %collective-permute-start.2 = (bf16[5,8,128,128]{3,2,1,0:T(8,128)(2,1)}, bf16[5,8,128,128]{3,2,1,0:T(8,128)(2,1)}, u32[]{:S(2)}, u32[]{:S(2)}) collective-permute-start(bf16[5,8,128,128]{3,2,1,0:T(8,128)(2,1)} %get-tuple-element.137), channel_id=1, source_target_pairs={{8,0},{24,16},{40,32},{56,48},{72,64},{88,80},{104,96},{120,112},{... | collective-permute-start | bytes 3932168 | tf_op jit(solution)/shard_map/ppermute | solution.py:110
  12.3 57.3 %collective-permute-start = (bf16[10,8,128,128]{3,2,1,0:T(8,128)(2,1)}, bf16[10,8,128,128]{3,2,1,0:T(8,128)(2,1)S(1)}, u32[]{:S(2)}, u32[]{:S(2)}) collective-permute-start(bf16[10,8,128,128]{3,2,1,0:T(8,128)(2,1)} %get-tuple-element.135), channel_id=1, source_target_pairs={{8,0},{16,8},{24,16},{32,24},{40,32},{48,40},{56,48},{64,56},{72,6... | collective-permute-start | bytes 7864328 | tf_op jit(solution)/shard_map/ppermute | solution.py:109
  14.9 54.7 %collective-permute-start.1 = (bf16[9,8,128,128]{3,2,1,0:T(8,128)(2,1)}, bf16[9,8,128,128]{3,2,1,0:T(8,128)(2,1)}, u32[]{:S(2)}, u32[]{:S(2)}) collective-permute-start(bf16[9,8,128,128]{3,2,1,0:T(8,128)(2,1)} %get-tuple-element.136), channel_id=1, source_target_pairs={{8,0},{16,8},{24,16},{32,24},{40,32},{48,40},{56,48},{64,56},{72,6... | collective-permute-start | bytes 7077896 | tf_op jit(solution)/shard_map/ppermute | solution.py:109
  25.4 22.1 %collective-permute-start.4 = (bf16[5,8,128,128]{3,2,1,0:T(8,128)(2,1)}, bf16[5,8,128,128]{3,2,1,0:T(8,128)(2,1)}, u32[]{:S(2)}, u32[]{:S(2)}) collective-permute-start(bf16[5,8,128,128]{3,2,1,0:T(8,128)(2,1)} %collective-permute-done.3), channel_id=1, source_target_pairs={{32,48},{48,0},{0,16},{80,96},{96,112},{112,64},{64,80},{144,160},... | collective-permute-start | bytes 3932168 | tf_op jit(solution)/shard_map/ppermute | solution.py:118
  47.5 22.2 %collective-permute-start.5 = (bf16[5,8,128,128]{3,2,1,0:T(8,128)(2,1)}, bf16[5,8,128,128]{3,2,1,0:T(8,128)(2,1)S(1)}, u32[]{:S(2)}, u32[]{:S(2)}) collective-permute-start(bf16[5,8,128,128]{3,2,1,0:T(8,128)(2,1)} %collective-permute-done.4), channel_id=1, source_target_pairs={{48,8},{0,24},{16,40},{96,56},{112,72},{64,88},{80,104},{160,120},... | collective-permute-start | bytes 3932168 | tf_op jit(solution)/shard_map/ppermute | solution.py:119
  74.8 8.8 %collective-permute-start.6 = (bf16[2,4,128,128]{3,2,1,0:T(8,128)(2,1)S(1)}, bf16[2,4,128,128]{3,2,1,0:T(8,128)(2,1)S(1)}, u32[]{:S(2)}, u32[]{:S(2)}) collective-permute-start(bf16[2,4,128,128]{3,2,1,0:T(8,128)(2,1)S(1)} %get-tuple-element.140), channel_id=1, source_target_pairs={{0,2},{1,3},{2,4},{3,5},{4,6},{5,7},{6,0},{7,1},{8,10},{9,11},{10,... | collective-permute-start | bytes 786440 | tf_op jit(solution)/shard_map/ppermute | solution.py:323
  75.2 8.6 %collective-permute-start.8 = (bf16[2,4,128,128]{3,2,1,0:T(8,128)(2,1)S(1)}, bf16[2,4,128,128]{3,2,1,0:T(8,128)(2,1)S(1)}, u32[]{:S(2)}, u32[]{:S(2)}) collective-permute-start(bf16[2,4,128,128]{3,2,1,0:T(8,128)(2,1)S(1)} %get-tuple-element.142), channel_id=1, source_target_pairs={{0,6},{1,7},{2,0},{3,1},{4,2},{5,3},{6,4},{7,5},{8,14},{9,15},{10,... | collective-permute-start | bytes 786440 | tf_op jit(solution)/shard_map/ppermute | solution.py:323
  83.7 15.7 %collective-permute-start.7 = (bf16[2,2,4,128,128]{4,3,2,0,1:T(8,128)(2,1)S(1)}, bf16[2,2,4,128,128]{4,3,2,0,1:T(8,128)(2,1)S(1)}, u32[]{:S(2)}, u32[]{:S(2)}) collective-permute-start(bf16[2,2,4,128,128]{4,3,2,0,1:T(8,128)(2,1)S(1)} %fusion.5), channel_id=1, source_target_pairs={{0,2},{1,3},{2,4},{3,5},{4,6},{5,7},{6,0},{7,1},{8,10},{9,11},{10,... | collective-permute-start | bytes 1572872 | tf_op jit(solution)/shard_map/ppermute | solution.py:323
  83.9 15.6 %collective-permute-start.9 = (bf16[2,2,4,128,128]{4,3,2,0,1:T(8,128)(2,1)S(1)}, bf16[2,2,4,128,128]{4,3,2,0,1:T(8,128)(2,1)S(1)}, u32[]{:S(2)}, u32[]{:S(2)}) collective-permute-start(bf16[2,2,4,128,128]{4,3,2,0,1:T(8,128)(2,1)S(1)} %fusion.7), channel_id=1, source_target_pairs={{0,6},{1,7},{2,0},{3,1},{4,2},{5,3},{6,4},{7,5},{8,14},{9,15},{10,... | collective-permute-start | bytes 1572872 | tf_op jit(solution)/shard_map/ppermute | solution.py:323
  99.7 12.8 %collective-permute-start.10 = (bf16[2,4,128,128]{3,2,1,0:T(8,128)(2,1)S(1)}, bf16[2,4,128,128]{3,2,1,0:T(8,128)(2,1)S(1)}, u32[]{:S(2)}, u32[]{:S(2)}) collective-permute-start(bf16[2,4,128,128]{3,2,1,0:T(8,128)(2,1)S(1)} %fusion.20), channel_id=1, source_target_pairs={{0,1},{1,0},{2,3},{3,2},{4,5},{5,4},{6,7},{7,6},{8,9},{9,8},{10,11... | collective-permute-start | bytes 786440 | tf_op jit(solution)/shard_map/ppermute | solution.py:328
  117.4 10.8 %collective-permute-start.11 = (bf16[2,4,128,128]{3,2,1,0:T(8,128)(2,1)S(1)}, bf16[2,4,128,128]{3,2,1,0:T(8,128)(2,1)S(1)}, u32[]{:S(2)}, u32[]{:S(2)}) collective-permute-start(bf16[2,4,128,128]{3,2,1,0:T(8,128)(2,1)S(1)} %get-tuple-element.147), channel_id=1, source_target_pairs={{0,2},{1,3},{2,4},{3,5},{4,6},{5,7},{6,0},{7,1},{8,10},{9,11},{10,... | collective-permute-start | bytes 786440 | tf_op jit(solution)/shard_map/ppermute | solution.py:323
  122.5 8.3 %collective-permute-start.13 = (bf16[2,4,128,128]{3,2,1,0:T(8,128)(2,1)S(1)}, bf16[2,4,128,128]{3,2,1,0:T(8,128)(2,1)S(1)}, u32[]{:S(2)}, u32[]{:S(2)}) collective-permute-start(bf16[2,4,128,128]{3,2,1,0:T(8,128)(2,1)S(1)} %get-tuple-element.149), channel_id=1, source_target_pairs={{0,6},{1,7},{2,0},{3,1},{4,2},{5,3},{6,4},{7,5},{8,14},{9,15},{10,... | collective-permute-start | bytes 786440 | tf_op jit(solution)/shard_map/ppermute | solution.py:323
  128.3 14.2 %collective-permute-start.12 = (bf16[2,2,4,128,128]{4,3,2,0,1:T(8,128)(2,1)S(1)}, bf16[2,2,4,128,128]{4,3,2,0,1:T(8,128)(2,1)S(1)}, u32[]{:S(2)}, u32[]{:S(2)}) collective-permute-start(bf16[2,2,4,128,128]{4,3,2,0,1:T(8,128)(2,1)S(1)} %fusion.9), channel_id=1, source_target_pairs={{0,2},{1,3},{2,4},{3,5},{4,6},{5,7},{6,0},{7,1},{8,10},{9,11},{10,... | collective-permute-start | bytes 1572872 | tf_op jit(solution)/shard_map/ppermute | solution.py:323
  131.0 12.7 %collective-permute-start.14 = (bf16[2,2,4,128,128]{4,3,2,0,1:T(8,128)(2,1)S(1)}, bf16[2,2,4,128,128]{4,3,2,0,1:T(8,128)(2,1)S(1)}, u32[]{:S(2)}, u32[]{:S(2)}) collective-permute-start(bf16[2,2,4,128,128]{4,3,2,0,1:T(8,128)(2,1)S(1)} %fusion.11), channel_id=1, source_target_pairs={{0,6},{1,7},{2,0},{3,1},{4,2},{5,3},{6,4},{7,5},{8,14},{9,15},{10,... | collective-permute-start | bytes 1572872 | tf_op jit(solution)/shard_map/ppermute | solution.py:323
  143.9 17.4 %collective-permute-start.15 = (bf16[2,4,128,128]{3,2,1,0:T(8,128)(2,1)S(1)}, bf16[2,4,128,128]{3,2,1,0:T(8,128)(2,1)S(1)}, u32[]{:S(2)}, u32[]{:S(2)}) collective-permute-start(bf16[2,4,128,128]{3,2,1,0:T(8,128)(2,1)S(1)} %fusion.21), channel_id=1, source_target_pairs={{0,1},{1,0},{2,3},{3,2},{4,5},{5,4},{6,7},{7,6},{8,9},{9,8},{10,11... | collective-permute-start | bytes 786440 | tf_op jit(solution)/shard_map/ppermute | solution.py:328
  166.1 10.5 %collective-permute-start.16 = (bf16[2,4,128,128]{3,2,1,0:T(8,128)(2,1)S(1)}, bf16[2,4,128,128]{3,2,1,0:T(8,128)(2,1)S(1)}, u32[]{:S(2)}, u32[]{:S(2)}) collective-permute-start(bf16[2,4,128,128]{3,2,1,0:T(8,128)(2,1)S(1)} %get-tuple-element.154), channel_id=1, source_target_pairs={{0,2},{1,3},{2,4},{3,5},{4,6},{5,7},{6,0},{7,1},{8,10},{9,11},{10,... | collective-permute-start | bytes 786440 | tf_op jit(solution)/shard_map/ppermute | solution.py:323
  166.1 10.7 %collective-permute-start.18 = (bf16[2,4,128,128]{3,2,1,0:T(8,128)(2,1)S(1)}, bf16[2,4,128,128]{3,2,1,0:T(8,128)(2,1)S(1)}, u32[]{:S(2)}, u32[]{:S(2)}) collective-permute-start(bf16[2,4,128,128]{3,2,1,0:T(8,128)(2,1)S(1)} %get-tuple-element.156), channel_id=1, source_target_pairs={{0,6},{1,7},{2,0},{3,1},{4,2},{5,3},{6,4},{7,5},{8,14},{9,15},{10,... | collective-permute-start | bytes 786440 | tf_op jit(solution)/shard_map/ppermute | solution.py:323
  176.7 10.5 %collective-permute-start.17 = (bf16[2,2,4,128,128]{4,3,2,0,1:T(8,128)(2,1)S(1)}, bf16[2,2,4,128,128]{4,3,2,0,1:T(8,128)(2,1)S(1)}, u32[]{:S(2)}, u32[]{:S(2)}) collective-permute-start(bf16[2,2,4,128,128]{4,3,2,0,1:T(8,128)(2,1)S(1)} %fusion.13), channel_id=1, source_target_pairs={{0,2},{1,3},{2,4},{3,5},{4,6},{5,7},{6,0},{7,1},{8,10},{9,11},{10,... | collective-permute-start | bytes 1572872 | tf_op jit(solution)/shard_map/ppermute | solution.py:323
  176.9 10.3 %collective-permute-start.19 = (bf16[2,2,4,128,128]{4,3,2,0,1:T(8,128)(2,1)S(1)}, bf16[2,2,4,128,128]{4,3,2,0,1:T(8,128)(2,1)S(1)}, u32[]{:S(2)}, u32[]{:S(2)}) collective-permute-start(bf16[2,2,4,128,128]{4,3,2,0,1:T(8,128)(2,1)S(1)} %fusion.15), channel_id=1, source_target_pairs={{0,6},{1,7},{2,0},{3,1},{4,2},{5,3},{6,4},{7,5},{8,14},{9,15},{10,... | collective-permute-start | bytes 1572872 | tf_op jit(solution)/shard_map/ppermute | solution.py:323
  187.4 15.4 %collective-permute-start.20 = (bf16[2,4,128,128]{3,2,1,0:T(8,128)(2,1)S(1)}, bf16[2,4,128,128]{3,2,1,0:T(8,128)(2,1)S(1)}, u32[]{:S(2)}, u32[]{:S(2)}) collective-permute-start(bf16[2,4,128,128]{3,2,1,0:T(8,128)(2,1)S(1)} %fusion.22), channel_id=1, source_target_pairs={{0,1},{1,0},{2,3},{3,2},{4,5},{5,4},{6,7},{7,6},{8,9},{9,8},{10,11... | collective-permute-start | bytes 786440 | tf_op jit(solution)/shard_map/ppermute | solution.py:328
  215.3 10.9 %collective-permute-start.22 = (bf16[2,2,4,128,128]{4,3,2,0,1:T(8,128)(2,1)S(1)}, bf16[2,2,4,128,128]{4,3,2,0,1:T(8,128)(2,1)S(1)}, u32[]{:S(2)}, u32[]{:S(2)}) collective-permute-start(bf16[2,2,4,128,128]{4,3,2,0,1:T(8,128)(2,1)S(1)} %fusion.17), channel_id=1, source_target_pairs={{0,2},{1,3},{2,4},{3,5},{4,6},{5,7},{6,0},{7,1},{8,10},{9,11},{10,... | collective-permute-start | bytes 1572872 | tf_op jit(solution)/shard_map/ppermute | solution.py:323
  215.5 10.7 %collective-permute-start.24 = (bf16[2,2,4,128,128]{4,3,2,0,1:T(8,128)(2,1)S(1)}, bf16[2,2,4,128,128]{4,3,2,0,1:T(8,128)(2,1)S(1)}, u32[]{:S(2)}, u32[]{:S(2)}) collective-permute-start(bf16[2,2,4,128,128]{4,3,2,0,1:T(8,128)(2,1)S(1)} %fusion.19), channel_id=1, source_target_pairs={{0,6},{1,7},{2,0},{3,1},{4,2},{5,3},{6,4},{7,5},{8,14},{9,15},{10,... | collective-permute-start | bytes 1572872 | tf_op jit(solution)/shard_map/ppermute | solution.py:323
  226.5 16.3 %collective-permute-start.25 = (bf16[2,4,128,128]{3,2,1,0:T(8,128)(2,1)S(1)}, bf16[2,4,128,128]{3,2,1,0:T(8,128)(2,1)S(1)}, u32[]{:S(2)}, u32[]{:S(2)}) collective-permute-start(bf16[2,4,128,128]{3,2,1,0:T(8,128)(2,1)S(1)} %fusion.23), channel_id=1, source_target_pairs={{0,1},{1,0},{2,3},{3,2},{4,5},{5,4},{6,7},{7,6},{8,9},{9,8},{10,11... | collective-permute-start | bytes 786440 | tf_op jit(solution)/shard_map/ppermute | solution.py:328
  (14 other events, 271.1 us)

commit v3 on v2

--- a/solution.py
+++ b/solution.py
@@ -11,7 +11,7 @@
 STEP = 0.15
 SCALE = 2.0**-8
 GROUP = 16
-STRAIGHT = (10, 9)
+STRAIGHT = (2, 10, 8)
 ALONG_X = 4
 ALONG_Y = 4
 ALONG_Z = 2
@@ -76,37 +76,32 @@
     )(where, here, *parts)
 
 
-def cut_kernel(value_ref, *refs):
-    parts, arrived = refs[:-1], refs[-1]
-    low, copies = 0, []
-    for part in parts:
-        for at in range(0, part.shape[0], 2):
-            here = pl.ds(at, min(2, part.shape[0] - at))
-            there = pl.ds(low + at, here.size)
-            copies.append(pltpu.make_async_copy(value_ref.at[there], part.at[here], arrived.at[len(copies)]))
-        low += part.shape[0]
-    for copy in copies:
-        copy.start()
-    for copy in copies:
-        copy.wait()
-
-
-def cut(value, lengths):
-    return pl.pallas_call(
-        cut_kernel,
-        in_specs=[pl.BlockSpec(memory_space=pltpu.HBM)],
-        out_specs=[pl.BlockSpec(memory_space=pltpu.VMEM)] * len(lengths),
-        out_shape=[jax.ShapeDtypeStruct((n,) + value.shape[1:], value.dtype) for n in lengths],
-        scratch_shapes=[pltpu.SemaphoreType.DMA((value.shape[0],))],
+def cut_kernel(low, value_ref, after_ref, part_ref, arrived):
+    copy = pltpu.make_async_copy(value_ref.at[pl.ds(low, part_ref.shape[0])], part_ref, arrived)
+    copy.start()
+    copy.wait()
+
+
+def cut(value, low, after):
+    shape = (value.shape[0] - low,) + value.shape[1:]
+    return pl.pallas_call(
+        functools.partial(cut_kernel, low),
+        in_specs=[pl.BlockSpec(memory_space=pltpu.HBM), pl.BlockSpec(memory_space=pl.ANY)],
+        out_specs=pl.BlockSpec(memory_space=pltpu.VMEM),
+        out_shape=jax.ShapeDtypeStruct(shape, value.dtype),
+        scratch_shapes=[pltpu.SemaphoreType.DMA],
         compiler_params=params(59),
-    )(value)
+    )(value, after)
 
 
 def next_section(value):
     count = lax.axis_size("sec")
     pairs = [(s, s - 1) for s in range(1, count)]
-    *straight, rest = cut(value, STRAIGHT + (value.shape[0] - sum(STRAIGHT),))
-    parts = [lax.ppermute(part, "sec", pairs) for part in straight]
+    low, parts = 0, []
+    for length in STRAIGHT:
+        parts.append(lax.ppermute(value[low : low + length], "sec", pairs))
+        low += length
+    rest = cut(value, low, parts[0])
     beside = lax.ppermute(rest, "sec", [(s, d) for s, d in pairs if s % 2 == 1])
 
     def after(s, steps):
@@ -353,7 +348,6 @@
     me_x, me_z = sym_index // ALONG_Z, sym_index % ALONG_Z
     section = lax.axis_index("sec")
     where = jnp.stack([section == count - 1, section % 2 == 1]).astype(jnp.int32)
-    parts = next_section(right_env[0])
     left = left_env[0]
     table = lax.dynamic_slice_in_dim(joining[0], sym_index * sectors, sectors, 1)
     device, place = table // sectors, table % sectors
@@ -370,7 +364,7 @@
     for step in range(ITERS):
         vector, middle = apply_left(step == 0, limits, sources, left)
         if right is None:
-            right = gather_right(where, right_env[0], parts)
+            right = gather_right(where, right_env[0], next_section(right_env[0]))
         far = sum_targets(far_pairs, middle, right, [far_shape] * HALVES, 0.25)
         rest = sum_targets(rest_pairs, middle, right, [rest_shape] * (ALONG_X - 1), 0.75)
         rest = [r.reshape((HALVES,) + far_shape) for r in rest]

time: 263 us -> 256 us (0.973)
  the two profiles are of different devices: /device:TPU:8 before, /device:TPU:40 now
where the time goes in v3:
time: 256 us; the launch traced here: 255 us
  waiting for transfers between devices  127 us (50%)
  starting transfers between devices  68.6 us (27%)
  Pallas kernels  39.6 us (15%)
  local copies, waits for them, and re-layouts  13 us (5%)
  other arithmetic  3.75 us (1%)
  between operations  2.57 us (1%)
    ppermute x16, waiting for transfers between devices, around_x(): lax.ppermute(value, 'sym', [(i, (i + steps * ALONG_Z) % count) for i in r...  50.8 us
    ppermute x8, waiting for transfers between devices, across(): return lax.ppermute(value, 'sym', [(i, i ^ bits) for i in range(count)])  50.1 us
    ppermute x16, starting transfers between devices, around_x(): lax.ppermute(value, 'sym', [(i, (i + steps * ALONG_Z) % count) for i in r...  27.9 us
    ppermute x8, starting transfers between devices, across(): return lax.ppermute(value, 'sym', [(i, i ^ bits) for i in range(count)])  24.7 us
    pallas_call x8, Pallas kernels, sum_targets(): pl.pallas_call(target_kernel, in_specs=[pl.BlockSpec(memory_space=pltpu.S...  22 us
    ppermute x2, waiting for transfers between devices, next_section(): lax.ppermute(around, 'sec', [(after(s, steps), after(s, steps + 1)) for s...  18.7 us
    pallas_call x4, Pallas kernels, apply_left(): pl.pallas_call(functools.partial(middle_kernel, first), in_specs=[pl.Bloc...  9.53 us
    slice x3, local copies, waits for them, and re-layouts, next_section(): parts.append(lax.ppermute(value[low:low + length], 'sec', pairs))  7.93 us
  transfers between devices with their start and end apart: 31, of which 22 were waited for; matrix products, arithmetic and copies ran while one was open for 4% of the time, Pallas kernels for 8%

profile of v3, /device:TPU:40, one launch (start us, length us, event | category | flops | bytes accessed | tf_op | source)
XLA Modules:
  0.0 254.7 jit_solution(14690410214127846828)
XLA Ops:
  3.6 3.6 %slice_bitcast_fusion = bf16[10,8,128,128]{3,2,1,0:T(8,128)(2,1)} fusion(bf16[1,24,8,128,128]{4,3,2,1,0:T(8,128)(2,1)} %param.23), kind=kLoop, calls=%fused_computation | loop fusion | bytes 5242880 | tf_op jit(solution)/shard_map/slice | solution.py:102
  13.3 3.5 %collective-permute-start.4 = (bf16[4,8,128,128]{3,2,1,0:T(8,128)(2,1)}, bf16[4,8,128,128]{3,2,1,0:T(8,128)(2,1)}, u32[]{:S(2)}, u32[]{:S(2)}) collective-permute-start(bf16[4,8,128,128]{3,2,1,0:T(8,128)(2,1)} %shard_map.70), channel_id=1, source_target_pairs={{16,32},{32,48},{48,0},{64,80},{80,96},{96,112},{112,64},{128,144}... | collective-permute-start | bytes 3145736 | tf_op jit(solution)/shard_map/ppermute | solution.py:113
  23.7 7.1 %collective-permute-done.4 = bf16[4,8,128,128]{3,2,1,0:T(8,128)(2,1)} collective-permute-done((bf16[4,8,128,128]{3,2,1,0:T(8,128)(2,1)}, bf16[4,8,128,128]{3,2,1,0:T(8,128)(2,1)}, u32[]{:S(2)}, u32[]{:S(2)}) %collective-permute-start.4) | collective-permute-done | bytes 1048608 | tf_op jit(solution)/shard_map/ppermute | solution.py:113
  37.4 11.6 %collective-permute-done.5 = bf16[4,8,128,128]{3,2,1,0:T(8,128)(2,1)} collective-permute-done((bf16[4,8,128,128]{3,2,1,0:T(8,128)(2,1)}, bf16[4,8,128,128]{3,2,1,0:T(8,128)(2,1)}, u32[]{:S(2)}, u32[]{:S(2)}) %collective-permute-start.5) | collective-permute-done | bytes 1048608 | tf_op jit(solution)/shard_map/ppermute | solution.py:113
  55.7 6.0 %collective-permute-done.2.refs_2_ = bf16[8,8,128,128]{3,2,1,0:T(8,128)(2,1)} collective-permute-done((bf16[8,8,128,128]{3,2,1,0:T(8,128)(2,1)}, bf16[8,8,128,128]{3,2,1,0:T(8,128)(2,1)}, u32[]{:S(2)}, u32[]{:S(2)}) %collective-permute-start.2) | collective-permute-done | bytes 2097184 | tf_op jit(solution)/shard_map/ppermute | solution.py:102
  71.0 3.7 %shard_map.72 = (bf16[4,4,128,128]{3,2,1,0:T(8,128)(2,1)S(1)}, bf16[4,4,128,128]{3,2,1,0:T(8,128)(2,1)S(1)}, bf16[4,4,128,128]{3,2,1,0:T(8,128)(2,1)S(1)}) custom-call(s32[4,144]{1,0:T(4,128)S(1)} %add_add_fusion.1.pairs_ref, bf16[193,128,128]{2,1,0:T(8,128)(2,1)S(1)} %get-tuple-element.131.middle_ref, bf16[24,8,128,128]{3,2,1,0:T(8,128)(2,1)S(1)} %shard_map.71.right_ref), custom_call_target="tpu_custom_call" | custom-call | flops 4831838208 | bytes 1048576 | tf_op jit(solution)/shard_map/pallas_call | solution.py:188
  79.3 10.8 %collective-permute-done.8 = bf16[2,2,4,128,128]{4,3,2,0,1:T(8,128)(2,1)S(1)} collective-permute-done((bf16[2,2,4,128,128]{4,3,2,0,1:T(8,128)(2,1)S(1)}, bf16[2,2,4,128,128]{4,3,2,0,1:T(8,128)(2,1)S(1)}, u32[]{:S(2)}, u32[]{:S(2)}) %collective-permute-start.8) | collective-permute-done | bytes 524320 | tf_op jit(solution)/shard_map/ppermute | solution.py:318
  90.7 7.3 %collective-permute-start.11 = (bf16[2,4,128,128]{3,2,1,0:T(8,128)(2,1)S(1)}, bf16[2,4,128,128]{3,2,1,0:T(8,128)(2,1)S(1)}, u32[]{:S(2)}, u32[]{:S(2)}) collective-permute-start(bf16[2,4,128,128]{3,2,1,0:T(8,128)(2,1)S(1)} %fusion.20), channel_id=1, source_target_pairs={{0,1},{1,0},{2,3},{3,2},{4,5},{5,4},{6,7},{7,6},{8,9},{9,8},{10,11... | collective-permute-start | bytes 786440 | tf_op jit(solution)/shard_map/ppermute | solution.py:323
  98.0 12.2 %collective-permute-done.11.refs_1_ = bf16[2,4,128,128]{3,2,1,0:T(8,128)(2,1)S(1)} collective-permute-done((bf16[2,4,128,128]{3,2,1,0:T(8,128)(2,1)S(1)}, bf16[2,4,128,128]{3,2,1,0:T(8,128)(2,1)S(1)}, u32[]{:S(2)}, u32[]{:S(2)}) %collective-permute-start.11) | collective-permute-done | bytes 262176 | tf_op jit(solution)/shard_map/ppermute | solution.py:323
  118.8 3.7 %shard_map.76 = (bf16[4,4,128,128]{3,2,1,0:T(8,128)(2,1)S(1)}, bf16[4,4,128,128]{3,2,1,0:T(8,128)(2,1)S(1)}, bf16[4,4,128,128]{3,2,1,0:T(8,128)(2,1)S(1)}) custom-call(s32[4,144]{1,0:T(4,128)S(1)} %add_add_fusion.1.pairs_ref, bf16[193,128,128]{2,1,0:T(8,128)(2,1)S(1)} %get-tuple-element.138.middle_ref, bf16[24,8,128,128]{3,2,1,0:T(8,128)(2,1)S(1)} %shard_map.71.right_ref), custom_call_target="tpu_custom_call" | custom-call | flops 4831838208 | bytes 1048576 | tf_op jit(solution)/shard_map/pallas_call | solution.py:188
  128.9 11.2 %collective-permute-done.13 = bf16[2,2,4,128,128]{4,3,2,0,1:T(8,128)(2,1)S(1)} collective-permute-done((bf16[2,2,4,128,128]{4,3,2,0,1:T(8,128)(2,1)S(1)}, bf16[2,2,4,128,128]{4,3,2,0,1:T(8,128)(2,1)S(1)}, u32[]{:S(2)}, u32[]{:S(2)}) %collective-permute-start.13) | collective-permute-done | bytes 524320 | tf_op jit(solution)/shard_map/ppermute | solution.py:318
  140.4 6.1 %collective-permute-start.16 = (bf16[2,4,128,128]{3,2,1,0:T(8,128)(2,1)S(1)}, bf16[2,4,128,128]{3,2,1,0:T(8,128)(2,1)S(1)}, u32[]{:S(2)}, u32[]{:S(2)}) collective-permute-start(bf16[2,4,128,128]{3,2,1,0:T(8,128)(2,1)S(1)} %fusion.21), channel_id=1, source_target_pairs={{0,1},{1,0},{2,3},{3,2},{4,5},{5,4},{6,7},{7,6},{8,9},{9,8},{10,11... | collective-permute-start | bytes 786440 | tf_op jit(solution)/shard_map/ppermute | solution.py:323
  146.5 7.1 %collective-permute-done.16.refs_1_ = bf16[2,4,128,128]{3,2,1,0:T(8,128)(2,1)S(1)} collective-permute-done((bf16[2,4,128,128]{3,2,1,0:T(8,128)(2,1)S(1)}, bf16[2,4,128,128]{3,2,1,0:T(8,128)(2,1)S(1)}, u32[]{:S(2)}, u32[]{:S(2)}) %collective-permute-start.16) | collective-permute-done | bytes 262176 | tf_op jit(solution)/shard_map/ppermute | solution.py:323
  161.1 3.7 %shard_map.80 = (bf16[4,4,128,128]{3,2,1,0:T(8,128)(2,1)S(1)}, bf16[4,4,128,128]{3,2,1,0:T(8,128)(2,1)S(1)}, bf16[4,4,128,128]{3,2,1,0:T(8,128)(2,1)S(1)}) custom-call(s32[4,144]{1,0:T(4,128)S(1)} %add_add_fusion.1.pairs_ref, bf16[193,128,128]{2,1,0:T(8,128)(2,1)S(1)} %get-tuple-element.145.middle_ref, bf16[24,8,128,128]{3,2,1,0:T(8,128)(2,1)S(1)} %shard_map.71.right_ref), custom_call_target="tpu_custom_call" | custom-call | flops 4831838208 | bytes 1048576 | tf_op jit(solution)/shard_map/pallas_call | solution.py:188
  167.5 3.5 %collective-permute-start.20 = (bf16[2,2,4,128,128]{4,3,2,0,1:T(8,128)(2,1)S(1)}, bf16[2,2,4,128,128]{4,3,2,0,1:T(8,128)(2,1)S(1)}, u32[]{:S(2)}, u32[]{:S(2)}) collective-permute-start(bf16[2,2,4,128,128]{4,3,2,0,1:T(8,128)(2,1)S(1)} %fusion.15), channel_id=1, source_target_pairs={{0,6},{1,7},{2,0},{3,1},{4,2},{5,3},{6,4},{7,5},{8,14},{9,15},{10,... | collective-permute-start | bytes 1572872 | tf_op jit(solution)/shard_map/ppermute | solution.py:318
  171.0 10.4 %collective-permute-done.18 = bf16[2,2,4,128,128]{4,3,2,0,1:T(8,128)(2,1)S(1)} collective-permute-done((bf16[2,2,4,128,128]{4,3,2,0,1:T(8,128)(2,1)S(1)}, bf16[2,2,4,128,128]{4,3,2,0,1:T(8,128)(2,1)S(1)}, u32[]{:S(2)}, u32[]{:S(2)}) %collective-permute-start.18) | collective-permute-done | bytes 524320 | tf_op jit(solution)/shard_map/ppermute | solution.py:318
  181.8 4.6 %collective-permute-start.21 = (bf16[2,4,128,128]{3,2,1,0:T(8,128)(2,1)S(1)}, bf16[2,4,128,128]{3,2,1,0:T(8,128)(2,1)S(1)}, u32[]{:S(2)}, u32[]{:S(2)}) collective-permute-start(bf16[2,4,128,128]{3,2,1,0:T(8,128)(2,1)S(1)} %fusion.22), channel_id=1, source_target_pairs={{0,1},{1,0},{2,3},{3,2},{4,5},{5,4},{6,7},{7,6},{8,9},{9,8},{10,11... | collective-permute-start | bytes 786440 | tf_op jit(solution)/shard_map/ppermute | solution.py:323
  186.4 8.5 %collective-permute-done.21.refs_1_ = bf16[2,4,128,128]{3,2,1,0:T(8,128)(2,1)S(1)} collective-permute-done((bf16[2,4,128,128]{3,2,1,0:T(8,128)(2,1)S(1)}, bf16[2,4,128,128]{3,2,1,0:T(8,128)(2,1)S(1)}, u32[]{:S(2)}, u32[]{:S(2)}) %collective-permute-start.21) | collective-permute-done | bytes 262176 | tf_op jit(solution)/shard_map/ppermute | solution.py:323
  199.2 3.3 %collective-permute-start.24 = (bf16[2,4,128,128]{3,2,1,0:T(8,128)(2,1)S(1)}, bf16[2,4,128,128]{3,2,1,0:T(8,128)(2,1)S(1)}, u32[]{:S(2)}, u32[]{:S(2)}) collective-permute-start(bf16[2,4,128,128]{3,2,1,0:T(8,128)(2,1)S(1)} %get-tuple-element.157), channel_id=1, source_target_pairs={{0,6},{1,7},{2,0},{3,1},{4,2},{5,3},{6,4},{7,5},{8,14},{9,15},{10,... | collective-permute-start | bytes 786440 | tf_op jit(solution)/shard_map/ppermute | solution.py:318
  202.5 3.7 %shard_map.84 = (bf16[4,4,128,128]{3,2,1,0:T(8,128)(2,1)S(1)}, bf16[4,4,128,128]{3,2,1,0:T(8,128)(2,1)S(1)}, bf16[4,4,128,128]{3,2,1,0:T(8,128)(2,1)S(1)}) custom-call(s32[4,144]{1,0:T(4,128)S(1)} %add_add_fusion.1.pairs_ref, bf16[193,128,128]{2,1,0:T(8,128)(2,1)S(1)} %get-tuple-element.152.middle_ref, bf16[24,8,128,128]{3,2,1,0:T(8,128)(2,1)S(1)} %shard_map.71.right_ref), custom_call_target="tpu_custom_call" | custom-call | flops 4831838208 | bytes 1048576 | tf_op jit(solution)/shard_map/pallas_call | solution.py:188
  212.7 9.9 %collective-permute-done.23 = bf16[2,2,4,128,128]{4,3,2,0,1:T(8,128)(2,1)S(1)} collective-permute-done((bf16[2,2,4,128,128]{4,3,2,0,1:T(8,128)(2,1)S(1)}, bf16[2,2,4,128,128]{4,3,2,0,1:T(8,128)(2,1)S(1)}, u32[]{:S(2)}, u32[]{:S(2)}) %collective-permute-start.23) | collective-permute-done | bytes 524320 | tf_op jit(solution)/shard_map/ppermute | solution.py:318
  223.7 10.2 %collective-permute-done.26.refs_1_ = bf16[2,4,128,128]{3,2,1,0:T(8,128)(2,1)S(1)} collective-permute-done((bf16[2,4,128,128]{3,2,1,0:T(8,128)(2,1)S(1)}, bf16[2,4,128,128]{3,2,1,0:T(8,128)(2,1)S(1)}, u32[]{:S(2)}, u32[]{:S(2)}) %collective-permute-start.26) | collective-permute-done | bytes 262176 | tf_op jit(solution)/shard_map/ppermute | solution.py:323
  235.5 4.7 %collective-permute-start.28 = (f32[40,128]{1,0:T(8,128)S(1)}, f32[40,128]{1,0:T(8,128)S(1)}, u32[]{:S(2)}, u32[]{:S(2)}) collective-permute-start(f32[40,128]{1,0:T(8,128)S(1)} %constant_dynamic-update-slice_fusion), channel_id=1, source_target_pairs={{0,4},{1,5},{2,6},{3,7},{4,0},{5,1},{6,2},{7,3},{8,12},{9,13},{10,... | collective-permute-start | bytes 61448 | tf_op jit(solution)/shard_map/ppermute | solution.py:323
  245.9 7.1 %collective-permute-done.30 = f32[40,128]{1,0:T(8,128)S(1)} collective-permute-done((f32[40,128]{1,0:T(8,128)S(1)}, f32[40,128]{1,0:T(8,128)S(1)}, u32[]{:S(2)}, u32[]{:S(2)}) %collective-permute-start.30) | collective-permute-done | bytes 20512 | tf_op jit(solution)/shard_map/ppermute | solution.py:323
  (140 shorter events, 88.5 us)
Async XLA Ops:
  7.3 54.5 %collective-permute-start.1 = (bf16[10,8,128,128]{3,2,1,0:T(8,128)(2,1)}, bf16[10,8,128,128]{3,2,1,0:T(8,128)(2,1)}, u32[]{:S(2)}, u32[]{:S(2)}) collective-permute-start(bf16[10,8,128,128]{3,2,1,0:T(8,128)(2,1)} %slice_bitcast_fusion), channel_id=1, source_target_pairs={{8,0},{16,8},{24,16},{32,24},{40,32},{48,40},{56,48},{64,56},{72,6... | collective-permute-start | bytes 7864328 | tf_op jit(solution)/shard_map/ppermute | solution.py:102
  13.3 17.4 %collective-permute-start.4 = (bf16[4,8,128,128]{3,2,1,0:T(8,128)(2,1)}, bf16[4,8,128,128]{3,2,1,0:T(8,128)(2,1)}, u32[]{:S(2)}, u32[]{:S(2)}) collective-permute-start(bf16[4,8,128,128]{3,2,1,0:T(8,128)(2,1)} %shard_map.70), channel_id=1, source_target_pairs={{16,32},{32,48},{48,0},{64,80},{80,96},{96,112},{112,64},{128,144}... | collective-permute-start | bytes 3145736 | tf_op jit(solution)/shard_map/ppermute | solution.py:113
  20.1 41.7 %collective-permute-start.2 = (bf16[8,8,128,128]{3,2,1,0:T(8,128)(2,1)}, bf16[8,8,128,128]{3,2,1,0:T(8,128)(2,1)}, u32[]{:S(2)}, u32[]{:S(2)}) collective-permute-start(bf16[8,8,128,128]{3,2,1,0:T(8,128)(2,1)} %slice_bitcast_fusion.1), channel_id=1, source_target_pairs={{8,0},{16,8},{24,16},{32,24},{40,32},{48,40},{56,48},{64,56},{72,6... | collective-permute-start | bytes 6291464 | tf_op jit(solution)/shard_map/ppermute | solution.py:102
  30.8 18.2 %collective-permute-start.5 = (bf16[4,8,128,128]{3,2,1,0:T(8,128)(2,1)}, bf16[4,8,128,128]{3,2,1,0:T(8,128)(2,1)}, u32[]{:S(2)}, u32[]{:S(2)}) collective-permute-start(bf16[4,8,128,128]{3,2,1,0:T(8,128)(2,1)} %collective-permute-done.4), channel_id=1, source_target_pairs={{32,48},{48,0},{0,16},{80,96},{96,112},{112,64},{64,80},{144,160},... | collective-permute-start | bytes 3145736 | tf_op jit(solution)/shard_map/ppermute | solution.py:113
  36.1 19.7 %collective-permute-start.3 = (bf16[4,8,128,128]{3,2,1,0:T(8,128)(2,1)}, bf16[4,8,128,128]{3,2,1,0:T(8,128)(2,1)S(1)}, u32[]{:S(2)}, u32[]{:S(2)}) collective-permute-start(bf16[4,8,128,128]{3,2,1,0:T(8,128)(2,1)} %shard_map.70), channel_id=1, source_target_pairs={{8,0},{24,16},{40,32},{56,48},{72,64},{88,80},{104,96},{120,112},{... | collective-permute-start | bytes 3145736 | tf_op jit(solution)/shard_map/ppermute | solution.py:105
  49.0 13.9 %collective-permute-start.6 = (bf16[4,8,128,128]{3,2,1,0:T(8,128)(2,1)}, bf16[4,8,128,128]{3,2,1,0:T(8,128)(2,1)S(1)}, u32[]{:S(2)}, u32[]{:S(2)}) collective-permute-start(bf16[4,8,128,128]{3,2,1,0:T(8,128)(2,1)} %collective-permute-done.5), channel_id=1, source_target_pairs={{48,8},{0,24},{16,40},{96,56},{112,72},{64,88},{80,104},{160,120},... | collective-permute-start | bytes 3145736 | tf_op jit(solution)/shard_map/ppermute | solution.py:114
  75.7 14.4 %collective-permute-start.8 = (bf16[2,2,4,128,128]{4,3,2,0,1:T(8,128)(2,1)S(1)}, bf16[2,2,4,128,128]{4,3,2,0,1:T(8,128)(2,1)S(1)}, u32[]{:S(2)}, u32[]{:S(2)}) collective-permute-start(bf16[2,2,4,128,128]{4,3,2,0,1:T(8,128)(2,1)S(1)} %fusion.5), channel_id=1, source_target_pairs={{0,2},{1,3},{2,4},{3,5},{4,6},{5,7},{6,0},{7,1},{8,10},{9,11},{10,... | collective-permute-start | bytes 1572872 | tf_op jit(solution)/shard_map/ppermute | solution.py:318
  76.3 14.1 %collective-permute-start.10 = (bf16[2,2,4,128,128]{4,3,2,0,1:T(8,128)(2,1)S(1)}, bf16[2,2,4,128,128]{4,3,2,0,1:T(8,128)(2,1)S(1)}, u32[]{:S(2)}, u32[]{:S(2)}) collective-permute-start(bf16[2,2,4,128,128]{4,3,2,0,1:T(8,128)(2,1)S(1)} %fusion.7), channel_id=1, source_target_pairs={{0,6},{1,7},{2,0},{3,1},{4,2},{5,3},{6,4},{7,5},{8,14},{9,15},{10,... | collective-permute-start | bytes 1572872 | tf_op jit(solution)/shard_map/ppermute | solution.py:318
  90.7 19.5 %collective-permute-start.11 = (bf16[2,4,128,128]{3,2,1,0:T(8,128)(2,1)S(1)}, bf16[2,4,128,128]{3,2,1,0:T(8,128)(2,1)S(1)}, u32[]{:S(2)}, u32[]{:S(2)}) collective-permute-start(bf16[2,4,128,128]{3,2,1,0:T(8,128)(2,1)S(1)} %fusion.20), channel_id=1, source_target_pairs={{0,1},{1,0},{2,3},{3,2},{4,5},{5,4},{6,7},{7,6},{8,9},{9,8},{10,11... | collective-permute-start | bytes 786440 | tf_op jit(solution)/shard_map/ppermute | solution.py:323
  114.6 10.7 %collective-permute-start.12 = (bf16[2,4,128,128]{3,2,1,0:T(8,128)(2,1)S(1)}, bf16[2,4,128,128]{3,2,1,0:T(8,128)(2,1)S(1)}, u32[]{:S(2)}, u32[]{:S(2)}) collective-permute-start(bf16[2,4,128,128]{3,2,1,0:T(8,128)(2,1)S(1)} %get-tuple-element.141), channel_id=1, source_target_pairs={{0,2},{1,3},{2,4},{3,5},{4,6},{5,7},{6,0},{7,1},{8,10},{9,11},{10,... | collective-permute-start | bytes 786440 | tf_op jit(solution)/shard_map/ppermute | solution.py:318
  115.6 9.8 %collective-permute-start.14 = (bf16[2,4,128,128]{3,2,1,0:T(8,128)(2,1)S(1)}, bf16[2,4,128,128]{3,2,1,0:T(8,128)(2,1)S(1)}, u32[]{:S(2)}, u32[]{:S(2)}) collective-permute-start(bf16[2,4,128,128]{3,2,1,0:T(8,128)(2,1)S(1)} %get-tuple-element.143), channel_id=1, source_target_pairs={{0,6},{1,7},{2,0},{3,1},{4,2},{5,3},{6,4},{7,5},{8,14},{9,15},{10,... | collective-permute-start | bytes 786440 | tf_op jit(solution)/shard_map/ppermute | solution.py:318
  125.4 14.7 %collective-permute-start.13 = (bf16[2,2,4,128,128]{4,3,2,0,1:T(8,128)(2,1)S(1)}, bf16[2,2,4,128,128]{4,3,2,0,1:T(8,128)(2,1)S(1)}, u32[]{:S(2)}, u32[]{:S(2)}) collective-permute-start(bf16[2,2,4,128,128]{4,3,2,0,1:T(8,128)(2,1)S(1)} %fusion.9), channel_id=1, source_target_pairs={{0,2},{1,3},{2,4},{3,5},{4,6},{5,7},{6,0},{7,1},{8,10},{9,11},{10,... | collective-permute-start | bytes 1572872 | tf_op jit(solution)/shard_map/ppermute | solution.py:318
  125.6 14.5 %collective-permute-start.15 = (bf16[2,2,4,128,128]{4,3,2,0,1:T(8,128)(2,1)S(1)}, bf16[2,2,4,128,128]{4,3,2,0,1:T(8,128)(2,1)S(1)}, u32[]{:S(2)}, u32[]{:S(2)}) collective-permute-start(bf16[2,2,4,128,128]{4,3,2,0,1:T(8,128)(2,1)S(1)} %fusion.11), channel_id=1, source_target_pairs={{0,6},{1,7},{2,0},{3,1},{4,2},{5,3},{6,4},{7,5},{8,14},{9,15},{10,... | collective-permute-start | bytes 1572872 | tf_op jit(solution)/shard_map/ppermute | solution.py:318
  140.4 13.3 %collective-permute-start.16 = (bf16[2,4,128,128]{3,2,1,0:T(8,128)(2,1)S(1)}, bf16[2,4,128,128]{3,2,1,0:T(8,128)(2,1)S(1)}, u32[]{:S(2)}, u32[]{:S(2)}) collective-permute-start(bf16[2,4,128,128]{3,2,1,0:T(8,128)(2,1)S(1)} %fusion.21), channel_id=1, source_target_pairs={{0,1},{1,0},{2,3},{3,2},{4,5},{5,4},{6,7},{7,6},{8,9},{9,8},{10,11... | collective-permute-start | bytes 786440 | tf_op jit(solution)/shard_map/ppermute | solution.py:323
  157.8 9.4 %collective-permute-start.17 = (bf16[2,4,128,128]{3,2,1,0:T(8,128)(2,1)S(1)}, bf16[2,4,128,128]{3,2,1,0:T(8,128)(2,1)S(1)}, u32[]{:S(2)}, u32[]{:S(2)}) collective-permute-start(bf16[2,4,128,128]{3,2,1,0:T(8,128)(2,1)S(1)} %get-tuple-element.148), channel_id=1, source_target_pairs={{0,2},{1,3},{2,4},{3,5},{4,6},{5,7},{6,0},{7,1},{8,10},{9,11},{10,... | collective-permute-start | bytes 786440 | tf_op jit(solution)/shard_map/ppermute | solution.py:318
  157.9 9.5 %collective-permute-start.19 = (bf16[2,4,128,128]{3,2,1,0:T(8,128)(2,1)S(1)}, bf16[2,4,128,128]{3,2,1,0:T(8,128)(2,1)S(1)}, u32[]{:S(2)}, u32[]{:S(2)}) collective-permute-start(bf16[2,4,128,128]{3,2,1,0:T(8,128)(2,1)S(1)} %get-tuple-element.150), channel_id=1, source_target_pairs={{0,6},{1,7},{2,0},{3,1},{4,2},{5,3},{6,4},{7,5},{8,14},{9,15},{10,... | collective-permute-start | bytes 786440 | tf_op jit(solution)/shard_map/ppermute | solution.py:318
  167.3 14.2 %collective-permute-start.18 = (bf16[2,2,4,128,128]{4,3,2,0,1:T(8,128)(2,1)S(1)}, bf16[2,2,4,128,128]{4,3,2,0,1:T(8,128)(2,1)S(1)}, u32[]{:S(2)}, u32[]{:S(2)}) collective-permute-start(bf16[2,2,4,128,128]{4,3,2,0,1:T(8,128)(2,1)S(1)} %fusion.13), channel_id=1, source_target_pairs={{0,2},{1,3},{2,4},{3,5},{4,6},{5,7},{6,0},{7,1},{8,10},{9,11},{10,... | collective-permute-start | bytes 1572872 | tf_op jit(solution)/shard_map/ppermute | solution.py:318
  167.5 14.0 %collective-permute-start.20 = (bf16[2,2,4,128,128]{4,3,2,0,1:T(8,128)(2,1)S(1)}, bf16[2,2,4,128,128]{4,3,2,0,1:T(8,128)(2,1)S(1)}, u32[]{:S(2)}, u32[]{:S(2)}) collective-permute-start(bf16[2,2,4,128,128]{4,3,2,0,1:T(8,128)(2,1)S(1)} %fusion.15), channel_id=1, source_target_pairs={{0,6},{1,7},{2,0},{3,1},{4,2},{5,3},{6,4},{7,5},{8,14},{9,15},{10,... | collective-permute-start | bytes 1572872 | tf_op jit(solution)/shard_map/ppermute | solution.py:318
  181.8 13.1 %collective-permute-start.21 = (bf16[2,4,128,128]{3,2,1,0:T(8,128)(2,1)S(1)}, bf16[2,4,128,128]{3,2,1,0:T(8,128)(2,1)S(1)}, u32[]{:S(2)}, u32[]{:S(2)}) collective-permute-start(bf16[2,4,128,128]{3,2,1,0:T(8,128)(2,1)S(1)} %fusion.22), channel_id=1, source_target_pairs={{0,1},{1,0},{2,3},{3,2},{4,5},{5,4},{6,7},{7,6},{8,9},{9,8},{10,11... | collective-permute-start | bytes 786440 | tf_op jit(solution)/shard_map/ppermute | solution.py:323
  199.1 9.4 %collective-permute-start.22 = (bf16[2,4,128,128]{3,2,1,0:T(8,128)(2,1)S(1)}, bf16[2,4,128,128]{3,2,1,0:T(8,128)(2,1)S(1)}, u32[]{:S(2)}, u32[]{:S(2)}) collective-permute-start(bf16[2,4,128,128]{3,2,1,0:T(8,128)(2,1)S(1)} %get-tuple-element.155), channel_id=1, source_target_pairs={{0,2},{1,3},{2,4},{3,5},{4,6},{5,7},{6,0},{7,1},{8,10},{9,11},{10,... | collective-permute-start | bytes 786440 | tf_op jit(solution)/shard_map/ppermute | solution.py:318
  199.2 9.5 %collective-permute-start.24 = (bf16[2,4,128,128]{3,2,1,0:T(8,128)(2,1)S(1)}, bf16[2,4,128,128]{3,2,1,0:T(8,128)(2,1)S(1)}, u32[]{:S(2)}, u32[]{:S(2)}) collective-permute-start(bf16[2,4,128,128]{3,2,1,0:T(8,128)(2,1)S(1)} %get-tuple-element.157), channel_id=1, source_target_pairs={{0,6},{1,7},{2,0},{3,1},{4,2},{5,3},{6,4},{7,5},{8,14},{9,15},{10,... | collective-permute-start | bytes 786440 | tf_op jit(solution)/shard_map/ppermute | solution.py:318
  208.6 14.1 %collective-permute-start.23 = (bf16[2,2,4,128,128]{4,3,2,0,1:T(8,128)(2,1)S(1)}, bf16[2,2,4,128,128]{4,3,2,0,1:T(8,128)(2,1)S(1)}, u32[]{:S(2)}, u32[]{:S(2)}) collective-permute-start(bf16[2,2,4,128,128]{4,3,2,0,1:T(8,128)(2,1)S(1)} %fusion.17), channel_id=1, source_target_pairs={{0,2},{1,3},{2,4},{3,5},{4,6},{5,7},{6,0},{7,1},{8,10},{9,11},{10,... | collective-permute-start | bytes 1572872 | tf_op jit(solution)/shard_map/ppermute | solution.py:318
  208.8 13.9 %collective-permute-start.25 = (bf16[2,2,4,128,128]{4,3,2,0,1:T(8,128)(2,1)S(1)}, bf16[2,2,4,128,128]{4,3,2,0,1:T(8,128)(2,1)S(1)}, u32[]{:S(2)}, u32[]{:S(2)}) collective-permute-start(bf16[2,2,4,128,128]{4,3,2,0,1:T(8,128)(2,1)S(1)} %fusion.19), channel_id=1, source_target_pairs={{0,6},{1,7},{2,0},{3,1},{4,2},{5,3},{6,4},{7,5},{8,14},{9,15},{10,... | collective-permute-start | bytes 1572872 | tf_op jit(solution)/shard_map/ppermute | solution.py:318
  223.0 10.9 %collective-permute-start.26 = (bf16[2,4,128,128]{3,2,1,0:T(8,128)(2,1)S(1)}, bf16[2,4,128,128]{3,2,1,0:T(8,128)(2,1)S(1)}, u32[]{:S(2)}, u32[]{:S(2)}) collective-permute-start(bf16[2,4,128,128]{3,2,1,0:T(8,128)(2,1)S(1)} %fusion.23), channel_id=1, source_target_pairs={{0,1},{1,0},{2,3},{3,2},{4,5},{5,4},{6,7},{7,6},{8,9},{9,8},{10,11... | collective-permute-start | bytes 786440 | tf_op jit(solution)/shard_map/ppermute | solution.py:323
  (17 other events, 330.7 us)

commit v4 on v3

--- a/solution.py
+++ b/solution.py
@@ -11,7 +11,7 @@
 STEP = 0.15
 SCALE = 2.0**-8
 GROUP = 16
-STRAIGHT = (2, 10, 8)
+STRAIGHT = (3, 10, 7)
 ALONG_X = 4
 ALONG_Y = 4
 ALONG_Z = 2

time: 256 us -> 260 us (1.016)
  the two profiles are of different devices: /device:TPU:40 before, /device:TPU:8 now
where the time goes in v4:
time: 260 us
  waiting for transfers between devices  106 us (41%)
  starting transfers between devices  92.4 us (36%)
  Pallas kernels  41.7 us (16%)
  local copies, waits for them, and re-layouts  13.1 us (5%)
  other arithmetic  3.67 us (1%)
    ppermute x8, starting transfers between devices, across(): return lax.ppermute(value, 'sym', [(i, i ^ bits) for i in range(count)])  42.3 us
    ppermute x16, waiting for transfers between devices, around_x(): lax.ppermute(value, 'sym', [(i, (i + steps * ALONG_Z) % count) for i in r...  41.9 us
    ppermute x8, waiting for transfers between devices, across(): return lax.ppermute(value, 'sym', [(i, i ^ bits) for i in range(count)])  37.8 us
    ppermute x16, starting transfers between devices, around_x(): lax.ppermute(value, 'sym', [(i, (i + steps * ALONG_Z) % count) for i in r...  33.3 us
    pallas_call x8, Pallas kernels, sum_targets(): pl.pallas_call(target_kernel, in_specs=[pl.BlockSpec(memory_space=pltpu.S...  24.2 us
    ppermute x2, waiting for transfers between devices, next_section(): lax.ppermute(around, 'sec', [(after(s, steps), after(s, steps + 1)) for s...  17.9 us
    pallas_call x4, Pallas kernels, apply_left(): pl.pallas_call(functools.partial(middle_kernel, first), in_specs=[pl.Bloc...  9.52 us
    ppermute x3, starting transfers between devices, next_section(): parts.append(lax.ppermute(value[low:low + length], 'sec', pairs))  8.41 us
  transfers between devices with their start and end apart: 31, of which 20 were waited for; matrix products, arithmetic and copies ran while one was open for 4% of the time, Pallas kernels for 9%

profile of v4, /device:TPU:8, one launch (start us, length us, event | category | flops | bytes accessed | tf_op | source)
XLA Modules:
  0.0 259.7 jit_solution(13613136207596719884)
XLA Ops:
  7.4 4.3 %collective-permute-start.1 = (bf16[10,8,128,128]{3,2,1,0:T(8,128)(2,1)}, bf16[10,8,128,128]{3,2,1,0:T(8,128)(2,1)}, u32[]{:S(2)}, u32[]{:S(2)}) collective-permute-start(bf16[10,8,128,128]{3,2,1,0:T(8,128)(2,1)} %slice_bitcast_fusion), channel_id=1, source_target_pairs={{8,0},{16,8},{24,16},{32,24},{40,32},{48,40},{56,48},{64,56},{72,6... | collective-permute-start | bytes 7864328 | tf_op jit(solution)/shard_map/ppermute | solution.py:102
  16.4 4.5 %collective-permute-start.4 = (bf16[4,8,128,128]{3,2,1,0:T(8,128)(2,1)}, bf16[4,8,128,128]{3,2,1,0:T(8,128)(2,1)}, u32[]{:S(2)}, u32[]{:S(2)}) collective-permute-start(bf16[4,8,128,128]{3,2,1,0:T(8,128)(2,1)} %shard_map.70), channel_id=1, source_target_pairs={{16,32},{32,48},{48,0},{64,80},{80,96},{96,112},{112,64},{128,144}... | collective-permute-start | bytes 3145736 | tf_op jit(solution)/shard_map/ppermute | solution.py:113
  26.6 5.9 %collective-permute-done.4 = bf16[4,8,128,128]{3,2,1,0:T(8,128)(2,1)} collective-permute-done((bf16[4,8,128,128]{3,2,1,0:T(8,128)(2,1)}, bf16[4,8,128,128]{3,2,1,0:T(8,128)(2,1)}, u32[]{:S(2)}, u32[]{:S(2)}) %collective-permute-start.4) | collective-permute-done | bytes 1048608 | tf_op jit(solution)/shard_map/ppermute | solution.py:113
  38.0 12.0 %collective-permute-done.5 = bf16[4,8,128,128]{3,2,1,0:T(8,128)(2,1)} collective-permute-done((bf16[4,8,128,128]{3,2,1,0:T(8,128)(2,1)}, bf16[4,8,128,128]{3,2,1,0:T(8,128)(2,1)}, u32[]{:S(2)}, u32[]{:S(2)}) %collective-permute-start.5) | collective-permute-done | bytes 1048608 | tf_op jit(solution)/shard_map/ppermute | solution.py:113
  56.8 4.3 %collective-permute-done.2.refs_2_ = bf16[7,8,128,128]{3,2,1,0:T(8,128)(2,1)} collective-permute-done((bf16[7,8,128,128]{3,2,1,0:T(8,128)(2,1)}, bf16[7,8,128,128]{3,2,1,0:T(8,128)(2,1)}, u32[]{:S(2)}, u32[]{:S(2)}) %collective-permute-start.2) | collective-permute-done | bytes 1835040 | tf_op jit(solution)/shard_map/ppermute | solution.py:102
  71.9 4.2 %shard_map.72 = (bf16[4,4,128,128]{3,2,1,0:T(8,128)(2,1)S(1)}, bf16[4,4,128,128]{3,2,1,0:T(8,128)(2,1)S(1)}, bf16[4,4,128,128]{3,2,1,0:T(8,128)(2,1)S(1)}) custom-call(s32[4,144]{1,0:T(4,128)S(1)} %add_add_fusion.1.pairs_ref, bf16[193,128,128]{2,1,0:T(8,128)(2,1)S(1)} %get-tuple-element.131.middle_ref, bf16[24,8,128,128]{3,2,1,0:T(8,128)(2,1)S(1)} %shard_map.71.right_ref), custom_call_target="tpu_custom_call" | custom-call | flops 4831838208 | bytes 1048576 | tf_op jit(solution)/shard_map/pallas_call | solution.py:188
  80.3 10.8 %collective-permute-done.8 = bf16[2,2,4,128,128]{4,3,2,0,1:T(8,128)(2,1)S(1)} collective-permute-done((bf16[2,2,4,128,128]{4,3,2,0,1:T(8,128)(2,1)S(1)}, bf16[2,2,4,128,128]{4,3,2,0,1:T(8,128)(2,1)S(1)}, u32[]{:S(2)}, u32[]{:S(2)}) %collective-permute-start.8) | collective-permute-done | bytes 524320 | tf_op jit(solution)/shard_map/ppermute | solution.py:318
  93.0 5.9 %collective-permute-start.11 = (bf16[2,4,128,128]{3,2,1,0:T(8,128)(2,1)S(1)}, bf16[2,4,128,128]{3,2,1,0:T(8,128)(2,1)S(1)}, u32[]{:S(2)}, u32[]{:S(2)}) collective-permute-start(bf16[2,4,128,128]{3,2,1,0:T(8,128)(2,1)S(1)} %fusion.20), channel_id=1, source_target_pairs={{0,1},{1,0},{2,3},{3,2},{4,5},{5,4},{6,7},{7,6},{8,9},{9,8},{10,11... | collective-permute-start | bytes 786440 | tf_op jit(solution)/shard_map/ppermute | solution.py:323
  99.0 6.8 %collective-permute-done.11.refs_1_ = bf16[2,4,128,128]{3,2,1,0:T(8,128)(2,1)S(1)} collective-permute-done((bf16[2,4,128,128]{3,2,1,0:T(8,128)(2,1)S(1)}, bf16[2,4,128,128]{3,2,1,0:T(8,128)(2,1)S(1)}, u32[]{:S(2)}, u32[]{:S(2)}) %collective-permute-start.11) | collective-permute-done | bytes 262176 | tf_op jit(solution)/shard_map/ppermute | solution.py:323
  111.5 7.7 %collective-permute-start.14 = (bf16[2,4,128,128]{3,2,1,0:T(8,128)(2,1)S(1)}, bf16[2,4,128,128]{3,2,1,0:T(8,128)(2,1)S(1)}, u32[]{:S(2)}, u32[]{:S(2)}) collective-permute-start(bf16[2,4,128,128]{3,2,1,0:T(8,128)(2,1)S(1)} %get-tuple-element.143), channel_id=1, source_target_pairs={{0,6},{1,7},{2,0},{3,1},{4,2},{5,3},{6,4},{7,5},{8,14},{9,15},{10,... | collective-permute-start | bytes 786440 | tf_op jit(solution)/shard_map/ppermute | solution.py:318
  119.2 4.2 %shard_map.76 = (bf16[4,4,128,128]{3,2,1,0:T(8,128)(2,1)S(1)}, bf16[4,4,128,128]{3,2,1,0:T(8,128)(2,1)S(1)}, bf16[4,4,128,128]{3,2,1,0:T(8,128)(2,1)S(1)}) custom-call(s32[4,144]{1,0:T(4,128)S(1)} %add_add_fusion.1.pairs_ref, bf16[193,128,128]{2,1,0:T(8,128)(2,1)S(1)} %get-tuple-element.138.middle_ref, bf16[24,8,128,128]{3,2,1,0:T(8,128)(2,1)S(1)} %shard_map.71.right_ref), custom_call_target="tpu_custom_call" | custom-call | flops 4831838208 | bytes 1048576 | tf_op jit(solution)/shard_map/pallas_call | solution.py:188
  129.6 11.4 %collective-permute-done.13 = bf16[2,2,4,128,128]{4,3,2,0,1:T(8,128)(2,1)S(1)} collective-permute-done((bf16[2,2,4,128,128]{4,3,2,0,1:T(8,128)(2,1)S(1)}, bf16[2,2,4,128,128]{4,3,2,0,1:T(8,128)(2,1)S(1)}, u32[]{:S(2)}, u32[]{:S(2)}) %collective-permute-start.13) | collective-permute-done | bytes 524320 | tf_op jit(solution)/shard_map/ppermute | solution.py:318
  141.3 6.1 %collective-permute-start.16 = (bf16[2,4,128,128]{3,2,1,0:T(8,128)(2,1)S(1)}, bf16[2,4,128,128]{3,2,1,0:T(8,128)(2,1)S(1)}, u32[]{:S(2)}, u32[]{:S(2)}) collective-permute-start(bf16[2,4,128,128]{3,2,1,0:T(8,128)(2,1)S(1)} %fusion.21), channel_id=1, source_target_pairs={{0,1},{1,0},{2,3},{3,2},{4,5},{5,4},{6,7},{7,6},{8,9},{9,8},{10,11... | collective-permute-start | bytes 786440 | tf_op jit(solution)/shard_map/ppermute | solution.py:323
  147.5 5.2 %collective-permute-done.16.refs_1_ = bf16[2,4,128,128]{3,2,1,0:T(8,128)(2,1)S(1)} collective-permute-done((bf16[2,4,128,128]{3,2,1,0:T(8,128)(2,1)S(1)}, bf16[2,4,128,128]{3,2,1,0:T(8,128)(2,1)S(1)}, u32[]{:S(2)}, u32[]{:S(2)}) %collective-permute-start.16) | collective-permute-done | bytes 262176 | tf_op jit(solution)/shard_map/ppermute | solution.py:323
  160.2 4.3 %shard_map.80 = (bf16[4,4,128,128]{3,2,1,0:T(8,128)(2,1)S(1)}, bf16[4,4,128,128]{3,2,1,0:T(8,128)(2,1)S(1)}, bf16[4,4,128,128]{3,2,1,0:T(8,128)(2,1)S(1)}) custom-call(s32[4,144]{1,0:T(4,128)S(1)} %add_add_fusion.1.pairs_ref, bf16[193,128,128]{2,1,0:T(8,128)(2,1)S(1)} %get-tuple-element.145.middle_ref, bf16[24,8,128,128]{3,2,1,0:T(8,128)(2,1)S(1)} %shard_map.71.right_ref), custom_call_target="tpu_custom_call" | custom-call | flops 4831838208 | bytes 1048576 | tf_op jit(solution)/shard_map/pallas_call | solution.py:188
  168.4 8.8 %collective-permute-done.18 = bf16[2,2,4,128,128]{4,3,2,0,1:T(8,128)(2,1)S(1)} collective-permute-done((bf16[2,2,4,128,128]{4,3,2,0,1:T(8,128)(2,1)S(1)}, bf16[2,2,4,128,128]{4,3,2,0,1:T(8,128)(2,1)S(1)}, u32[]{:S(2)}, u32[]{:S(2)}) %collective-permute-start.18) | collective-permute-done | bytes 524320 | tf_op jit(solution)/shard_map/ppermute | solution.py:318
  177.4 12.1 %collective-permute-start.21 = (bf16[2,4,128,128]{3,2,1,0:T(8,128)(2,1)S(1)}, bf16[2,4,128,128]{3,2,1,0:T(8,128)(2,1)S(1)}, u32[]{:S(2)}, u32[]{:S(2)}) collective-permute-start(bf16[2,4,128,128]{3,2,1,0:T(8,128)(2,1)S(1)} %fusion.22), channel_id=1, source_target_pairs={{0,1},{1,0},{2,3},{3,2},{4,5},{5,4},{6,7},{7,6},{8,9},{9,8},{10,11... | collective-permute-start | bytes 786440 | tf_op jit(solution)/shard_map/ppermute | solution.py:323
  189.6 9.5 %collective-permute-done.21.refs_1_ = bf16[2,4,128,128]{3,2,1,0:T(8,128)(2,1)S(1)} collective-permute-done((bf16[2,4,128,128]{3,2,1,0:T(8,128)(2,1)S(1)}, bf16[2,4,128,128]{3,2,1,0:T(8,128)(2,1)S(1)}, u32[]{:S(2)}, u32[]{:S(2)}) %collective-permute-start.21) | collective-permute-done | bytes 262176 | tf_op jit(solution)/shard_map/ppermute | solution.py:323
  207.1 4.3 %shard_map.84 = (bf16[4,4,128,128]{3,2,1,0:T(8,128)(2,1)S(1)}, bf16[4,4,128,128]{3,2,1,0:T(8,128)(2,1)S(1)}, bf16[4,4,128,128]{3,2,1,0:T(8,128)(2,1)S(1)}) custom-call(s32[4,144]{1,0:T(4,128)S(1)} %add_add_fusion.1.pairs_ref, bf16[193,128,128]{2,1,0:T(8,128)(2,1)S(1)} %get-tuple-element.152.middle_ref, bf16[24,8,128,128]{3,2,1,0:T(8,128)(2,1)S(1)} %shard_map.71.right_ref), custom_call_target="tpu_custom_call" | custom-call | flops 4831838208 | bytes 1048576 | tf_op jit(solution)/shard_map/pallas_call | solution.py:188
  215.7 6.5 %collective-permute-done.23 = bf16[2,2,4,128,128]{4,3,2,0,1:T(8,128)(2,1)S(1)} collective-permute-done((bf16[2,2,4,128,128]{4,3,2,0,1:T(8,128)(2,1)S(1)}, bf16[2,2,4,128,128]{4,3,2,0,1:T(8,128)(2,1)S(1)}, u32[]{:S(2)}, u32[]{:S(2)}) %collective-permute-start.23) | collective-permute-done | bytes 524320 | tf_op jit(solution)/shard_map/ppermute | solution.py:318
  222.5 6.5 %collective-permute-start.26 = (bf16[2,4,128,128]{3,2,1,0:T(8,128)(2,1)S(1)}, bf16[2,4,128,128]{3,2,1,0:T(8,128)(2,1)S(1)}, u32[]{:S(2)}, u32[]{:S(2)}) collective-permute-start(bf16[2,4,128,128]{3,2,1,0:T(8,128)(2,1)S(1)} %fusion.23), channel_id=1, source_target_pairs={{0,1},{1,0},{2,3},{3,2},{4,5},{5,4},{6,7},{7,6},{8,9},{9,8},{10,11... | collective-permute-start | bytes 786440 | tf_op jit(solution)/shard_map/ppermute | solution.py:323
  229.0 9.5 %collective-permute-done.26.refs_1_ = bf16[2,4,128,128]{3,2,1,0:T(8,128)(2,1)S(1)} collective-permute-done((bf16[2,4,128,128]{3,2,1,0:T(8,128)(2,1)S(1)}, bf16[2,4,128,128]{3,2,1,0:T(8,128)(2,1)S(1)}, u32[]{:S(2)}, u32[]{:S(2)}) %collective-permute-start.26) | collective-permute-done | bytes 262176 | tf_op jit(solution)/shard_map/ppermute | solution.py:323
  240.1 4.6 %collective-permute-start.28 = (f32[40,128]{1,0:T(8,128)S(1)}, f32[40,128]{1,0:T(8,128)S(1)}, u32[]{:S(2)}, u32[]{:S(2)}) collective-permute-start(f32[40,128]{1,0:T(8,128)S(1)} %constant_dynamic-update-slice_fusion), channel_id=1, source_target_pairs={{0,4},{1,5},{2,6},{3,7},{4,0},{5,1},{6,2},{7,3},{8,12},{9,13},{10,... | collective-permute-start | bytes 61448 | tf_op jit(solution)/shard_map/ppermute | solution.py:323
  249.7 6.5 %collective-permute-start.30 = (f32[40,128]{1,0:T(8,128)S(1)}, f32[40,128]{1,0:T(8,128)S(1)}, u32[]{:S(2)}, u32[]{:S(2)}) collective-permute-start(f32[40,128]{1,0:T(8,128)S(1)} %add_add_fusion), channel_id=1, source_target_pairs={{0,1},{1,0},{2,3},{3,2},{4,5},{5,4},{6,7},{7,6},{8,9},{9,8},{10,11... | collective-permute-start | bytes 61448 | tf_op jit(solution)/shard_map/ppermute | solution.py:323
  (140 shorter events, 91.2 us)
Async XLA Ops:
  1.8 11.4 %collective-permute-start = (bf16[3,8,128,128]{3,2,1,0:T(8,128)(2,1)S(1)}, bf16[3,8,128,128]{3,2,1,0:T(8,128)(2,1)S(1)}, u32[]{:S(2)}, u32[]{:S(2)}) collective-permute-start(bf16[3,8,128,128]{3,2,1,0:T(8,128)(2,1)S(1)} %slice_bitcast_fusion.2), channel_id=1, source_target_pairs={{8,0},{16,8},{24,16},{32,24},{40,32},{48,40},{56,48},{64,56},{72,6... | collective-permute-start | bytes 2359304 | tf_op jit(solution)/shard_map/ppermute | solution.py:102
  7.4 53.7 %collective-permute-start.1 = (bf16[10,8,128,128]{3,2,1,0:T(8,128)(2,1)}, bf16[10,8,128,128]{3,2,1,0:T(8,128)(2,1)}, u32[]{:S(2)}, u32[]{:S(2)}) collective-permute-start(bf16[10,8,128,128]{3,2,1,0:T(8,128)(2,1)} %slice_bitcast_fusion), channel_id=1, source_target_pairs={{8,0},{16,8},{24,16},{32,24},{40,32},{48,40},{56,48},{64,56},{72,6... | collective-permute-start | bytes 7864328 | tf_op jit(solution)/shard_map/ppermute | solution.py:102
  16.4 16.1 %collective-permute-start.4 = (bf16[4,8,128,128]{3,2,1,0:T(8,128)(2,1)}, bf16[4,8,128,128]{3,2,1,0:T(8,128)(2,1)}, u32[]{:S(2)}, u32[]{:S(2)}) collective-permute-start(bf16[4,8,128,128]{3,2,1,0:T(8,128)(2,1)} %shard_map.70), channel_id=1, source_target_pairs={{16,32},{32,48},{48,0},{64,80},{80,96},{96,112},{112,64},{128,144}... | collective-permute-start | bytes 3145736 | tf_op jit(solution)/shard_map/ppermute | solution.py:113
  23.9 37.2 %collective-permute-start.2 = (bf16[7,8,128,128]{3,2,1,0:T(8,128)(2,1)}, bf16[7,8,128,128]{3,2,1,0:T(8,128)(2,1)}, u32[]{:S(2)}, u32[]{:S(2)}) collective-permute-start(bf16[7,8,128,128]{3,2,1,0:T(8,128)(2,1)} %slice_bitcast_fusion.1), channel_id=1, source_target_pairs={{8,0},{16,8},{24,16},{32,24},{40,32},{48,40},{56,48},{64,56},{72,6... | collective-permute-start | bytes 5505032 | tf_op jit(solution)/shard_map/ppermute | solution.py:102
  32.5 17.5 %collective-permute-start.5 = (bf16[4,8,128,128]{3,2,1,0:T(8,128)(2,1)}, bf16[4,8,128,128]{3,2,1,0:T(8,128)(2,1)}, u32[]{:S(2)}, u32[]{:S(2)}) collective-permute-start(bf16[4,8,128,128]{3,2,1,0:T(8,128)(2,1)} %collective-permute-done.4), channel_id=1, source_target_pairs={{32,48},{48,0},{0,16},{80,96},{96,112},{112,64},{64,80},{144,160},... | collective-permute-start | bytes 3145736 | tf_op jit(solution)/shard_map/ppermute | solution.py:113
  36.7 20.0 %collective-permute-start.3 = (bf16[4,8,128,128]{3,2,1,0:T(8,128)(2,1)}, bf16[4,8,128,128]{3,2,1,0:T(8,128)(2,1)S(1)}, u32[]{:S(2)}, u32[]{:S(2)}) collective-permute-start(bf16[4,8,128,128]{3,2,1,0:T(8,128)(2,1)} %shard_map.70), channel_id=1, source_target_pairs={{8,0},{24,16},{40,32},{56,48},{72,64},{88,80},{104,96},{120,112},{... | collective-permute-start | bytes 3145736 | tf_op jit(solution)/shard_map/ppermute | solution.py:105
  50.0 13.9 %collective-permute-start.6 = (bf16[4,8,128,128]{3,2,1,0:T(8,128)(2,1)}, bf16[4,8,128,128]{3,2,1,0:T(8,128)(2,1)S(1)}, u32[]{:S(2)}, u32[]{:S(2)}) collective-permute-start(bf16[4,8,128,128]{3,2,1,0:T(8,128)(2,1)} %collective-permute-done.5), channel_id=1, source_target_pairs={{48,8},{0,24},{16,40},{96,56},{112,72},{64,88},{80,104},{160,120},... | collective-permute-start | bytes 3145736 | tf_op jit(solution)/shard_map/ppermute | solution.py:114
  68.6 8.0 %collective-permute-start.7 = (bf16[2,4,128,128]{3,2,1,0:T(8,128)(2,1)S(1)}, bf16[2,4,128,128]{3,2,1,0:T(8,128)(2,1)S(1)}, u32[]{:S(2)}, u32[]{:S(2)}) collective-permute-start(bf16[2,4,128,128]{3,2,1,0:T(8,128)(2,1)S(1)} %get-tuple-element.134), channel_id=1, source_target_pairs={{0,2},{1,3},{2,4},{3,5},{4,6},{5,7},{6,0},{7,1},{8,10},{9,11},{10,... | collective-permute-start | bytes 786440 | tf_op jit(solution)/shard_map/ppermute | solution.py:318
  76.7 14.4 %collective-permute-start.8 = (bf16[2,2,4,128,128]{4,3,2,0,1:T(8,128)(2,1)S(1)}, bf16[2,2,4,128,128]{4,3,2,0,1:T(8,128)(2,1)S(1)}, u32[]{:S(2)}, u32[]{:S(2)}) collective-permute-start(bf16[2,2,4,128,128]{4,3,2,0,1:T(8,128)(2,1)S(1)} %fusion.5), channel_id=1, source_target_pairs={{0,2},{1,3},{2,4},{3,5},{4,6},{5,7},{6,0},{7,1},{8,10},{9,11},{10,... | collective-permute-start | bytes 1572872 | tf_op jit(solution)/shard_map/ppermute | solution.py:318
  78.3 14.4 %collective-permute-start.10 = (bf16[2,2,4,128,128]{4,3,2,0,1:T(8,128)(2,1)S(1)}, bf16[2,2,4,128,128]{4,3,2,0,1:T(8,128)(2,1)S(1)}, u32[]{:S(2)}, u32[]{:S(2)}) collective-permute-start(bf16[2,2,4,128,128]{4,3,2,0,1:T(8,128)(2,1)S(1)} %fusion.7), channel_id=1, source_target_pairs={{0,6},{1,7},{2,0},{3,1},{4,2},{5,3},{6,4},{7,5},{8,14},{9,15},{10,... | collective-permute-start | bytes 1572872 | tf_op jit(solution)/shard_map/ppermute | solution.py:318
  93.0 12.8 %collective-permute-start.11 = (bf16[2,4,128,128]{3,2,1,0:T(8,128)(2,1)S(1)}, bf16[2,4,128,128]{3,2,1,0:T(8,128)(2,1)S(1)}, u32[]{:S(2)}, u32[]{:S(2)}) collective-permute-start(bf16[2,4,128,128]{3,2,1,0:T(8,128)(2,1)S(1)} %fusion.20), channel_id=1, source_target_pairs={{0,1},{1,0},{2,3},{3,2},{4,5},{5,4},{6,7},{7,6},{8,9},{9,8},{10,11... | collective-permute-start | bytes 786440 | tf_op jit(solution)/shard_map/ppermute | solution.py:323
  110.1 15.9 %collective-permute-start.12 = (bf16[2,4,128,128]{3,2,1,0:T(8,128)(2,1)S(1)}, bf16[2,4,128,128]{3,2,1,0:T(8,128)(2,1)S(1)}, u32[]{:S(2)}, u32[]{:S(2)}) collective-permute-start(bf16[2,4,128,128]{3,2,1,0:T(8,128)(2,1)S(1)} %get-tuple-element.141), channel_id=1, source_target_pairs={{0,2},{1,3},{2,4},{3,5},{4,6},{5,7},{6,0},{7,1},{8,10},{9,11},{10,... | collective-permute-start | bytes 786440 | tf_op jit(solution)/shard_map/ppermute | solution.py:318
  111.5 14.7 %collective-permute-start.14 = (bf16[2,4,128,128]{3,2,1,0:T(8,128)(2,1)S(1)}, bf16[2,4,128,128]{3,2,1,0:T(8,128)(2,1)S(1)}, u32[]{:S(2)}, u32[]{:S(2)}) collective-permute-start(bf16[2,4,128,128]{3,2,1,0:T(8,128)(2,1)S(1)} %get-tuple-element.143), channel_id=1, source_target_pairs={{0,6},{1,7},{2,0},{3,1},{4,2},{5,3},{6,4},{7,5},{8,14},{9,15},{10,... | collective-permute-start | bytes 786440 | tf_op jit(solution)/shard_map/ppermute | solution.py:318
  126.1 14.9 %collective-permute-start.13 = (bf16[2,2,4,128,128]{4,3,2,0,1:T(8,128)(2,1)S(1)}, bf16[2,2,4,128,128]{4,3,2,0,1:T(8,128)(2,1)S(1)}, u32[]{:S(2)}, u32[]{:S(2)}) collective-permute-start(bf16[2,2,4,128,128]{4,3,2,0,1:T(8,128)(2,1)S(1)} %fusion.9), channel_id=1, source_target_pairs={{0,2},{1,3},{2,4},{3,5},{4,6},{5,7},{6,0},{7,1},{8,10},{9,11},{10,... | collective-permute-start | bytes 1572872 | tf_op jit(solution)/shard_map/ppermute | solution.py:318
  126.3 14.7 %collective-permute-start.15 = (bf16[2,2,4,128,128]{4,3,2,0,1:T(8,128)(2,1)S(1)}, bf16[2,2,4,128,128]{4,3,2,0,1:T(8,128)(2,1)S(1)}, u32[]{:S(2)}, u32[]{:S(2)}) collective-permute-start(bf16[2,2,4,128,128]{4,3,2,0,1:T(8,128)(2,1)S(1)} %fusion.11), channel_id=1, source_target_pairs={{0,6},{1,7},{2,0},{3,1},{4,2},{5,3},{6,4},{7,5},{8,14},{9,15},{10,... | collective-permute-start | bytes 1572872 | tf_op jit(solution)/shard_map/ppermute | solution.py:318
  141.3 11.4 %collective-permute-start.16 = (bf16[2,4,128,128]{3,2,1,0:T(8,128)(2,1)S(1)}, bf16[2,4,128,128]{3,2,1,0:T(8,128)(2,1)S(1)}, u32[]{:S(2)}, u32[]{:S(2)}) collective-permute-start(bf16[2,4,128,128]{3,2,1,0:T(8,128)(2,1)S(1)} %fusion.21), channel_id=1, source_target_pairs={{0,1},{1,0},{2,3},{3,2},{4,5},{5,4},{6,7},{7,6},{8,9},{9,8},{10,11... | collective-permute-start | bytes 786440 | tf_op jit(solution)/shard_map/ppermute | solution.py:323
  164.7 12.5 %collective-permute-start.18 = (bf16[2,2,4,128,128]{4,3,2,0,1:T(8,128)(2,1)S(1)}, bf16[2,2,4,128,128]{4,3,2,0,1:T(8,128)(2,1)S(1)}, u32[]{:S(2)}, u32[]{:S(2)}) collective-permute-start(bf16[2,2,4,128,128]{4,3,2,0,1:T(8,128)(2,1)S(1)} %fusion.13), channel_id=1, source_target_pairs={{0,2},{1,3},{2,4},{3,5},{4,6},{5,7},{6,0},{7,1},{8,10},{9,11},{10,... | collective-permute-start | bytes 1572872 | tf_op jit(solution)/shard_map/ppermute | solution.py:318
  164.9 12.3 %collective-permute-start.20 = (bf16[2,2,4,128,128]{4,3,2,0,1:T(8,128)(2,1)S(1)}, bf16[2,2,4,128,128]{4,3,2,0,1:T(8,128)(2,1)S(1)}, u32[]{:S(2)}, u32[]{:S(2)}) collective-permute-start(bf16[2,2,4,128,128]{4,3,2,0,1:T(8,128)(2,1)S(1)} %fusion.15), channel_id=1, source_target_pairs={{0,6},{1,7},{2,0},{3,1},{4,2},{5,3},{6,4},{7,5},{8,14},{9,15},{10,... | collective-permute-start | bytes 1572872 | tf_op jit(solution)/shard_map/ppermute | solution.py:318
  177.4 21.6 %collective-permute-start.21 = (bf16[2,4,128,128]{3,2,1,0:T(8,128)(2,1)S(1)}, bf16[2,4,128,128]{3,2,1,0:T(8,128)(2,1)S(1)}, u32[]{:S(2)}, u32[]{:S(2)}) collective-permute-start(bf16[2,4,128,128]{3,2,1,0:T(8,128)(2,1)S(1)} %fusion.22), channel_id=1, source_target_pairs={{0,1},{1,0},{2,3},{3,2},{4,5},{5,4},{6,7},{7,6},{8,9},{9,8},{10,11... | collective-permute-start | bytes 786440 | tf_op jit(solution)/shard_map/ppermute | solution.py:323
  203.2 8.2 %collective-permute-start.22 = (bf16[2,4,128,128]{3,2,1,0:T(8,128)(2,1)S(1)}, bf16[2,4,128,128]{3,2,1,0:T(8,128)(2,1)S(1)}, u32[]{:S(2)}, u32[]{:S(2)}) collective-permute-start(bf16[2,4,128,128]{3,2,1,0:T(8,128)(2,1)S(1)} %get-tuple-element.155), channel_id=1, source_target_pairs={{0,2},{1,3},{2,4},{3,5},{4,6},{5,7},{6,0},{7,1},{8,10},{9,11},{10,... | collective-permute-start | bytes 786440 | tf_op jit(solution)/shard_map/ppermute | solution.py:318
  211.5 10.7 %collective-permute-start.23 = (bf16[2,2,4,128,128]{4,3,2,0,1:T(8,128)(2,1)S(1)}, bf16[2,2,4,128,128]{4,3,2,0,1:T(8,128)(2,1)S(1)}, u32[]{:S(2)}, u32[]{:S(2)}) collective-permute-start(bf16[2,2,4,128,128]{4,3,2,0,1:T(8,128)(2,1)S(1)} %fusion.17), channel_id=1, source_target_pairs={{0,2},{1,3},{2,4},{3,5},{4,6},{5,7},{6,0},{7,1},{8,10},{9,11},{10,... | collective-permute-start | bytes 1572872 | tf_op jit(solution)/shard_map/ppermute | solution.py:318
  211.8 10.5 %collective-permute-start.25 = (bf16[2,2,4,128,128]{4,3,2,0,1:T(8,128)(2,1)S(1)}, bf16[2,2,4,128,128]{4,3,2,0,1:T(8,128)(2,1)S(1)}, u32[]{:S(2)}, u32[]{:S(2)}) collective-permute-start(bf16[2,2,4,128,128]{4,3,2,0,1:T(8,128)(2,1)S(1)} %fusion.19), channel_id=1, source_target_pairs={{0,6},{1,7},{2,0},{3,1},{4,2},{5,3},{6,4},{7,5},{8,14},{9,15},{10,... | collective-permute-start | bytes 1572872 | tf_op jit(solution)/shard_map/ppermute | solution.py:318
  222.5 16.0 %collective-permute-start.26 = (bf16[2,4,128,128]{3,2,1,0:T(8,128)(2,1)S(1)}, bf16[2,4,128,128]{3,2,1,0:T(8,128)(2,1)S(1)}, u32[]{:S(2)}, u32[]{:S(2)}) collective-permute-start(bf16[2,4,128,128]{3,2,1,0:T(8,128)(2,1)S(1)} %fusion.23), channel_id=1, source_target_pairs={{0,1},{1,0},{2,3},{3,2},{4,5},{5,4},{6,7},{7,6},{8,9},{9,8},{10,11... | collective-permute-start | bytes 786440 | tf_op jit(solution)/shard_map/ppermute | solution.py:323
  249.7 8.2 %collective-permute-start.30 = (f32[40,128]{1,0:T(8,128)S(1)}, f32[40,128]{1,0:T(8,128)S(1)}, u32[]{:S(2)}, u32[]{:S(2)}) collective-permute-start(f32[40,128]{1,0:T(8,128)S(1)} %add_add_fusion), channel_id=1, source_target_pairs={{0,1},{1,0},{2,3},{3,2},{4,5},{5,4},{6,7},{7,6},{8,9},{9,8},{10,11... | collective-permute-start | bytes 61448 | tf_op jit(solution)/shard_map/ppermute | solution.py:323
  (17 other events, 318.0 us)

commit v5 on v3

--- a/solution.py
+++ b/solution.py
@@ -31,12 +31,12 @@
     return ((rows < limit) & (cols < limit)).astype(F32)
 
 
-def gather_kernel(where_ref, here_ref, *refs):
-    parts, (right_ref, arrived) = refs[:-2], refs[-2:]
+def gather_kernel(low, last, where_ref, here_ref, *refs):
+    parts, (right_ref, arrived) = refs[: -3 if last else -2], refs[-2:]
     at_end, is_odd = where_ref[0] == 1, where_ref[1] == 1
-    straight, (beside, around) = parts[:-2], parts[-2:]
-    low = 0
-    for part in straight + (beside,):
+    straight, (beside, around) = (parts[:-2], parts[-2:]) if last else (parts, (None, None))
+    begin = low
+    for part in straight + ((beside,) if last else ()):
         rows = pl.ds(low, part.shape[0])
         low += part.shape[0]
 
@@ -60,20 +60,29 @@
             def _(rows=rows):
                 pltpu.make_async_copy(beside, right_ref.at[rows], arrived).start()
 
-    pltpu.make_async_copy(here_ref, right_ref, arrived).wait()
+    rows = pl.ds(begin, low - begin)
+    pltpu.make_async_copy(here_ref.at[rows], right_ref.at[rows], arrived).wait()
 
 
 def gather_right(where, here, parts):
     anywhere = pl.BlockSpec(memory_space=pl.ANY)
-    return pl.pallas_call(
-        gather_kernel,
-        in_specs=[pl.BlockSpec(memory_space=pltpu.SMEM), pl.BlockSpec(memory_space=pltpu.HBM)]
-        + [anywhere] * len(parts),
-        out_specs=pl.BlockSpec(memory_space=pltpu.VMEM),
-        out_shape=jax.ShapeDtypeStruct(here.shape, here.dtype),
-        scratch_shapes=[pltpu.SemaphoreType.DMA],
-        compiler_params=params(),
-    )(where, here, *parts)
+    in_vmem = pl.BlockSpec(memory_space=pltpu.VMEM)
+
+    def call(low, some, held):
+        return pl.pallas_call(
+            functools.partial(gather_kernel, low, bool(held)),
+            in_specs=[pl.BlockSpec(memory_space=pltpu.SMEM), pl.BlockSpec(memory_space=pltpu.HBM)]
+            + [anywhere] * len(some)
+            + [in_vmem] * len(held),
+            out_specs=in_vmem,
+            out_shape=jax.ShapeDtypeStruct(here.shape, here.dtype),
+            scratch_shapes=[pltpu.SemaphoreType.DMA],
+            input_output_aliases={2 + len(some): 0} if held else {},
+            compiler_params=params(),
+        )(where, here, *some, *held)
+
+    early = len(STRAIGHT) - 1
+    return call(sum(STRAIGHT[:early]), parts[early:], [call(0, parts[:early], [])])
 
 
 def cut_kernel(low, value_ref, after_ref, part_ref, arrived):

time: 256 us -> 253 us (0.988)
  the two profiles are of different devices: /device:TPU:40 before, /device:TPU:8 now
where the time goes in v5:
time: 253 us; the launch traced here: 250 us
  waiting for transfers between devices  107 us (42%)
  starting transfers between devices  82.3 us (33%)
  Pallas kernels  40.9 us (16%)
  local copies, waits for them, and re-layouts  12.9 us (5%)
  other arithmetic  3.74 us (1%)
  between operations  2.64 us (1%)
    ppermute x8, waiting for transfers between devices, across(): return lax.ppermute(value, 'sym', [(i, i ^ bits) for i in range(count)])  41.9 us
    ppermute x16, waiting for transfers between devices, around_x(): lax.ppermute(value, 'sym', [(i, (i + steps * ALONG_Z) % count) for i in r...  40.3 us
    ppermute x8, starting transfers between devices, across(): return lax.ppermute(value, 'sym', [(i, i ^ bits) for i in range(count)])  38.9 us
    ppermute x16, starting transfers between devices, around_x(): lax.ppermute(value, 'sym', [(i, (i + steps * ALONG_Z) % count) for i in r...  27.8 us
    pallas_call x8, Pallas kernels, sum_targets(): pl.pallas_call(target_kernel, in_specs=[pl.BlockSpec(memory_space=pltpu.S...  21.7 us
    ppermute x2, waiting for transfers between devices, next_section(): lax.ppermute(around, 'sec', [(after(s, steps), after(s, steps + 1)) for s...  17.6 us
    pallas_call x4, Pallas kernels, apply_left(): pl.pallas_call(functools.partial(middle_kernel, first), in_specs=[pl.Bloc...  9.52 us
    ppermute x3, starting transfers between devices, next_section(): parts.append(lax.ppermute(value[low:low + length], 'sec', pairs))  8.41 us
  transfers between devices with their start and end apart: 31, of which 18 were waited for; matrix products, arithmetic and copies ran while one was open for 4% of the time, Pallas kernels for 9%

profile of v5, /device:TPU:8, one launch (start us, length us, event | category | flops | bytes accessed | tf_op | source)
XLA Modules:
  0.0 249.6 jit_solution(9492240153990744384)
XLA Ops:
  3.6 3.6 %slice_bitcast_fusion = bf16[10,8,128,128]{3,2,1,0:T(8,128)(2,1)} fusion(bf16[1,24,8,128,128]{4,3,2,1,0:T(8,128)(2,1)} %param.23), kind=kLoop, calls=%fused_computation | loop fusion | bytes 5242880 | tf_op jit(solution)/shard_map/slice | solution.py:111
  7.2 4.3 %collective-permute-start.6 = (bf16[10,8,128,128]{3,2,1,0:T(8,128)(2,1)}, bf16[10,8,128,128]{3,2,1,0:T(8,128)(2,1)}, u32[]{:S(2)}, u32[]{:S(2)}) collective-permute-start(bf16[10,8,128,128]{3,2,1,0:T(8,128)(2,1)} %slice_bitcast_fusion), channel_id=1, source_target_pairs={{8,0},{16,8},{24,16},{32,24},{40,32},{48,40},{56,48},{64,56},{72,6... | collective-permute-start | bytes 7864328 | tf_op jit(solution)/shard_map/ppermute | solution.py:111
  24.6 4.9 %collective-permute-done.3 = bf16[4,8,128,128]{3,2,1,0:T(8,128)(2,1)} collective-permute-done((bf16[4,8,128,128]{3,2,1,0:T(8,128)(2,1)}, bf16[4,8,128,128]{3,2,1,0:T(8,128)(2,1)}, u32[]{:S(2)}, u32[]{:S(2)}) %collective-permute-start.3) | collective-permute-done | bytes 1048608 | tf_op jit(solution)/shard_map/ppermute | solution.py:122
  34.3 12.7 %collective-permute-done.4 = bf16[4,8,128,128]{3,2,1,0:T(8,128)(2,1)} collective-permute-done((bf16[4,8,128,128]{3,2,1,0:T(8,128)(2,1)}, bf16[4,8,128,128]{3,2,1,0:T(8,128)(2,1)}, u32[]{:S(2)}, u32[]{:S(2)}) %collective-permute-start.4) | collective-permute-done | bytes 1048608 | tf_op jit(solution)/shard_map/ppermute | solution.py:122
  56.1 7.4 %collective-permute-done.refs_0_ = bf16[8,8,128,128]{3,2,1,0:T(8,128)(2,1)} collective-permute-done((bf16[8,8,128,128]{3,2,1,0:T(8,128)(2,1)}, bf16[8,8,128,128]{3,2,1,0:T(8,128)(2,1)}, u32[]{:S(2)}, u32[]{:S(2)}) %collective-permute-start) | collective-permute-done | bytes 2097184 | tf_op jit(solution)/shard_map/ppermute | solution.py:111
  70.7 3.6 %shard_map.73 = (bf16[4,4,128,128]{3,2,1,0:T(8,128)(2,1)S(1)}, bf16[4,4,128,128]{3,2,1,0:T(8,128)(2,1)S(1)}, bf16[4,4,128,128]{3,2,1,0:T(8,128)(2,1)S(1)}) custom-call(s32[4,144]{1,0:T(4,128)S(1)} %add_add_fusion.1.pairs_ref, bf16[193,128,128]{2,1,0:T(8,128)(2,1)S(1)} %get-tuple-element.131.middle_ref, bf16[24,8,128,128]{3,2,1,0:T(8,128)(2,1)S(1)} %shard_map.72.right_ref), custom_call_target="tpu_custom_call" | custom-call | flops 4831838208 | bytes 1048576 | tf_op jit(solution)/shard_map/pallas_call | solution.py:197
  81.3 11.5 %collective-permute-done.8 = bf16[2,2,4,128,128]{4,3,2,0,1:T(8,128)(2,1)S(1)} collective-permute-done((bf16[2,2,4,128,128]{4,3,2,0,1:T(8,128)(2,1)S(1)}, bf16[2,2,4,128,128]{4,3,2,0,1:T(8,128)(2,1)S(1)}, u32[]{:S(2)}, u32[]{:S(2)}) %collective-permute-start.8) | collective-permute-done | bytes 524320 | tf_op jit(solution)/shard_map/ppermute | solution.py:327
  93.1 4.9 %collective-permute-start.11 = (bf16[2,4,128,128]{3,2,1,0:T(8,128)(2,1)S(1)}, bf16[2,4,128,128]{3,2,1,0:T(8,128)(2,1)S(1)}, u32[]{:S(2)}, u32[]{:S(2)}) collective-permute-start(bf16[2,4,128,128]{3,2,1,0:T(8,128)(2,1)S(1)} %fusion.20), channel_id=1, source_target_pairs={{0,1},{1,0},{2,3},{3,2},{4,5},{5,4},{6,7},{7,6},{8,9},{9,8},{10,11... | collective-permute-start | bytes 786440 | tf_op jit(solution)/shard_map/ppermute | solution.py:332
  98.0 7.0 %collective-permute-done.11.refs_1_ = bf16[2,4,128,128]{3,2,1,0:T(8,128)(2,1)S(1)} collective-permute-done((bf16[2,4,128,128]{3,2,1,0:T(8,128)(2,1)S(1)}, bf16[2,4,128,128]{3,2,1,0:T(8,128)(2,1)S(1)}, u32[]{:S(2)}, u32[]{:S(2)}) %collective-permute-start.11) | collective-permute-done | bytes 262176 | tf_op jit(solution)/shard_map/ppermute | solution.py:332
  112.9 3.6 %shard_map.77 = (bf16[4,4,128,128]{3,2,1,0:T(8,128)(2,1)S(1)}, bf16[4,4,128,128]{3,2,1,0:T(8,128)(2,1)S(1)}, bf16[4,4,128,128]{3,2,1,0:T(8,128)(2,1)S(1)}) custom-call(s32[4,144]{1,0:T(4,128)S(1)} %add_add_fusion.1.pairs_ref, bf16[193,128,128]{2,1,0:T(8,128)(2,1)S(1)} %get-tuple-element.138.middle_ref, bf16[24,8,128,128]{3,2,1,0:T(8,128)(2,1)S(1)} %shard_map.72.right_ref), custom_call_target="tpu_custom_call" | custom-call | flops 4831838208 | bytes 1048576 | tf_op jit(solution)/shard_map/pallas_call | solution.py:197
  121.7 9.8 %collective-permute-done.13 = bf16[2,2,4,128,128]{4,3,2,0,1:T(8,128)(2,1)S(1)} collective-permute-done((bf16[2,2,4,128,128]{4,3,2,0,1:T(8,128)(2,1)S(1)}, bf16[2,2,4,128,128]{4,3,2,0,1:T(8,128)(2,1)S(1)}, u32[]{:S(2)}, u32[]{:S(2)}) %collective-permute-start.13) | collective-permute-done | bytes 524320 | tf_op jit(solution)/shard_map/ppermute | solution.py:327
  131.7 9.9 %collective-permute-start.16 = (bf16[2,4,128,128]{3,2,1,0:T(8,128)(2,1)S(1)}, bf16[2,4,128,128]{3,2,1,0:T(8,128)(2,1)S(1)}, u32[]{:S(2)}, u32[]{:S(2)}) collective-permute-start(bf16[2,4,128,128]{3,2,1,0:T(8,128)(2,1)S(1)} %fusion.21), channel_id=1, source_target_pairs={{0,1},{1,0},{2,3},{3,2},{4,5},{5,4},{6,7},{7,6},{8,9},{9,8},{10,11... | collective-permute-start | bytes 786440 | tf_op jit(solution)/shard_map/ppermute | solution.py:332
  141.7 9.5 %collective-permute-done.16.refs_1_ = bf16[2,4,128,128]{3,2,1,0:T(8,128)(2,1)S(1)} collective-permute-done((bf16[2,4,128,128]{3,2,1,0:T(8,128)(2,1)S(1)}, bf16[2,4,128,128]{3,2,1,0:T(8,128)(2,1)S(1)}, u32[]{:S(2)}, u32[]{:S(2)}) %collective-permute-start.16) | collective-permute-done | bytes 262176 | tf_op jit(solution)/shard_map/ppermute | solution.py:332
  158.9 3.6 %shard_map.81 = (bf16[4,4,128,128]{3,2,1,0:T(8,128)(2,1)S(1)}, bf16[4,4,128,128]{3,2,1,0:T(8,128)(2,1)S(1)}, bf16[4,4,128,128]{3,2,1,0:T(8,128)(2,1)S(1)}) custom-call(s32[4,144]{1,0:T(4,128)S(1)} %add_add_fusion.1.pairs_ref, bf16[193,128,128]{2,1,0:T(8,128)(2,1)S(1)} %get-tuple-element.145.middle_ref, bf16[24,8,128,128]{3,2,1,0:T(8,128)(2,1)S(1)} %shard_map.72.right_ref), custom_call_target="tpu_custom_call" | custom-call | flops 4831838208 | bytes 1048576 | tf_op jit(solution)/shard_map/pallas_call | solution.py:197
  163.5 3.5 %collective-permute-start.20 = (bf16[2,2,4,128,128]{4,3,2,0,1:T(8,128)(2,1)S(1)}, bf16[2,2,4,128,128]{4,3,2,0,1:T(8,128)(2,1)S(1)}, u32[]{:S(2)}, u32[]{:S(2)}) collective-permute-start(bf16[2,2,4,128,128]{4,3,2,0,1:T(8,128)(2,1)S(1)} %fusion.15), channel_id=1, source_target_pairs={{0,6},{1,7},{2,0},{3,1},{4,2},{5,3},{6,4},{7,5},{8,14},{9,15},{10,... | collective-permute-start | bytes 1572872 | tf_op jit(solution)/shard_map/ppermute | solution.py:327
  167.0 6.7 %collective-permute-done.18 = bf16[2,2,4,128,128]{4,3,2,0,1:T(8,128)(2,1)S(1)} collective-permute-done((bf16[2,2,4,128,128]{4,3,2,0,1:T(8,128)(2,1)S(1)}, bf16[2,2,4,128,128]{4,3,2,0,1:T(8,128)(2,1)S(1)}, u32[]{:S(2)}, u32[]{:S(2)}) %collective-permute-start.18) | collective-permute-done | bytes 524320 | tf_op jit(solution)/shard_map/ppermute | solution.py:327
  174.0 6.5 %collective-permute-start.21 = (bf16[2,4,128,128]{3,2,1,0:T(8,128)(2,1)S(1)}, bf16[2,4,128,128]{3,2,1,0:T(8,128)(2,1)S(1)}, u32[]{:S(2)}, u32[]{:S(2)}) collective-permute-start(bf16[2,4,128,128]{3,2,1,0:T(8,128)(2,1)S(1)} %fusion.22), channel_id=1, source_target_pairs={{0,1},{1,0},{2,3},{3,2},{4,5},{5,4},{6,7},{7,6},{8,9},{9,8},{10,11... | collective-permute-start | bytes 786440 | tf_op jit(solution)/shard_map/ppermute | solution.py:332
  180.5 9.5 %collective-permute-done.21.refs_1_ = bf16[2,4,128,128]{3,2,1,0:T(8,128)(2,1)S(1)} collective-permute-done((bf16[2,4,128,128]{3,2,1,0:T(8,128)(2,1)S(1)}, bf16[2,4,128,128]{3,2,1,0:T(8,128)(2,1)S(1)}, u32[]{:S(2)}, u32[]{:S(2)}) %collective-permute-start.21) | collective-permute-done | bytes 262176 | tf_op jit(solution)/shard_map/ppermute | solution.py:332
  197.9 3.6 %shard_map.85 = (bf16[4,4,128,128]{3,2,1,0:T(8,128)(2,1)S(1)}, bf16[4,4,128,128]{3,2,1,0:T(8,128)(2,1)S(1)}, bf16[4,4,128,128]{3,2,1,0:T(8,128)(2,1)S(1)}) custom-call(s32[4,144]{1,0:T(4,128)S(1)} %add_add_fusion.1.pairs_ref, bf16[193,128,128]{2,1,0:T(8,128)(2,1)S(1)} %get-tuple-element.152.middle_ref, bf16[24,8,128,128]{3,2,1,0:T(8,128)(2,1)S(1)} %shard_map.72.right_ref), custom_call_target="tpu_custom_call" | custom-call | flops 4831838208 | bytes 1048576 | tf_op jit(solution)/shard_map/pallas_call | solution.py:197
  206.4 6.5 %collective-permute-done.23 = bf16[2,2,4,128,128]{4,3,2,0,1:T(8,128)(2,1)S(1)} collective-permute-done((bf16[2,2,4,128,128]{4,3,2,0,1:T(8,128)(2,1)S(1)}, bf16[2,2,4,128,128]{4,3,2,0,1:T(8,128)(2,1)S(1)}, u32[]{:S(2)}, u32[]{:S(2)}) %collective-permute-start.23) | collective-permute-done | bytes 524320 | tf_op jit(solution)/shard_map/ppermute | solution.py:327
  213.2 6.5 %collective-permute-start.26 = (bf16[2,4,128,128]{3,2,1,0:T(8,128)(2,1)S(1)}, bf16[2,4,128,128]{3,2,1,0:T(8,128)(2,1)S(1)}, u32[]{:S(2)}, u32[]{:S(2)}) collective-permute-start(bf16[2,4,128,128]{3,2,1,0:T(8,128)(2,1)S(1)} %fusion.23), channel_id=1, source_target_pairs={{0,1},{1,0},{2,3},{3,2},{4,5},{5,4},{6,7},{7,6},{8,9},{9,8},{10,11... | collective-permute-start | bytes 786440 | tf_op jit(solution)/shard_map/ppermute | solution.py:332
  219.7 9.5 %collective-permute-done.26.refs_1_ = bf16[2,4,128,128]{3,2,1,0:T(8,128)(2,1)S(1)} collective-permute-done((bf16[2,4,128,128]{3,2,1,0:T(8,128)(2,1)S(1)}, bf16[2,4,128,128]{3,2,1,0:T(8,128)(2,1)S(1)}, u32[]{:S(2)}, u32[]{:S(2)}) %collective-permute-start.26) | collective-permute-done | bytes 262176 | tf_op jit(solution)/shard_map/ppermute | solution.py:332
  230.3 4.4 %collective-permute-start.28 = (f32[40,128]{1,0:T(8,128)S(1)}, f32[40,128]{1,0:T(8,128)S(1)}, u32[]{:S(2)}, u32[]{:S(2)}) collective-permute-start(f32[40,128]{1,0:T(8,128)S(1)} %constant_dynamic-update-slice_fusion), channel_id=1, source_target_pairs={{0,4},{1,5},{2,6},{3,7},{4,0},{5,1},{6,2},{7,3},{8,12},{9,13},{10,... | collective-permute-start | bytes 61448 | tf_op jit(solution)/shard_map/ppermute | solution.py:332
  239.7 6.4 %collective-permute-start.30 = (f32[40,128]{1,0:T(8,128)S(1)}, f32[40,128]{1,0:T(8,128)S(1)}, u32[]{:S(2)}, u32[]{:S(2)}) collective-permute-start(f32[40,128]{1,0:T(8,128)S(1)} %add_add_fusion), channel_id=1, source_target_pairs={{0,1},{1,0},{2,3},{3,2},{4,5},{5,4},{6,7},{7,6},{8,9},{9,8},{10,11... | collective-permute-start | bytes 61448 | tf_op jit(solution)/shard_map/ppermute | solution.py:332
  (141 shorter events, 87.6 us)
Async XLA Ops:
  1.7 9.8 %collective-permute-start.1 = (bf16[2,8,128,128]{3,2,1,0:T(8,128)(2,1)S(1)}, bf16[2,8,128,128]{3,2,1,0:T(8,128)(2,1)S(1)}, u32[]{:S(2)}, u32[]{:S(2)}) collective-permute-start(bf16[2,8,128,128]{3,2,1,0:T(8,128)(2,1)S(1)} %slice_bitcast_fusion.6), channel_id=1, source_target_pairs={{8,0},{16,8},{24,16},{32,24},{40,32},{48,40},{56,48},{64,56},{72,6... | collective-permute-start | bytes 1572872 | tf_op jit(solution)/shard_map/ppermute | solution.py:111
  7.2 46.5 %collective-permute-start.6 = (bf16[10,8,128,128]{3,2,1,0:T(8,128)(2,1)}, bf16[10,8,128,128]{3,2,1,0:T(8,128)(2,1)}, u32[]{:S(2)}, u32[]{:S(2)}) collective-permute-start(bf16[10,8,128,128]{3,2,1,0:T(8,128)(2,1)} %slice_bitcast_fusion), channel_id=1, source_target_pairs={{8,0},{16,8},{24,16},{32,24},{40,32},{48,40},{56,48},{64,56},{72,6... | collective-permute-start | bytes 7864328 | tf_op jit(solution)/shard_map/ppermute | solution.py:111
  14.6 14.9 %collective-permute-start.3 = (bf16[4,8,128,128]{3,2,1,0:T(8,128)(2,1)}, bf16[4,8,128,128]{3,2,1,0:T(8,128)(2,1)}, u32[]{:S(2)}, u32[]{:S(2)}) collective-permute-start(bf16[4,8,128,128]{3,2,1,0:T(8,128)(2,1)} %shard_map.70), channel_id=1, source_target_pairs={{16,32},{32,48},{48,0},{64,80},{80,96},{96,112},{112,64},{128,144}... | collective-permute-start | bytes 3145736 | tf_op jit(solution)/shard_map/ppermute | solution.py:122
  21.1 42.4 %collective-permute-start = (bf16[8,8,128,128]{3,2,1,0:T(8,128)(2,1)}, bf16[8,8,128,128]{3,2,1,0:T(8,128)(2,1)}, u32[]{:S(2)}, u32[]{:S(2)}) collective-permute-start(bf16[8,8,128,128]{3,2,1,0:T(8,128)(2,1)} %slice_bitcast_fusion.1), channel_id=1, source_target_pairs={{8,0},{16,8},{24,16},{32,24},{40,32},{48,40},{56,48},{64,56},{72,6... | collective-permute-start | bytes 6291464 | tf_op jit(solution)/shard_map/ppermute | solution.py:111
  29.5 17.5 %collective-permute-start.4 = (bf16[4,8,128,128]{3,2,1,0:T(8,128)(2,1)}, bf16[4,8,128,128]{3,2,1,0:T(8,128)(2,1)}, u32[]{:S(2)}, u32[]{:S(2)}) collective-permute-start(bf16[4,8,128,128]{3,2,1,0:T(8,128)(2,1)} %collective-permute-done.3), channel_id=1, source_target_pairs={{32,48},{48,0},{0,16},{80,96},{96,112},{112,64},{64,80},{144,160},... | collective-permute-start | bytes 3145736 | tf_op jit(solution)/shard_map/ppermute | solution.py:122
  33.0 23.1 %collective-permute-start.2 = (bf16[4,8,128,128]{3,2,1,0:T(8,128)(2,1)}, bf16[4,8,128,128]{3,2,1,0:T(8,128)(2,1)S(1)}, u32[]{:S(2)}, u32[]{:S(2)}) collective-permute-start(bf16[4,8,128,128]{3,2,1,0:T(8,128)(2,1)} %shard_map.70), channel_id=1, source_target_pairs={{8,0},{24,16},{40,32},{56,48},{72,64},{88,80},{104,96},{120,112},{... | collective-permute-start | bytes 3145736 | tf_op jit(solution)/shard_map/ppermute | solution.py:114
  47.0 16.5 %collective-permute-start.5 = (bf16[4,8,128,128]{3,2,1,0:T(8,128)(2,1)}, bf16[4,8,128,128]{3,2,1,0:T(8,128)(2,1)S(1)}, u32[]{:S(2)}, u32[]{:S(2)}) collective-permute-start(bf16[4,8,128,128]{3,2,1,0:T(8,128)(2,1)} %collective-permute-done.4), channel_id=1, source_target_pairs={{48,8},{0,24},{16,40},{96,56},{112,72},{64,88},{80,104},{160,120},... | collective-permute-start | bytes 3145736 | tf_op jit(solution)/shard_map/ppermute | solution.py:123
  67.4 10.3 %collective-permute-start.7 = (bf16[2,4,128,128]{3,2,1,0:T(8,128)(2,1)S(1)}, bf16[2,4,128,128]{3,2,1,0:T(8,128)(2,1)S(1)}, u32[]{:S(2)}, u32[]{:S(2)}) collective-permute-start(bf16[2,4,128,128]{3,2,1,0:T(8,128)(2,1)S(1)} %get-tuple-element.134), channel_id=1, source_target_pairs={{0,2},{1,3},{2,4},{3,5},{4,6},{5,7},{6,0},{7,1},{8,10},{9,11},{10,... | collective-permute-start | bytes 786440 | tf_op jit(solution)/shard_map/ppermute | solution.py:327
  67.5 10.4 %collective-permute-start.9 = (bf16[2,4,128,128]{3,2,1,0:T(8,128)(2,1)S(1)}, bf16[2,4,128,128]{3,2,1,0:T(8,128)(2,1)S(1)}, u32[]{:S(2)}, u32[]{:S(2)}) collective-permute-start(bf16[2,4,128,128]{3,2,1,0:T(8,128)(2,1)S(1)} %get-tuple-element.136), channel_id=1, source_target_pairs={{0,6},{1,7},{2,0},{3,1},{4,2},{5,3},{6,4},{7,5},{8,14},{9,15},{10,... | collective-permute-start | bytes 786440 | tf_op jit(solution)/shard_map/ppermute | solution.py:327
  77.8 15.0 %collective-permute-start.8 = (bf16[2,2,4,128,128]{4,3,2,0,1:T(8,128)(2,1)S(1)}, bf16[2,2,4,128,128]{4,3,2,0,1:T(8,128)(2,1)S(1)}, u32[]{:S(2)}, u32[]{:S(2)}) collective-permute-start(bf16[2,2,4,128,128]{4,3,2,0,1:T(8,128)(2,1)S(1)} %fusion.5), channel_id=1, source_target_pairs={{0,2},{1,3},{2,4},{3,5},{4,6},{5,7},{6,0},{7,1},{8,10},{9,11},{10,... | collective-permute-start | bytes 1572872 | tf_op jit(solution)/shard_map/ppermute | solution.py:327
  78.0 14.8 %collective-permute-start.10 = (bf16[2,2,4,128,128]{4,3,2,0,1:T(8,128)(2,1)S(1)}, bf16[2,2,4,128,128]{4,3,2,0,1:T(8,128)(2,1)S(1)}, u32[]{:S(2)}, u32[]{:S(2)}) collective-permute-start(bf16[2,2,4,128,128]{4,3,2,0,1:T(8,128)(2,1)S(1)} %fusion.7), channel_id=1, source_target_pairs={{0,6},{1,7},{2,0},{3,1},{4,2},{5,3},{6,4},{7,5},{8,14},{9,15},{10,... | collective-permute-start | bytes 1572872 | tf_op jit(solution)/shard_map/ppermute | solution.py:327
  93.1 11.9 %collective-permute-start.11 = (bf16[2,4,128,128]{3,2,1,0:T(8,128)(2,1)S(1)}, bf16[2,4,128,128]{3,2,1,0:T(8,128)(2,1)S(1)}, u32[]{:S(2)}, u32[]{:S(2)}) collective-permute-start(bf16[2,4,128,128]{3,2,1,0:T(8,128)(2,1)S(1)} %fusion.20), channel_id=1, source_target_pairs={{0,1},{1,0},{2,3},{3,2},{4,5},{5,4},{6,7},{7,6},{8,9},{9,8},{10,11... | collective-permute-start | bytes 786440 | tf_op jit(solution)/shard_map/ppermute | solution.py:332
  109.3 8.7 %collective-permute-start.12 = (bf16[2,4,128,128]{3,2,1,0:T(8,128)(2,1)S(1)}, bf16[2,4,128,128]{3,2,1,0:T(8,128)(2,1)S(1)}, u32[]{:S(2)}, u32[]{:S(2)}) collective-permute-start(bf16[2,4,128,128]{3,2,1,0:T(8,128)(2,1)S(1)} %get-tuple-element.141), channel_id=1, source_target_pairs={{0,2},{1,3},{2,4},{3,5},{4,6},{5,7},{6,0},{7,1},{8,10},{9,11},{10,... | collective-permute-start | bytes 786440 | tf_op jit(solution)/shard_map/ppermute | solution.py:327
  109.4 8.8 %collective-permute-start.14 = (bf16[2,4,128,128]{3,2,1,0:T(8,128)(2,1)S(1)}, bf16[2,4,128,128]{3,2,1,0:T(8,128)(2,1)S(1)}, u32[]{:S(2)}, u32[]{:S(2)}) collective-permute-start(bf16[2,4,128,128]{3,2,1,0:T(8,128)(2,1)S(1)} %get-tuple-element.143), channel_id=1, source_target_pairs={{0,6},{1,7},{2,0},{3,1},{4,2},{5,3},{6,4},{7,5},{8,14},{9,15},{10,... | collective-permute-start | bytes 786440 | tf_op jit(solution)/shard_map/ppermute | solution.py:327
  118.2 13.3 %collective-permute-start.13 = (bf16[2,2,4,128,128]{4,3,2,0,1:T(8,128)(2,1)S(1)}, bf16[2,2,4,128,128]{4,3,2,0,1:T(8,128)(2,1)S(1)}, u32[]{:S(2)}, u32[]{:S(2)}) collective-permute-start(bf16[2,2,4,128,128]{4,3,2,0,1:T(8,128)(2,1)S(1)} %fusion.9), channel_id=1, source_target_pairs={{0,2},{1,3},{2,4},{3,5},{4,6},{5,7},{6,0},{7,1},{8,10},{9,11},{10,... | collective-permute-start | bytes 1572872 | tf_op jit(solution)/shard_map/ppermute | solution.py:327
  118.4 13.1 %collective-permute-start.15 = (bf16[2,2,4,128,128]{4,3,2,0,1:T(8,128)(2,1)S(1)}, bf16[2,2,4,128,128]{4,3,2,0,1:T(8,128)(2,1)S(1)}, u32[]{:S(2)}, u32[]{:S(2)}) collective-permute-start(bf16[2,2,4,128,128]{4,3,2,0,1:T(8,128)(2,1)S(1)} %fusion.11), channel_id=1, source_target_pairs={{0,6},{1,7},{2,0},{3,1},{4,2},{5,3},{6,4},{7,5},{8,14},{9,15},{10,... | collective-permute-start | bytes 1572872 | tf_op jit(solution)/shard_map/ppermute | solution.py:327
  131.7 19.4 %collective-permute-start.16 = (bf16[2,4,128,128]{3,2,1,0:T(8,128)(2,1)S(1)}, bf16[2,4,128,128]{3,2,1,0:T(8,128)(2,1)S(1)}, u32[]{:S(2)}, u32[]{:S(2)}) collective-permute-start(bf16[2,4,128,128]{3,2,1,0:T(8,128)(2,1)S(1)} %fusion.21), channel_id=1, source_target_pairs={{0,1},{1,0},{2,3},{3,2},{4,5},{5,4},{6,7},{7,6},{8,9},{9,8},{10,11... | collective-permute-start | bytes 786440 | tf_op jit(solution)/shard_map/ppermute | solution.py:332
  163.3 10.5 %collective-permute-start.18 = (bf16[2,2,4,128,128]{4,3,2,0,1:T(8,128)(2,1)S(1)}, bf16[2,2,4,128,128]{4,3,2,0,1:T(8,128)(2,1)S(1)}, u32[]{:S(2)}, u32[]{:S(2)}) collective-permute-start(bf16[2,2,4,128,128]{4,3,2,0,1:T(8,128)(2,1)S(1)} %fusion.13), channel_id=1, source_target_pairs={{0,2},{1,3},{2,4},{3,5},{4,6},{5,7},{6,0},{7,1},{8,10},{9,11},{10,... | collective-permute-start | bytes 1572872 | tf_op jit(solution)/shard_map/ppermute | solution.py:327
  163.5 10.3 %collective-permute-start.20 = (bf16[2,2,4,128,128]{4,3,2,0,1:T(8,128)(2,1)S(1)}, bf16[2,2,4,128,128]{4,3,2,0,1:T(8,128)(2,1)S(1)}, u32[]{:S(2)}, u32[]{:S(2)}) collective-permute-start(bf16[2,2,4,128,128]{4,3,2,0,1:T(8,128)(2,1)S(1)} %fusion.15), channel_id=1, source_target_pairs={{0,6},{1,7},{2,0},{3,1},{4,2},{5,3},{6,4},{7,5},{8,14},{9,15},{10,... | collective-permute-start | bytes 1572872 | tf_op jit(solution)/shard_map/ppermute | solution.py:327
  174.0 16.0 %collective-permute-start.21 = (bf16[2,4,128,128]{3,2,1,0:T(8,128)(2,1)S(1)}, bf16[2,4,128,128]{3,2,1,0:T(8,128)(2,1)S(1)}, u32[]{:S(2)}, u32[]{:S(2)}) collective-permute-start(bf16[2,4,128,128]{3,2,1,0:T(8,128)(2,1)S(1)} %fusion.22), channel_id=1, source_target_pairs={{0,1},{1,0},{2,3},{3,2},{4,5},{5,4},{6,7},{7,6},{8,9},{9,8},{10,11... | collective-permute-start | bytes 786440 | tf_op jit(solution)/shard_map/ppermute | solution.py:332
  202.2 10.7 %collective-permute-start.23 = (bf16[2,2,4,128,128]{4,3,2,0,1:T(8,128)(2,1)S(1)}, bf16[2,2,4,128,128]{4,3,2,0,1:T(8,128)(2,1)S(1)}, u32[]{:S(2)}, u32[]{:S(2)}) collective-permute-start(bf16[2,2,4,128,128]{4,3,2,0,1:T(8,128)(2,1)S(1)} %fusion.17), channel_id=1, source_target_pairs={{0,2},{1,3},{2,4},{3,5},{4,6},{5,7},{6,0},{7,1},{8,10},{9,11},{10,... | collective-permute-start | bytes 1572872 | tf_op jit(solution)/shard_map/ppermute | solution.py:327
  202.5 10.5 %collective-permute-start.25 = (bf16[2,2,4,128,128]{4,3,2,0,1:T(8,128)(2,1)S(1)}, bf16[2,2,4,128,128]{4,3,2,0,1:T(8,128)(2,1)S(1)}, u32[]{:S(2)}, u32[]{:S(2)}) collective-permute-start(bf16[2,2,4,128,128]{4,3,2,0,1:T(8,128)(2,1)S(1)} %fusion.19), channel_id=1, source_target_pairs={{0,6},{1,7},{2,0},{3,1},{4,2},{5,3},{6,4},{7,5},{8,14},{9,15},{10,... | collective-permute-start | bytes 1572872 | tf_op jit(solution)/shard_map/ppermute | solution.py:327
  213.2 16.0 %collective-permute-start.26 = (bf16[2,4,128,128]{3,2,1,0:T(8,128)(2,1)S(1)}, bf16[2,4,128,128]{3,2,1,0:T(8,128)(2,1)S(1)}, u32[]{:S(2)}, u32[]{:S(2)}) collective-permute-start(bf16[2,4,128,128]{3,2,1,0:T(8,128)(2,1)S(1)} %fusion.23), channel_id=1, source_target_pairs={{0,1},{1,0},{2,3},{3,2},{4,5},{5,4},{6,7},{7,6},{8,9},{9,8},{10,11... | collective-permute-start | bytes 786440 | tf_op jit(solution)/shard_map/ppermute | solution.py:332
  239.7 8.2 %collective-permute-start.30 = (f32[40,128]{1,0:T(8,128)S(1)}, f32[40,128]{1,0:T(8,128)S(1)}, u32[]{:S(2)}, u32[]{:S(2)}) collective-permute-start(f32[40,128]{1,0:T(8,128)S(1)} %add_add_fusion), channel_id=1, source_target_pairs={{0,1},{1,0},{2,3},{3,2},{4,5},{5,4},{6,7},{7,6},{8,9},{9,8},{10,11... | collective-permute-start | bytes 61448 | tf_op jit(solution)/shard_map/ppermute | solution.py:332
  (17 other events, 291.7 us)
